TPU v7x, 32 devices: a whole 2x2x4 slice. The times are simulated.
32 devices in a mesh: seq: 8 (over z, y), opt: 4 (over x, core).
Axes of the slice: x: 2, y: 2, z: 4, core: 2. Of those that a mesh axis runs over, the one named last changes fastest.
Arguments:
- inputs: bfloat16 [2, 4, 2048, 768], P(None, 'opt', 'seq'), may hold values from -6 to 6
- key_mask: int32 [2, 4, 2048], P(None, 'opt', 'seq'), may hold values 0 or 1
- lengths: int32 [2, 4], P(None, 'opt'), may hold values from 512 to 2048, as said below
- cotangent: bfloat16 [2, 4, 256, 1280], P(None, 'opt', 'seq'), may hold values from -6 to 6
- latents: float32 [256, 1280], replicated, may hold values from -6 to 6
- lat_vectors: float32 [6, 1280], replicated
- in_vectors: float32 [2, 768], replicated
- w_query: float32 [1280, 768], P('opt'), may hold values from -0.15625 to 0.15625
- w_key: float32 [768, 768], P('opt'), may hold values from -0.21875 to 0.21875
- w_value: float32 [768, 768], P('opt'), may hold values from -0.21875 to 0.21875
- w_out: float32 [768, 1280], P('opt'), may hold values from -3 to 3
- w_up: float32 [1280, 1280], P('opt'), may hold values from -0.15625 to 0.15625
- w_down: float32 [1280, 1280], P('opt'), may hold values from -0.15625 to 0.15625
- mom_query: float32 [1280, 768], P('opt')
- mom_key: float32 [768, 768], P('opt')
- mom_value: float32 [768, 768], P('opt')
- mom_out: float32 [768, 1280], P('opt')
- mom_up: float32 [1280, 1280], P('opt')
- mom_down: float32 [1280, 1280], P('opt')
- lat_first: float32 [6, 1280], replicated
- lat_second: float32 [6, 1280], replicated, as said below
- in_first: float32 [2, 768], replicated
- in_second: float32 [2, 768], replicated, as said below
- latent_first: float32 [256, 1280], replicated
- latent_second: float32 [256, 1280], replicated, as said below
Outputs:
- block_out: bfloat16 [2, 4, 256, 1280], P(None, 'opt', 'seq')
- input_grad: float32 [2, 4, 2048, 768], P(None, 'opt', 'seq')
- mom_query_new: float32 [1280, 768], P('opt')
- mom_key_new: float32 [768, 768], P('opt')
- mom_value_new: float32 [768, 768], P('opt')
- mom_out_new: float32 [768, 1280], P('opt')
- mom_up_new: float32 [1280, 1280], P('opt')
- mom_down_new: float32 [1280, 1280], P('opt')
- w_query_new: float32 [1280, 768], P('opt')
- w_key_new: float32 [768, 768], P('opt')
- w_value_new: float32 [768, 768], P('opt')
- w_out_new: float32 [768, 1280], P('opt')
- w_up_new: float32 [1280, 1280], P('opt')
- w_down_new: float32 [1280, 1280], P('opt')
- lat_first_new: float32 [6, 1280], replicated
- lat_second_new: float32 [6, 1280], replicated
- lat_vectors_new: float32 [6, 1280], replicated
- in_first_new: float32 [2, 768], replicated
- in_second_new: float32 [2, 768], replicated
- in_vectors_new: float32 [2, 768], replicated
- latent_first_new: float32 [256, 1280], replicated
- latent_second_new: float32 [256, 1280], replicated
- latents_new: float32 [256, 1280], replicated
Inputs may be any that keep to these rules, and one draw needn't show every extreme that they name: `lengths`: among the 1 documents of each micro-batch on one index of opt, one has length exactly 2048. `lat_second`: every entry is positive. `in_second`: every entry is positive. `latent_second`: every entry is positive.
All inputs are finite; a program needn't handle non-finite values. No bound on the sum of `key_mask` on one device may be relied on, other than what follows from the above.
Results may differ from a plain program's by a relative error of at most 0.025.
Values may be sent and summed in bfloat16 or wider, within the bound.
A program may use at most 256 MiB of HBM per device.

v0:
```python
import jax
import jax.numpy as jnp
from jax import lax
from jax.sharding import PartitionSpec as P

D_LAT = 1280
HEADS = 8
HEAD_DIM = 96
E_IN = 768
STEP = 10
OUT_FAN = 4


highest = lax.Precision.HIGHEST
coef_one = 3.4445
coef_two = -4.775
coef_three = 2.0315


def as_sent(array):

    def short(part):
        return part.astype(jnp.bfloat16) if part.dtype == jnp.float32 else part

    return jax.tree.map(short, array)


def layer_norm(values, scale_vec, offset):
    center = jnp.mean(values, axis=-1, keepdims=True)
    shifted = values - center
    inverse = lax.rsqrt(jnp.mean(shifted * shifted, axis=-1, keepdims=True) + 1e-05)
    normal_hat = shifted * inverse
    return (normal_hat * scale_vec + offset, normal_hat, inverse)


def norm_back(grad_out, normal_hat, inverse, scale_vec):
    scaled = grad_out * scale_vec
    return inverse * (
        scaled
        - jnp.mean(scaled, axis=-1, keepdims=True)
        - normal_hat * jnp.mean(scaled * normal_hat, axis=-1, keepdims=True)
    )


def exact_gelu(values):
    return jax.nn.gelu(values, approximate=False)


def masked_scores(query_heads, key_heads, usable, score_scale):
    scores = (
        jnp.einsum("nhd,bshd->bhns", query_heads, key_heads, preferred_element_type=jnp.float32)
        * score_scale
    )
    return jnp.where(usable[:, None, None, :], scores, -1e30)


def summed_gram(currents):
    grams = [jnp.matmul(current.T, current, precision=highest) for current in currents]
    shares = (
        lax.psum_scatter(grams[0], ("seq", "opt"), scatter_dimension=0, tiled=True),
        lax.psum_scatter(grams[1], ("seq", "opt"), scatter_dimension=0, tiled=True),
        lax.psum_scatter(grams[2], ("seq", "opt"), scatter_dimension=0, tiled=True),
        lax.psum_scatter(grams[3], ("seq", "opt"), scatter_dimension=0, tiled=True),
        lax.psum_scatter(grams[4], ("seq", "opt"), scatter_dimension=0, tiled=True),
        lax.psum_scatter(grams[5], ("seq", "opt"), scatter_dimension=0, tiled=True),
    )
    return (
        lax.all_gather(shares[0].astype(jnp.bfloat16), ("seq", "opt"), axis=0, tiled=True).astype(
            jnp.float32
        ),
        lax.all_gather(shares[1].astype(jnp.bfloat16), ("seq", "opt"), axis=0, tiled=True).astype(
            jnp.float32
        ),
        lax.all_gather(shares[2].astype(jnp.bfloat16), ("seq", "opt"), axis=0, tiled=True).astype(
            jnp.float32
        ),
        lax.all_gather(shares[3].astype(jnp.bfloat16), ("seq", "opt"), axis=0, tiled=True).astype(
            jnp.float32
        ),
        lax.all_gather(shares[4].astype(jnp.bfloat16), ("seq", "opt"), axis=0, tiled=True).astype(
            jnp.float32
        ),
        lax.all_gather(shares[5].astype(jnp.bfloat16), ("seq", "opt"), axis=0, tiled=True).astype(
            jnp.float32
        ),
    )


def newton_step(currents, grams):
    results = []
    for current, gram in zip(currents, grams):
        product = jnp.matmul(current, gram, precision=highest)
        results.append(
            coef_one * current
            + coef_two * product
            + coef_three * jnp.matmul(product, gram, precision=highest)
        )
    return results


def adam_update(param, gradient, first, second, step_rate, decay):
    first_new = 0.9 * first + 0.1 * gradient
    second_new = 0.95 * second + 0.05 * gradient * gradient
    ratio = first_new / (1.0 - 0.9**STEP) / (jnp.sqrt(second_new / (1.0 - 0.95**STEP)) + 1e-08)
    return (first_new, second_new, param - step_rate * (ratio + decay * param))


def local(
    inputs,
    key_mask,
    lengths,
    cotangent,
    latents,
    lat_vectors,
    in_vectors,
    w_query,
    w_key,
    w_value,
    w_out,
    w_up,
    w_down,
    mom_query,
    mom_key,
    mom_value,
    mom_out,
    mom_up,
    mom_down,
    lat_first,
    lat_second,
    in_first,
    in_second,
    latent_first,
    latent_second,
):
    query_low, key_low, value_low, out_low, up_low, down_low = (
        lax.all_gather(w_query.astype(jnp.bfloat16), "opt", axis=0, tiled=True),
        lax.all_gather(w_key.astype(jnp.bfloat16), "opt", axis=0, tiled=True),
        lax.all_gather(w_value.astype(jnp.bfloat16), "opt", axis=0, tiled=True),
        lax.all_gather(w_out.astype(jnp.bfloat16), "opt", axis=0, tiled=True),
        lax.all_gather(w_up.astype(jnp.bfloat16), "opt", axis=0, tiled=True),
        lax.all_gather(w_down.astype(jnp.bfloat16), "opt", axis=0, tiled=True),
    )
    pair_low = jnp.concatenate([key_low, value_low], axis=1)
    seq_index = lax.axis_index("seq")
    seq_size = lax.axis_size("seq")
    opt_index = lax.axis_index("opt")
    opt_size = lax.axis_size("opt")
    micro_count, doc_local, span, width_in = inputs.shape
    lat_count, width_lat = latents.shape
    own_rows = lat_count // seq_size
    row_start = seq_index * own_rows
    score_scale = HEAD_DIM ** (-0.5)
    lat_normed, lat_hat, lat_inv = layer_norm(latents, lat_vectors[0], lat_vectors[1])
    lat_low = lat_normed.astype(jnp.bfloat16)
    query_rows = jnp.dot(lat_low, query_low, preferred_element_type=jnp.float32).astype(
        jnp.bfloat16
    )
    query_heads = query_rows.reshape(lat_count, HEADS, HEAD_DIM)
    own_latents = lax.dynamic_slice_in_dim(latents, row_start, own_rows, 0)
    positions = seq_index * span + jnp.arange(span, dtype=jnp.int32)
    grad_query_rows = jnp.zeros((lat_count, width_in), jnp.float32)
    grad_pair = jnp.zeros((width_in, 2 * width_in), jnp.float32)
    grad_out_w = jnp.zeros((width_in, width_lat), jnp.float32)
    grad_up_w = jnp.zeros((width_lat, width_lat), jnp.float32)
    grad_down_w = jnp.zeros((width_lat, width_lat), jnp.float32)
    mlp_gain = jnp.zeros((width_lat,), jnp.float32)
    mlp_shift = jnp.zeros((width_lat,), jnp.float32)
    bias_up = jnp.zeros((width_lat,), jnp.float32)
    bias_down = jnp.zeros((width_lat,), jnp.float32)
    in_gain = jnp.zeros((width_in,), jnp.float32)
    in_shift = jnp.zeros((width_in,), jnp.float32)
    latent_rest = jnp.zeros((own_rows, width_lat), jnp.float32)
    block_parts = []
    input_parts = []
    for micro_step in range(micro_count):
        tokens = inputs[micro_step]
        usable = (positions[None, :] < lengths[micro_step][:, None]) & (
            (key_mask[micro_step] == 1) | (positions[None, :] == 0)
        )
        in_normed, in_hat, in_inv = layer_norm(
            tokens.astype(jnp.float32), in_vectors[0], in_vectors[1]
        )
        in_low = in_normed.astype(jnp.bfloat16)
        pair_rows = jnp.einsum(
            "bse,ef->bsf", in_low, pair_low, preferred_element_type=jnp.float32
        ).astype(jnp.bfloat16)
        key_heads = pair_rows[:, :, :width_in].reshape(doc_local, span, HEADS, HEAD_DIM)
        value_heads = pair_rows[:, :, width_in:].reshape(doc_local, span, HEADS, HEAD_DIM)
        masked = masked_scores(query_heads, key_heads, usable, score_scale)
        row_max = lax.pmax(jnp.max(masked, axis=-1), "seq")
        weights = jnp.exp(masked - row_max[..., None])
        weights_low = weights.astype(jnp.bfloat16)
        summed, row_sum = (
            lax.psum(
                jnp.einsum(
                    "bhns,bshd->bnhd", weights_low, value_heads, preferred_element_type=jnp.float32
                ).astype(jnp.bfloat16),
                "seq",
            ).astype(jnp.float32),
            lax.psum(jnp.sum(weights, axis=-1).astype(jnp.bfloat16), "seq").astype(jnp.float32),
        )
        sum_heads = jnp.transpose(row_sum, (0, 2, 1))[..., None]
        attended = summed / sum_heads
        own_att = (
            lax.dynamic_slice_in_dim(attended, row_start, own_rows, 1)
            .reshape(doc_local, own_rows, width_in)
            .astype(jnp.bfloat16)
        )
        hidden = own_latents[None] + jnp.einsum(
            "bne,ef->bnf", own_att, out_low, preferred_element_type=jnp.float32
        )
        mlp_normed, mlp_hat, mlp_inv = layer_norm(hidden, lat_vectors[2], lat_vectors[3])
        mlp_low = mlp_normed.astype(jnp.bfloat16)
        pre_act = (
            jnp.einsum("bnf,fg->bng", mlp_low, up_low, preferred_element_type=jnp.float32)
            + lat_vectors[4]
        )
        activated, gelu_pull = jax.vjp(exact_gelu, pre_act)
        act_low = activated.astype(jnp.bfloat16)
        block_parts.append(
            (
                hidden
                + jnp.einsum("bng,gk->bnk", act_low, down_low, preferred_element_type=jnp.float32)
                + lat_vectors[5]
            ).astype(jnp.bfloat16)
        )
        back_rows = cotangent[micro_step]
        grad_down_w = grad_down_w + jnp.einsum(
            "bng,bnk->gk", act_low, back_rows, preferred_element_type=jnp.float32
        )
        bias_down = bias_down + jnp.sum(back_rows.astype(jnp.float32), axis=(0, 1))
        grad_act = jnp.einsum(
            "bnk,gk->bng", back_rows, down_low, preferred_element_type=jnp.float32
        )
        grad_pre = gelu_pull(grad_act)[0].astype(jnp.bfloat16)
        grad_up_w = grad_up_w + jnp.einsum(
            "bnf,bng->fg", mlp_low, grad_pre, preferred_element_type=jnp.float32
        )
        bias_up = bias_up + jnp.sum(grad_pre.astype(jnp.float32), axis=(0, 1))
        grad_mlp = jnp.einsum("bng,fg->bnf", grad_pre, up_low, preferred_element_type=jnp.float32)
        mlp_gain = mlp_gain + jnp.sum(grad_mlp * mlp_hat, axis=(0, 1))
        mlp_shift = mlp_shift + jnp.sum(grad_mlp, axis=(0, 1))
        grad_hidden = back_rows.astype(jnp.float32) + norm_back(
            grad_mlp, mlp_hat, mlp_inv, lat_vectors[2]
        )
        latent_rest = latent_rest + jnp.sum(grad_hidden, axis=0)
        grad_branch = grad_hidden.astype(jnp.bfloat16)
        grad_out_w = grad_out_w + jnp.einsum(
            "bne,bnf->ef", own_att, grad_branch, preferred_element_type=jnp.float32
        )
        grad_own = jnp.einsum(
            "bnf,ef->bne", grad_branch, out_low, preferred_element_type=jnp.float32
        ).astype(jnp.bfloat16)
        grad_att = (
            lax.all_gather(grad_own, "seq", axis=1, tiled=True)
            .astype(jnp.float32)
            .reshape(doc_local, lat_count, HEADS, HEAD_DIM)
        )
        grad_summed = (grad_att / sum_heads).astype(jnp.bfloat16)
        inner = jnp.transpose(jnp.sum(grad_att * attended, axis=-1) / sum_heads[..., 0], (0, 2, 1))
        grad_prob = jnp.einsum(
            "bnhd,bshd->bhns", grad_summed, value_heads, preferred_element_type=jnp.float32
        )
        grad_scores = (weights * (grad_prob - inner[..., None])).astype(jnp.bfloat16)
        grad_query_rows = grad_query_rows + score_scale * jnp.einsum(
            "bhns,bshd->nhd", grad_scores, key_heads, preferred_element_type=jnp.float32
        ).reshape(lat_count, width_in)
        grad_keys = (
            score_scale
            * jnp.einsum(
                "bhns,nhd->bshd", grad_scores, query_heads, preferred_element_type=jnp.float32
            )
        ).astype(jnp.bfloat16)
        grad_values = jnp.einsum(
            "bhns,bnhd->bshd", weights_low, grad_summed, preferred_element_type=jnp.float32
        ).astype(jnp.bfloat16)
        grad_pairs = jnp.concatenate(
            [
                grad_keys.reshape(doc_local, span, width_in),
                grad_values.reshape(doc_local, span, width_in),
            ],
            axis=-1,
        )
        grad_pair = grad_pair + jnp.einsum(
            "bse,bsf->ef", in_low, grad_pairs, preferred_element_type=jnp.float32
        )
        grad_in = jnp.einsum(
            "bsf,ef->bse", grad_pairs, pair_low, preferred_element_type=jnp.float32
        )
        in_gain = in_gain + jnp.sum(grad_in * in_hat, axis=(0, 1))
        in_shift = in_shift + jnp.sum(grad_in, axis=(0, 1))
        input_parts.append(norm_back(grad_in, in_hat, in_inv, in_vectors[0]))
    grad_query_w = jnp.matmul(lat_low.astype(jnp.float32).T, grad_query_rows, precision=highest)
    grad_lat = jnp.matmul(grad_query_rows, query_low.astype(jnp.float32).T, precision=highest)
    zero_index = jnp.zeros((), jnp.int32)
    latent_grad = norm_back(grad_lat, lat_hat, lat_inv, lat_vectors[0]) + lax.dynamic_update_slice(
        jnp.zeros_like(latents), latent_rest, (row_start, zero_index)
    )
    lat_vec_grad = jnp.stack(
        [
            jnp.sum(grad_lat * lat_hat, axis=0),
            jnp.sum(grad_lat, axis=0),
            mlp_gain,
            mlp_shift,
            bias_up,
            bias_down,
        ]
    )
    in_vec_grad = jnp.stack([in_gain, in_shift])
    weight_grads = (
        grad_query_w,
        grad_pair[:, :width_in],
        grad_pair[:, width_in:],
        grad_out_w,
        grad_up_w,
        grad_down_w,
    )
    reduced_all = lax.psum(
        (
            weight_grads[0],
            weight_grads[1],
            weight_grads[2],
            weight_grads[3],
            weight_grads[4],
            weight_grads[5],
            lat_vec_grad,
            in_vec_grad,
            latent_grad,
        ),
        ("seq", "opt"),
    )
    row_grads = [
        lax.dynamic_slice_in_dim(
            reduced, opt_index * (reduced.shape[0] // opt_size), reduced.shape[0] // opt_size, 0
        )
        for reduced in reduced_all[:6]
    ]
    lat_vec_sum, in_vec_sum, latent_sum = (reduced_all[6], reduced_all[7], reduced_all[8])
    masters = (w_query, w_key, w_value, w_out, w_up, w_down)
    moments = (mom_query, mom_key, mom_value, mom_out, mom_up, mom_down)
    moments_new = [0.95 * moment + gradient for moment, gradient in zip(moments, row_grads)]
    pieces = [
        lax.dynamic_slice_in_dim(
            moment, seq_index * (moment.shape[0] // seq_size), moment.shape[0] // seq_size, 0
        )
        for moment in moments_new
    ]
    squares = lax.psum(
        (
            jnp.sum(pieces[0] * pieces[0]),
            jnp.sum(pieces[1] * pieces[1]),
            jnp.sum(pieces[2] * pieces[2]),
            jnp.sum(pieces[3] * pieces[3]),
            jnp.sum(pieces[4] * pieces[4]),
            jnp.sum(pieces[5] * pieces[5]),
        ),
        ("seq", "opt"),
    )
    thin_rows = [piece / (jnp.sqrt(square) + 1e-07) for piece, square in zip(pieces, squares)]
    for sweep in range(5):
        thin_rows = newton_step(thin_rows, summed_gram(thin_rows))
    currents = (
        lax.all_gather(as_sent(thin_rows[0]), "seq", axis=0, tiled=True),
        lax.all_gather(as_sent(thin_rows[1]), "seq", axis=0, tiled=True),
        lax.all_gather(as_sent(thin_rows[2]), "seq", axis=0, tiled=True),
        lax.all_gather(as_sent(thin_rows[3]), "seq", axis=0, tiled=True),
        lax.all_gather(as_sent(thin_rows[4]), "seq", axis=0, tiled=True),
        lax.all_gather(as_sent(thin_rows[5]), "seq", axis=0, tiled=True),
    )
    fans = (D_LAT, E_IN, E_IN, OUT_FAN, D_LAT, D_LAT)
    sides = (D_LAT, E_IN, E_IN, D_LAT, D_LAT, D_LAT)
    new_masters = []
    for master, current, fan_in, long_side in zip(masters, currents, fans, sides):
        step_rate = fan_in ** (-0.5)
        new_masters.append((1.0 - 0.1 * step_rate) * master - step_rate * long_side**0.5 * current)
    lat_m, lat_v, lat_p = adam_update(lat_vectors, lat_vec_sum, lat_first, lat_second, 0.6, 0.0)
    in_m, in_v, in_p = adam_update(in_vectors, in_vec_sum, in_first, in_second, 0.6, 0.0)
    latent_m, latent_v, latent_p = adam_update(
        latents, latent_sum, latent_first, latent_second, 1.0, 0.1
    )
    block_out = jnp.stack(block_parts)
    input_grad = jnp.stack(input_parts)
    return (
        block_out,
        input_grad,
        moments_new[0],
        moments_new[1],
        moments_new[2],
        moments_new[3],
        moments_new[4],
        moments_new[5],
        new_masters[0],
        new_masters[1],
        new_masters[2],
        new_masters[3],
        new_masters[4],
        new_masters[5],
        lat_m,
        lat_v,
        lat_p,
        in_m,
        in_v,
        in_p,
        latent_m,
        latent_v,
        latent_p,
    )


def solution(mesh):
    return jax.shard_map(
        local,
        mesh=mesh,
        in_specs=(
            P(None, "opt", "seq", None),
            P(None, "opt", "seq"),
            P(None, "opt"),
            P(None, "opt", "seq", None),
            P(),
            P(),
            P(),
            P("opt", None),
            P("opt", None),
            P("opt", None),
            P("opt", None),
            P("opt", None),
            P("opt", None),
            P("opt", None),
            P("opt", None),
            P("opt", None),
            P("opt", None),
            P("opt", None),
            P("opt", None),
            P(),
            P(),
            P(),
            P(),
            P(),
            P(),
        ),
        out_specs=(
            P(None, "opt", "seq", None),
            P(None, "opt", "seq", None),
            P("opt", None),
            P("opt", None),
            P("opt", None),
            P("opt", None),
            P("opt", None),
            P("opt", None),
            P("opt", None),
            P("opt", None),
            P("opt", None),
            P("opt", None),
            P("opt", None),
            P("opt", None),
            P(),
            P(),
            P(),
            P(),
            P(),
            P(),
            P(),
            P(),
            P(),
        ),
        check_vma=False,
    )
```

profile of v0, /device:TPU:0, one launch (start us, length us, event | category | flops | bytes accessed | tf_op | source)
XLA Modules:
  0.0 6425.8 jit_solution(18038545911694794026)
XLA Ops:
  415.7 419.6 %all-reduce.8.cloned.1.call-done = (f32[1280,768]{1,0:T(8,128)}, f32[768,768]{1,0:T(8,128)}, f32[768,768]{1,0:T(8,128)}, f32[768,1280]{1,0:T(8,128)}, f32[1280,1...) async-done(((f32[1280,768]{1,0:T(8,128)}, f32[768,768]{1,0:T(8,128)}, f32[768,768]{1,0:T(8,128)}, f32[768,1280]{1,0:T(8,128)}, f32[1280,1280]{1,0:T(8,128)}, ...) | async-done | bytes 27000848 | tf_op jit(solution)/shard_map/psum | solution.py:318
  932.4 61.7 reduce-scatter.41.cloned.1.call-done
  995.7 102.5 %reduce-scatter.51.cloned.1.call-done = f32[24,768]{1,0:T(8,128)} async-done(((f32[768,768]{1,0:T(8,128)}), f32[24,768]{1,0:T(8,128)}) %reduce-scatter.51.cloned.1.call-update) | async-done | bytes 73744 | tf_op jit(solution)/shard_map/reduce_scatter | solution.py:62
  1099.7 101.9 %reduce-scatter.31.cloned.1.call-done = f32[24,768]{1,0:T(8,128)} async-done(((f32[768,768]{1,0:T(8,128)}), f32[24,768]{1,0:T(8,128)}) %reduce-scatter.31.cloned.1.call-update) | async-done | bytes 73744 | tf_op jit(solution)/shard_map/reduce_scatter | solution.py:60
  1203.2 145.2 %reduce-scatter.61.cloned.1.call-done = f32[40,1280]{1,0:T(8,128)} async-done(((f32[1280,1280]{1,0:T(8,128)}), f32[40,1280]{1,0:T(8,128)}) %reduce-scatter.61.cloned.1.call-update) | async-done | bytes 204816 | tf_op jit(solution)/shard_map/reduce_scatter | solution.py:63
  1350.0 142.4 %reduce-scatter.71.cloned.1.call-done = f32[40,1280]{1,0:T(8,128)} async-done(((f32[1280,1280]{1,0:T(8,128)}), f32[40,1280]{1,0:T(8,128)}) %reduce-scatter.71.cloned.1.call-update) | async-done | bytes 204816 | tf_op jit(solution)/shard_map/reduce_scatter | solution.py:64
  1494.1 142.0 %reduce-scatter.81.cloned.1.call-done = f32[40,1280]{1,0:T(8,128)} async-done(((f32[1280,1280]{1,0:T(8,128)}), f32[40,1280]{1,0:T(8,128)}) %reduce-scatter.81.cloned.1.call-update) | async-done | bytes 204816 | tf_op jit(solution)/shard_map/reduce_scatter | solution.py:65
  2003.2 90.2 %reduce-scatter.43.cloned.1.call-done = f32[24,768]{1,0:T(8,128)} async-done(((f32[768,768]{1,0:T(8,128)}), f32[24,768]{1,0:T(8,128)}) %reduce-scatter.43.cloned.1.call-update) | async-done | bytes 73744 | tf_op jit(solution)/shard_map/reduce_scatter | solution.py:61
  2095.0 101.8 %reduce-scatter.53.cloned.1.call-done = f32[24,768]{1,0:T(8,128)} async-done(((f32[768,768]{1,0:T(8,128)}), f32[24,768]{1,0:T(8,128)}) %reduce-scatter.53.cloned.1.call-update) | async-done | bytes 73744 | tf_op jit(solution)/shard_map/reduce_scatter | solution.py:62
  2198.4 102.6 %reduce-scatter.33.cloned.1.call-done = f32[24,768]{1,0:T(8,128)} async-done(((f32[768,768]{1,0:T(8,128)}), f32[24,768]{1,0:T(8,128)}) %reduce-scatter.33.cloned.1.call-update) | async-done | bytes 73744 | tf_op jit(solution)/shard_map/reduce_scatter | solution.py:60
  2302.6 144.8 %reduce-scatter.63.cloned.1.call-done = f32[40,1280]{1,0:T(8,128)} async-done(((f32[1280,1280]{1,0:T(8,128)}), f32[40,1280]{1,0:T(8,128)}) %reduce-scatter.63.cloned.1.call-update) | async-done | bytes 204816 | tf_op jit(solution)/shard_map/reduce_scatter | solution.py:63
  2449.0 142.0 %reduce-scatter.73.cloned.1.call-done = f32[40,1280]{1,0:T(8,128)} async-done(((f32[1280,1280]{1,0:T(8,128)}), f32[40,1280]{1,0:T(8,128)}) %reduce-scatter.73.cloned.1.call-update) | async-done | bytes 204816 | tf_op jit(solution)/shard_map/reduce_scatter | solution.py:64
  2592.7 142.1 %reduce-scatter.83.cloned.1.call-done = f32[40,1280]{1,0:T(8,128)} async-done(((f32[1280,1280]{1,0:T(8,128)}), f32[40,1280]{1,0:T(8,128)}) %reduce-scatter.83.cloned.1.call-update) | async-done | bytes 204816 | tf_op jit(solution)/shard_map/reduce_scatter | solution.py:65
  3098.9 90.2 %reduce-scatter.45.cloned.1.call-done = f32[24,768]{1,0:T(8,128)} async-done(((f32[768,768]{1,0:T(8,128)}), f32[24,768]{1,0:T(8,128)}) %reduce-scatter.45.cloned.1.call-update) | async-done | bytes 73744 | tf_op jit(solution)/shard_map/reduce_scatter | solution.py:61
  3190.7 102.6 %reduce-scatter.55.cloned.1.call-done = f32[24,768]{1,0:T(8,128)} async-done(((f32[768,768]{1,0:T(8,128)}), f32[24,768]{1,0:T(8,128)}) %reduce-scatter.55.cloned.1.call-update) | async-done | bytes 73744 | tf_op jit(solution)/shard_map/reduce_scatter | solution.py:62
  3294.9 101.7 %reduce-scatter.35.cloned.1.call-done = f32[24,768]{1,0:T(8,128)} async-done(((f32[768,768]{1,0:T(8,128)}), f32[24,768]{1,0:T(8,128)}) %reduce-scatter.35.cloned.1.call-update) | async-done | bytes 73744 | tf_op jit(solution)/shard_map/reduce_scatter | solution.py:60
  3398.2 144.8 %reduce-scatter.65.cloned.1.call-done = f32[40,1280]{1,0:T(8,128)} async-done(((f32[1280,1280]{1,0:T(8,128)}), f32[40,1280]{1,0:T(8,128)}) %reduce-scatter.65.cloned.1.call-update) | async-done | bytes 204816 | tf_op jit(solution)/shard_map/reduce_scatter | solution.py:63
  3544.7 142.0 %reduce-scatter.75.cloned.1.call-done = f32[40,1280]{1,0:T(8,128)} async-done(((f32[1280,1280]{1,0:T(8,128)}), f32[40,1280]{1,0:T(8,128)}) %reduce-scatter.75.cloned.1.call-update) | async-done | bytes 204816 | tf_op jit(solution)/shard_map/reduce_scatter | solution.py:64
  3688.3 142.2 %reduce-scatter.85.cloned.1.call-done = f32[40,1280]{1,0:T(8,128)} async-done(((f32[1280,1280]{1,0:T(8,128)}), f32[40,1280]{1,0:T(8,128)}) %reduce-scatter.85.cloned.1.call-update) | async-done | bytes 204816 | tf_op jit(solution)/shard_map/reduce_scatter | solution.py:65
  4006.0 54.3 all-gather.85.cloned.1.call-done
  4197.1 91.1 %reduce-scatter.47.cloned.1.call-done = f32[24,768]{1,0:T(8,128)} async-done(((f32[768,768]{1,0:T(8,128)}), f32[24,768]{1,0:T(8,128)}) %reduce-scatter.47.cloned.1.call-update) | async-done | bytes 73744 | tf_op jit(solution)/shard_map/reduce_scatter | solution.py:61
  4289.8 101.6 %reduce-scatter.57.cloned.1.call-done = f32[24,768]{1,0:T(8,128)} async-done(((f32[768,768]{1,0:T(8,128)}), f32[24,768]{1,0:T(8,128)}) %reduce-scatter.57.cloned.1.call-update) | async-done | bytes 73744 | tf_op jit(solution)/shard_map/reduce_scatter | solution.py:62
  4393.0 102.5 %reduce-scatter.37.cloned.1.call-done = f32[24,768]{1,0:T(8,128)} async-done(((f32[768,768]{1,0:T(8,128)}), f32[24,768]{1,0:T(8,128)}) %reduce-scatter.37.cloned.1.call-update) | async-done | bytes 73744 | tf_op jit(solution)/shard_map/reduce_scatter | solution.py:60
  4497.1 144.7 %reduce-scatter.67.cloned.1.call-done = f32[40,1280]{1,0:T(8,128)} async-done(((f32[1280,1280]{1,0:T(8,128)}), f32[40,1280]{1,0:T(8,128)}) %reduce-scatter.67.cloned.1.call-update) | async-done | bytes 204816 | tf_op jit(solution)/shard_map/reduce_scatter | solution.py:63
  4643.4 141.7 %reduce-scatter.77.cloned.1.call-done = f32[40,1280]{1,0:T(8,128)} async-done(((f32[1280,1280]{1,0:T(8,128)}), f32[40,1280]{1,0:T(8,128)}) %reduce-scatter.77.cloned.1.call-update) | async-done | bytes 204816 | tf_op jit(solution)/shard_map/reduce_scatter | solution.py:64
  4786.8 142.0 %reduce-scatter.87.cloned.1.call-done = f32[40,1280]{1,0:T(8,128)} async-done(((f32[1280,1280]{1,0:T(8,128)}), f32[40,1280]{1,0:T(8,128)}) %reduce-scatter.87.cloned.1.call-update) | async-done | bytes 204816 | tf_op jit(solution)/shard_map/reduce_scatter | solution.py:65
  5293.1 90.4 %reduce-scatter.49.cloned.1.call-done = f32[24,768]{1,0:T(8,128)} async-done(((f32[768,768]{1,0:T(8,128)}), f32[24,768]{1,0:T(8,128)}) %reduce-scatter.49.cloned.1.call-update) | async-done | bytes 73744 | tf_op jit(solution)/shard_map/reduce_scatter | solution.py:61
  5385.1 102.5 %reduce-scatter.59.cloned.1.call-done = f32[24,768]{1,0:T(8,128)} async-done(((f32[768,768]{1,0:T(8,128)}), f32[24,768]{1,0:T(8,128)}) %reduce-scatter.59.cloned.1.call-update) | async-done | bytes 73744 | tf_op jit(solution)/shard_map/reduce_scatter | solution.py:62
  5489.2 101.6 %reduce-scatter.39.cloned.1.call-done = f32[24,768]{1,0:T(8,128)} async-done(((f32[768,768]{1,0:T(8,128)}), f32[24,768]{1,0:T(8,128)}) %reduce-scatter.39.cloned.1.call-update) | async-done | bytes 73744 | tf_op jit(solution)/shard_map/reduce_scatter | solution.py:60
  5592.4 145.2 %reduce-scatter.69.cloned.1.call-done = f32[40,1280]{1,0:T(8,128)} async-done(((f32[1280,1280]{1,0:T(8,128)}), f32[40,1280]{1,0:T(8,128)}) %reduce-scatter.69.cloned.1.call-update) | async-done | bytes 204816 | tf_op jit(solution)/shard_map/reduce_scatter | solution.py:63
  5739.3 142.3 %reduce-scatter.79.cloned.1.call-done = f32[40,1280]{1,0:T(8,128)} async-done(((f32[1280,1280]{1,0:T(8,128)}), f32[40,1280]{1,0:T(8,128)}) %reduce-scatter.79.cloned.1.call-update) | async-done | bytes 204816 | tf_op jit(solution)/shard_map/reduce_scatter | solution.py:64
  5892.6 132.4 %reduce-scatter.89.cloned.1.call-done = f32[40,1280]{1,0:T(8,128)} async-done(((f32[1280,1280]{1,0:T(8,128)}), f32[40,1280]{1,0:T(8,128)}) %reduce-scatter.89.cloned.1.call-update) | async-done | bytes 204816 | tf_op jit(solution)/shard_map/reduce_scatter | solution.py:65
  (774 shorter events, 2349.2 us)
Async XLA Ops:
  128.0 707.3 %all-reduce.8.cloned.1.call-start = ((), (), s32[]{:S(2)}) async-start(), calls=%async_computation.96 | async-start | bytes 54001664 | tf_op jit(solution)/shard_map/psum | solution.py:318
  923.3 712.9 %reduce-scatter.81.cloned.1.call-start = ((), (), s32[]{:S(2)}) async-start(), calls=%async_computation.86 | async-start | bytes 6758400 | tf_op jit(solution)/shard_map/reduce_scatter | solution.py:65
  932.3 757.7 %all-gather.61.cloned.1.call-start = ((), (), s32[]{:S(2)}) async-start(), calls=%async_computation.47 | async-start | bytes 1216512 | tf_op jit(solution)/shard_map/all_gather | solution.py:71
  995.6 751.2 %all-gather.71.cloned.1.call-start = ((), (), s32[]{:S(2)}) async-start(), calls=%async_computation.57 | async-start | bytes 1216512 | tf_op jit(solution)/shard_map/all_gather | solution.py:74
  1099.7 703.8 %all-gather.51.cloned.1.call-start = ((), (), s32[]{:S(2)}) async-start(), calls=%async_computation.37 | async-start | bytes 1216512 | tf_op jit(solution)/shard_map/all_gather | solution.py:68
  1203.1 662.3 %all-gather.81.cloned.1.call-start = ((), (), s32[]{:S(2)}) async-start(), calls=%async_computation.67 | async-start | bytes 3379200 | tf_op jit(solution)/shard_map/all_gather | solution.py:77
  1811.1 636.3 %reduce-scatter.63.cloned.1.call-start = ((), (), s32[]{:S(2)}) async-start(), calls=%async_computation.68 | async-start | bytes 6758400 | tf_op jit(solution)/shard_map/reduce_scatter | solution.py:63
  1878.6 712.5 %reduce-scatter.73.cloned.1.call-start = ((), (), s32[]{:S(2)}) async-start(), calls=%async_computation.78 | async-start | bytes 6758400 | tf_op jit(solution)/shard_map/reduce_scatter | solution.py:64
  1940.4 794.4 %reduce-scatter.83.cloned.1.call-start = ((), (), s32[]{:S(2)}) async-start(), calls=%async_computation.88 | async-start | bytes 6758400 | tf_op jit(solution)/shard_map/reduce_scatter | solution.py:65
  2003.2 785.2 %all-gather.63.cloned.1.call-start = ((), (), s32[]{:S(2)}) async-start(), calls=%async_computation.49 | async-start | bytes 1216512 | tf_op jit(solution)/shard_map/all_gather | solution.py:71
  2094.9 749.9 %all-gather.73.cloned.1.call-start = ((), (), s32[]{:S(2)}) async-start(), calls=%async_computation.59 | async-start | bytes 1216512 | tf_op jit(solution)/shard_map/all_gather | solution.py:74
  2198.3 703.0 %all-gather.53.cloned.1.call-start = ((), (), s32[]{:S(2)}) async-start(), calls=%async_computation.39 | async-start | bytes 1216512 | tf_op jit(solution)/shard_map/all_gather | solution.py:68
  2302.5 660.3 %all-gather.83.cloned.1.call-start = ((), (), s32[]{:S(2)}) async-start(), calls=%async_computation.69 | async-start | bytes 3379200 | tf_op jit(solution)/shard_map/all_gather | solution.py:77
  2975.0 711.7 %reduce-scatter.75.cloned.1.call-start = ((), (), s32[]{:S(2)}) async-start(), calls=%async_computation.80 | async-start | bytes 6758400 | tf_op jit(solution)/shard_map/reduce_scatter | solution.py:64
  3037.3 793.2 %reduce-scatter.85.cloned.1.call-start = ((), (), s32[]{:S(2)}) async-start(), calls=%async_computation.90 | async-start | bytes 6758400 | tf_op jit(solution)/shard_map/reduce_scatter | solution.py:65
  3098.9 785.7 %all-gather.65.cloned.1.call-start = ((), (), s32[]{:S(2)}) async-start(), calls=%async_computation.51 | async-start | bytes 1216512 | tf_op jit(solution)/shard_map/all_gather | solution.py:71
  3190.6 750.8 %all-gather.75.cloned.1.call-start = ((), (), s32[]{:S(2)}) async-start(), calls=%async_computation.61 | async-start | bytes 1216512 | tf_op jit(solution)/shard_map/all_gather | solution.py:74
  3294.8 703.5 %all-gather.55.cloned.1.call-start = ((), (), s32[]{:S(2)}) async-start(), calls=%async_computation.41 | async-start | bytes 1216512 | tf_op jit(solution)/shard_map/all_gather | solution.py:68
  3398.1 662.2 %all-gather.85.cloned.1.call-start = ((), (), s32[]{:S(2)}) async-start(), calls=%async_computation.71 | async-start | bytes 3379200 | tf_op jit(solution)/shard_map/all_gather | solution.py:77
  4005.8 635.9 %reduce-scatter.67.cloned.1.call-start = ((), (), s32[]{:S(2)}) async-start(), calls=%async_computation.72 | async-start | bytes 6758400 | tf_op jit(solution)/shard_map/reduce_scatter | solution.py:63
  4072.6 712.6 %reduce-scatter.77.cloned.1.call-start = ((), (), s32[]{:S(2)}) async-start(), calls=%async_computation.82 | async-start | bytes 6758400 | tf_op jit(solution)/shard_map/reduce_scatter | solution.py:64
  4135.1 793.7 %reduce-scatter.87.cloned.1.call-start = ((), (), s32[]{:S(2)}) async-start(), calls=%async_computation.92 | async-start | bytes 6758400 | tf_op jit(solution)/shard_map/reduce_scatter | solution.py:65
  4197.1 785.5 %all-gather.67.cloned.1.call-start = ((), (), s32[]{:S(2)}) async-start(), calls=%async_computation.53 | async-start | bytes 1216512 | tf_op jit(solution)/shard_map/all_gather | solution.py:71
  4289.8 749.3 %all-gather.77.cloned.1.call-start = ((), (), s32[]{:S(2)}) async-start(), calls=%async_computation.63 | async-start | bytes 1216512 | tf_op jit(solution)/shard_map/all_gather | solution.py:74
  4393.0 702.4 %all-gather.57.cloned.1.call-start = ((), (), s32[]{:S(2)}) async-start(), calls=%async_computation.43 | async-start | bytes 1216512 | tf_op jit(solution)/shard_map/all_gather | solution.py:68
  4497.0 660.0 %all-gather.87.cloned.1.call-start = ((), (), s32[]{:S(2)}) async-start(), calls=%async_computation.73 | async-start | bytes 3379200 | tf_op jit(solution)/shard_map/all_gather | solution.py:77
  5169.1 712.4 %reduce-scatter.79.cloned.1.call-start = ((), (), s32[]{:S(2)}) async-start(), calls=%async_computation.84 | async-start | bytes 6758400 | tf_op jit(solution)/shard_map/reduce_scatter | solution.py:64
  5231.5 793.6 %reduce-scatter.89.cloned.1.call-start = ((), (), s32[]{:S(2)}) async-start(), calls=%async_computation.94 | async-start | bytes 6758400 | tf_op jit(solution)/shard_map/reduce_scatter | solution.py:65
  5293.1 786.1 %all-gather.69.cloned.1.call-start = ((), (), s32[]{:S(2)}) async-start(), calls=%async_computation.55 | async-start | bytes 1216512 | tf_op jit(solution)/shard_map/all_gather | solution.py:71
  5385.0 750.3 %all-gather.79.cloned.1.call-start = ((), (), s32[]{:S(2)}) async-start(), calls=%async_computation.65 | async-start | bytes 1216512 | tf_op jit(solution)/shard_map/all_gather | solution.py:74
  5489.1 703.2 %all-gather.59.cloned.1.call-start = ((), (), s32[]{:S(2)}) async-start(), calls=%async_computation.45 | async-start | bytes 1216512 | tf_op jit(solution)/shard_map/all_gather | solution.py:68
  5592.4 661.9 %all-gather.89.cloned.1.call-start = ((), (), s32[]{:S(2)}) async-start(), calls=%async_computation.75 | async-start | bytes 3379200 | tf_op jit(solution)/shard_map/all_gather | solution.py:77
  (199 other events, 21865.9 us)
Sparse Core Ops, SparseCore 0:
  122.2 71.2 all-reduce.9
  409.0 426.2 all-reduce.7
  895.4 98.6 reduce-scatter.40
  1000.1 98.0 reduce-scatter.50
  1103.4 98.1 reduce-scatter.30
  1203.9 144.4 reduce-scatter.60
  1350.8 141.6 reduce-scatter.70
  1494.7 141.3 reduce-scatter.80
  1995.4 97.9 reduce-scatter.42
  2098.7 98.0 reduce-scatter.52
  2202.9 97.9 reduce-scatter.32
  2303.1 144.1 reduce-scatter.62
  2449.7 141.3 reduce-scatter.72
  2593.2 141.5 reduce-scatter.82
  3091.1 97.9 reduce-scatter.44
  3195.3 97.9 reduce-scatter.54
  3298.6 97.9 reduce-scatter.34
  3398.9 144.1 reduce-scatter.64
  3545.3 141.3 reduce-scatter.74
  3689.1 141.4 reduce-scatter.84
  4190.2 97.9 reduce-scatter.46
  4293.4 98.0 reduce-scatter.56
  4397.4 98.0 reduce-scatter.36
  4497.7 144.0 reduce-scatter.66
  4643.9 141.1 reduce-scatter.76
  4787.5 141.3 reduce-scatter.86
  5285.5 97.9 reduce-scatter.48
  5389.5 98.0 reduce-scatter.58
  5492.7 98.0 reduce-scatter.38
  5593.2 144.3 reduce-scatter.68
  5740.0 141.4 reduce-scatter.78
  5884.0 141.0 reduce-scatter.88
  (36 shorter events, 1792.4 us)
where the time goes:
time: 6440 us; the launch traced here: 6430 us
  waiting for transfers between devices  5540 us (86%)
  matrix products  383 us (6%)
  blocking collectives  353 us (5%)
  other arithmetic  93.9 us (1%)
    reduce_scatter x5, waiting for transfers between devices, summed_gram(): lax.psum_scatter(grams[3], ('seq', 'opt'), scatter_dimension=0, tiled=True)  725 us
    reduce_scatter x5, waiting for transfers between devices, summed_gram(): lax.psum_scatter(grams[4], ('seq', 'opt'), scatter_dimension=0, tiled=True)  710 us
    reduce_scatter x5, waiting for transfers between devices, summed_gram(): lax.psum_scatter(grams[5], ('seq', 'opt'), scatter_dimension=0, tiled=True)  701 us
    reduce_scatter x5, waiting for transfers between devices, summed_gram(): lax.psum_scatter(grams[2], ('seq', 'opt'), scatter_dimension=0, tiled=True)  511 us
    reduce_scatter x5, waiting for transfers between devices, summed_gram(): lax.psum_scatter(grams[0], ('seq', 'opt'), scatter_dimension=0, tiled=True)  510 us
    reduce_scatter x5, waiting for transfers between devices, summed_gram(): lax.psum_scatter(grams[1], ('seq', 'opt'), scatter_dimension=0, tiled=True)  424 us
    psum x1, waiting for transfers between devices, local(): lax.psum((weight_grads[0], weight_grads[1], weight_grads[2], weight_grads...  420 us
    all_gather x5, waiting for transfers between devices, summed_gram(): lax.all_gather(shares[1].astype(jnp.bfloat16), ('seq', 'opt'), axis=0, ti...  259 us
  transfers between devices with their start and end apart: 68, of which 68 were waited for; matrix products, arithmetic and copies ran while one was open for 6% of the time, Pallas kernels for 0%

commit v1 on v0

--- a/solution.py
+++ b/solution.py
@@ -1,6 +1,8 @@
 import jax
 import jax.numpy as jnp
 from jax import lax
+from jax.experimental import pallas as pl
+from jax.experimental.pallas import tpu as pltpu
 from jax.sharding import PartitionSpec as P
 
 D_LAT = 1280
@@ -9,20 +11,13 @@
 E_IN = 768
 STEP = 10
 OUT_FAN = 4
+TILE = 256
 
 
 highest = lax.Precision.HIGHEST
 coef_one = 3.4445
 coef_two = -4.775
 coef_three = 2.0315
-
-
-def as_sent(array):
-
-    def short(part):
-        return part.astype(jnp.bfloat16) if part.dtype == jnp.float32 else part
-
-    return jax.tree.map(short, array)
 
 
 def layer_norm(values, scale_vec, offset):
@@ -54,48 +49,84 @@
     return jnp.where(usable[:, None, None, :], scores, -1e30)
 
 
-def summed_gram(currents):
-    grams = [jnp.matmul(current.T, current, precision=highest) for current in currents]
-    shares = (
-        lax.psum_scatter(grams[0], ("seq", "opt"), scatter_dimension=0, tiled=True),
-        lax.psum_scatter(grams[1], ("seq", "opt"), scatter_dimension=0, tiled=True),
-        lax.psum_scatter(grams[2], ("seq", "opt"), scatter_dimension=0, tiled=True),
-        lax.psum_scatter(grams[3], ("seq", "opt"), scatter_dimension=0, tiled=True),
-        lax.psum_scatter(grams[4], ("seq", "opt"), scatter_dimension=0, tiled=True),
-        lax.psum_scatter(grams[5], ("seq", "opt"), scatter_dimension=0, tiled=True),
-    )
-    return (
-        lax.all_gather(shares[0].astype(jnp.bfloat16), ("seq", "opt"), axis=0, tiled=True).astype(
-            jnp.float32
-        ),
-        lax.all_gather(shares[1].astype(jnp.bfloat16), ("seq", "opt"), axis=0, tiled=True).astype(
-            jnp.float32
-        ),
-        lax.all_gather(shares[2].astype(jnp.bfloat16), ("seq", "opt"), axis=0, tiled=True).astype(
-            jnp.float32
-        ),
-        lax.all_gather(shares[3].astype(jnp.bfloat16), ("seq", "opt"), axis=0, tiled=True).astype(
-            jnp.float32
-        ),
-        lax.all_gather(shares[4].astype(jnp.bfloat16), ("seq", "opt"), axis=0, tiled=True).astype(
-            jnp.float32
-        ),
-        lax.all_gather(shares[5].astype(jnp.bfloat16), ("seq", "opt"), axis=0, tiled=True).astype(
-            jnp.float32
-        ),
-    )
-
-
-def newton_step(currents, grams):
-    results = []
-    for current, gram in zip(currents, grams):
-        product = jnp.matmul(current, gram, precision=highest)
-        results.append(
-            coef_one * current
-            + coef_two * product
-            + coef_three * jnp.matmul(product, gram, precision=highest)
-        )
-    return results
+def newton_body(rows_ref, out_ref, wide, low, gram, poly, total):
+    count, side = rows_ref.shape
+    row_tiles, side_tiles = count // TILE, side // TILE
+    total[0] = 0.0
+
+    def add_squares(tile, carry):
+        block = rows_ref[pl.ds(tile * TILE, TILE), :].astype(jnp.float32)
+        total[0] = total[0] + jnp.sum(block * block)
+        return carry
+
+    lax.fori_loop(0, row_tiles, add_squares, 0)
+    scale = 1.0 / (jnp.sqrt(jnp.full((1, 1), total[0], jnp.float32)) + 1e-07)
+
+    def normalise(tile, carry):
+        block = rows_ref[pl.ds(tile * TILE, TILE), :].astype(jnp.float32) * scale
+        wide[pl.ds(tile * TILE, TILE), :] = block
+        low[pl.ds(tile * TILE, TILE), :] = block.astype(jnp.bfloat16)
+        return carry
+
+    lax.fori_loop(0, row_tiles, normalise, 0)
+
+    def sweep(index, carry):
+        for i in range(side_tiles):
+            own = slice(i * TILE, (i + 1) * TILE)
+            for j in range(i, side_tiles):
+                other = slice(j * TILE, (j + 1) * TILE)
+                block = lax.dot_general(
+                    low[:, own],
+                    low[:, other],
+                    (((0,), (0,)), ((), ())),
+                    preferred_element_type=jnp.float32,
+                )
+                gram[own, other] = block.astype(jnp.bfloat16)
+                if j > i:
+                    gram[other, own] = block.T.astype(jnp.bfloat16)
+        for i in range(side_tiles):
+            own = slice(i * TILE, (i + 1) * TILE)
+            block = coef_three * jnp.dot(
+                gram[own, :], gram[:, i * TILE :], preferred_element_type=jnp.float32
+            ) + coef_two * gram[own, i * TILE :].astype(jnp.float32)
+            poly[own, i * TILE :] = block.astype(jnp.bfloat16)
+            for j in range(i + 1, side_tiles):
+                part = block[:, (j - i) * TILE : (j - i + 1) * TILE]
+                poly[j * TILE : (j + 1) * TILE, own] = part.T.astype(jnp.bfloat16)
+
+        def update(tile, inner):
+            rows = pl.ds(tile * TILE, TILE)
+            block = coef_one * wide[rows, :] + jnp.dot(
+                low[rows, :], poly[...], preferred_element_type=jnp.float32
+            )
+            wide[rows, :] = block
+            low[rows, :] = block.astype(jnp.bfloat16)
+            return inner
+
+        lax.fori_loop(0, row_tiles, update, 0)
+        return carry
+
+    lax.fori_loop(0, 5, sweep, 0)
+    out_ref[...] = low[...]
+
+
+def newton(rows):
+    shape = rows.shape
+    return pl.pallas_call(
+        newton_body,
+        out_shape=jax.ShapeDtypeStruct(shape, jnp.bfloat16),
+        in_specs=[pl.BlockSpec(memory_space=pltpu.VMEM)],
+        out_specs=pl.BlockSpec(memory_space=pltpu.VMEM),
+        scratch_shapes=[
+            pltpu.VMEM(shape, jnp.float32),
+            pltpu.VMEM(shape, jnp.bfloat16),
+            pltpu.VMEM((shape[1], shape[1]), jnp.bfloat16),
+            pltpu.VMEM((shape[1], shape[1]), jnp.bfloat16),
+            pltpu.SMEM((1,), jnp.float32),
+        ],
+        compiler_params=pltpu.CompilerParams(vmem_limit_bytes=60 * 2**20),
+        name="newton",
+    )(rows)
 
 
 def adam_update(param, gradient, first, second, step_rate, decay):
@@ -315,58 +346,53 @@
         grad_up_w,
         grad_down_w,
     )
-    reduced_all = lax.psum(
-        (
-            weight_grads[0],
-            weight_grads[1],
-            weight_grads[2],
-            weight_grads[3],
-            weight_grads[4],
-            weight_grads[5],
-            lat_vec_grad,
-            in_vec_grad,
-            latent_grad,
-        ),
-        ("seq", "opt"),
-    )
-    row_grads = [
-        lax.dynamic_slice_in_dim(
-            reduced, opt_index * (reduced.shape[0] // opt_size), reduced.shape[0] // opt_size, 0
-        )
-        for reduced in reduced_all[:6]
-    ]
-    lat_vec_sum, in_vec_sum, latent_sum = (reduced_all[6], reduced_all[7], reduced_all[8])
     masters = (w_query, w_key, w_value, w_out, w_up, w_down)
     moments = (mom_query, mom_key, mom_value, mom_out, mom_up, mom_down)
-    moments_new = [0.95 * moment + gradient for moment, gradient in zip(moments, row_grads)]
-    pieces = [
-        lax.dynamic_slice_in_dim(
-            moment, seq_index * (moment.shape[0] // seq_size), moment.shape[0] // seq_size, 0
-        )
-        for moment in moments_new
+    first_here = jnp.where(seq_index == 0, 0.95, 0.0)
+    with_moment = []
+    for gradient, moment in zip(weight_grads, moments):
+        start = opt_index * moment.shape[0]
+        rows = lax.dynamic_slice_in_dim(gradient, start, moment.shape[0], 0) + first_here * moment
+        with_moment.append(
+            lax.dynamic_update_slice(gradient, rows, (start, zero_index)).astype(jnp.bfloat16)
+        )
+    summed_low = lax.psum(tuple(with_moment), ("seq", "opt"))
+    lat_vec_sum, in_vec_sum, latent_sum = lax.psum(
+        (lat_vec_grad, in_vec_grad, latent_grad), ("seq", "opt")
+    )
+    moments_new = [
+        lax.dynamic_slice_in_dim(summed, opt_index * moment.shape[0], moment.shape[0], 0).astype(
+            jnp.float32
+        )
+        for summed, moment in zip(summed_low, moments)
     ]
-    squares = lax.psum(
-        (
-            jnp.sum(pieces[0] * pieces[0]),
-            jnp.sum(pieces[1] * pieces[1]),
-            jnp.sum(pieces[2] * pieces[2]),
-            jnp.sum(pieces[3] * pieces[3]),
-            jnp.sum(pieces[4] * pieces[4]),
-            jnp.sum(pieces[5] * pieces[5]),
-        ),
-        ("seq", "opt"),
-    )
-    thin_rows = [piece / (jnp.sqrt(square) + 1e-07) for piece, square in zip(pieces, squares)]
-    for sweep in range(5):
-        thin_rows = newton_step(thin_rows, summed_gram(thin_rows))
-    currents = (
-        lax.all_gather(as_sent(thin_rows[0]), "seq", axis=0, tiled=True),
-        lax.all_gather(as_sent(thin_rows[1]), "seq", axis=0, tiled=True),
-        lax.all_gather(as_sent(thin_rows[2]), "seq", axis=0, tiled=True),
-        lax.all_gather(as_sent(thin_rows[3]), "seq", axis=0, tiled=True),
-        lax.all_gather(as_sent(thin_rows[4]), "seq", axis=0, tiled=True),
-        lax.all_gather(as_sent(thin_rows[5]), "seq", axis=0, tiled=True),
-    )
+
+    def padded(index):
+        def pick():
+            matrix = summed_low[index].T if index == 3 else summed_low[index]
+            return jnp.pad(
+                matrix, ((0, width_lat - matrix.shape[0]), (0, width_lat - matrix.shape[1]))
+            )
+
+        return pick
+
+    slot = seq_index % 8
+    own_matrix = lax.switch(jnp.minimum(slot, 5), [padded(index) for index in range(6)])
+    own_result = newton(own_matrix)
+    own_result = lax.cond(slot == 3, lambda: own_result.T, lambda: own_result)
+    mine = jnp.stack(
+        [
+            lax.dynamic_slice_in_dim(own_result, opt_index * height, width_lat // opt_size, 0)
+            for height in (width_in // opt_size, width_lat // opt_size)
+        ]
+    )
+    is_wide = (slot == 0) | (slot >= 4)
+    mine = jnp.where(is_wide, mine[1], mine[0])
+    spread = lax.all_gather(mine, "seq", axis=0, tiled=False)
+    currents = [
+        spread[index, : moment.shape[0], : moment.shape[1]].astype(jnp.float32)
+        for index, moment in enumerate(moments)
+    ]
     fans = (D_LAT, E_IN, E_IN, OUT_FAN, D_LAT, D_LAT)
     sides = (D_LAT, E_IN, E_IN, D_LAT, D_LAT, D_LAT)
     new_masters = []

time: 6440 us -> 908 us (0.14)
  waiting for transfers between devices: 5540 us -> 488 us
  matrix products: 383 us -> 73.8 us
  blocking collectives: 353 us -> 164 us
    reduce_scatter x30 -> x0, waiting for transfers between devices: 3580 us -> none  [the longest x5 725 us: summed_gram(): lax.psum_scatter(grams[3], ('seq', 'opt'), scatter_dimension=0, tiled=True)]
    all_gather x30 -> x1, waiting for transfers between devices: 1370 us -> 87.1 us  [local(): spread = lax.all_gather(mine, 'seq', axis=0, tiled=False)]
    dot_general x90 -> x0, matrix products: 305 us -> none  [the longest x30 165 us: summed_gram(): jnp.matmul(current.T, current, precision=highest)]
    all_gather x6 -> x0, blocking collectives: 191 us -> none  [the longest x1 33 us: local(): lax.all_gather(as_sent(thin_rows[4]), 'seq', axis=0, tiled=True)]
    psum x1 -> x2, waiting for transfers between devices: 420 us -> 235 us  [the longest x1 232 us: local(): summed_low = lax.psum(tuple(with_moment), ('seq', 'opt'))]
  transfers between devices with their start and end apart: 68 -> 10, of which waited for: 68 -> 10; matrix products, arithmetic and copies ran while one was open for 6% -> 10% of each run, Pallas kernels for 0% -> 7%
where the time goes in v1:
time: 908 us; the launch traced here: 900 us
  waiting for transfers between devices  488 us (54%)
  blocking collectives  164 us (18%)
  matrix products  73.8 us (8%)
  other arithmetic  63.4 us (7%)
  Pallas kernels  60.1 us (7%)
  local copies, waits for them, and re-layouts  33.3 us (4%)
  between operations  16.6 us (2%)
    psum x1, waiting for transfers between devices, local(): summed_low = lax.psum(tuple(with_moment), ('seq', 'opt'))  232 us
    all_gather x1, waiting for transfers between devices, local(): spread = lax.all_gather(mine, 'seq', axis=0, tiled=False)  87.1 us
    all_gather x2, blocking collectives, local(): lax.all_gather(grad_own, 'seq', axis=1, tiled=True).astype(jnp.float32)  62.4 us
    pallas_call x1, Pallas kernels, newton(): pl.pallas_call(newton_body, out_shape=jax.ShapeDtypeStruct(shape, jnp.bfl...  60.1 us
    psum x1, blocking collectives, local(): lax.psum((lat_vec_grad, in_vec_grad, latent_grad), ('seq', 'opt'))  46.2 us
    psum x1, waiting for transfers between devices, local(): lax.psum(jnp.einsum('bhns,bshd->bnhd', weights_low, value_heads, preferre...  45.3 us
    pmax x1, blocking collectives, local(): row_max = lax.pmax(jnp.max(masked, axis=-1), 'seq')  37.2 us
    all_gather x1, waiting for transfers between devices, local(): lax.all_gather(w_up.astype(jnp.bfloat16), 'opt', axis=0, tiled=True)  27.9 us
  transfers between devices with their start and end apart: 10, of which 10 were waited for; matrix products, arithmetic and copies ran while one was open for 10% of the time, Pallas kernels for 7%

profile of v1, /device:TPU:0, one launch (start us, length us, event | category | flops | bytes accessed | tf_op | source)
XLA Modules:
  0.0 900.0 jit_solution(13280075891281778603)
XLA Ops:
  16.0 14.4 %all-gather.11.cloned.1.call-done = bf16[768,768]{1,0:T(8,128)(2,1)} async-done(((bf16[192,768]{1,0:T(8,128)(2,1)}), bf16[768,768]{1,0:T(8,128)(2,1)}) %all-gather.11.cloned.1.call-update) | async-done | bytes 1179664 | tf_op jit(solution)/shard_map/all_gather | solution.py:168
  32.8 17.2 %all-gather.13.cloned.1.call-done = bf16[768,768]{1,0:T(8,128)(2,1)} async-done(((bf16[192,768]{1,0:T(8,128)(2,1)}), bf16[768,768]{1,0:T(8,128)(2,1)}) %all-gather.13.cloned.1.call-update) | async-done | bytes 1179664 | tf_op jit(solution)/shard_map/all_gather | solution.py:169
  56.2 2.7 fusion
  60.1 14.0 %all-gather.15.cloned.1.call-done = bf16[1280,768]{1,0:T(8,128)(2,1)} async-done(((bf16[320,768]{1,0:T(8,128)(2,1)}), bf16[1280,768]{1,0:T(8,128)(2,1)}) %all-gather.15.cloned.1.call-update) | async-done | bytes 1966096 | tf_op jit(solution)/shard_map/all_gather | solution.py:167
  80.3 37.2 %all-reduce.5 = (f32[8,256]{1,0:T(8,128)S(1)}, f32[8,256]{1,0:T(8,128)S(1)}) all-reduce(f32[8,256]{1,0:T(8,128)S(1)} %get-tuple-element.130, f32[8,256]{1,0:T(8,128)S(1)} %get-tuple-element.132), channel_id=1, replica_groups=mesh['seq'=8,'opt'=4] {'seq'}, use_global_device_ids=true, to_apply=%region_14.15 | all-reduce | flops 4096 | bytes 32768 | tf_op jit(solution)/shard_map/pmax | solution.py:221
  117.5 3.2 fusion.19
  130.2 17.9 %all-reduce.7 = (bf16[1,8,256]{2,1,0:T(8,128)(2,1)S(1)}, bf16[1,8,256]{2,1,0:T(8,128)(2,1)S(1)}) all-reduce(bf16[1,8,256]{2,1,0:T(8,128)(2,1)S(1)} %bitcast.383, bf16[1,8,256]{2,1,0:T(8,128)(2,1)S(1)} %bitcast.384), channel_id=1, replica_groups=mesh['seq'=8,'opt'=4] {'seq'}, use_global_device_ids=true, to_apply=%region_17.18 | all-reduce | flops 4096 | bytes 16384 | tf_op jit(solution)/shard_map/psum | solution.py:231
  148.2 45.3 %all-reduce.17.cloned.1.call-done = (bf16[1,256,8,96]{1,3,2,0:T(8,128)(2,1)}, bf16[1,256,8,96]{1,3,2,0:T(8,128)(2,1)}) async-done(((bf16[1,256,8,96]{1,3,2,0:T(8,128)(2,1)}, bf16[1,256,8,96]{1,3,2,0:T(8,128)(2,1)}), (bf16[1,256,8,96]{1,3,2,0:T(8,128)(2,1)}, bf16[1,256,8,96]{1,3,2,0:T(8,128)(2,1)})) %all-reduce.17.cloned.1.call-update) | async-done | bytes 786448 | tf_op jit(solution)/shard_map/psum | solution.py:225
  196.0 20.4 %all-gather.17.cloned.1.call-done = bf16[768,1280]{1,0:T(8,128)(2,1)} async-done(((bf16[192,1280]{1,0:T(8,128)(2,1)}), bf16[768,1280]{1,0:T(8,128)(2,1)}) %all-gather.17.cloned.1.call-update) | async-done | bytes 1966096 | tf_op jit(solution)/shard_map/all_gather | solution.py:170
  219.9 27.9 %all-gather.19.cloned.1.call-done = bf16[1280,1280]{1,0:T(8,128)(2,1)} async-done(((bf16[320,1280]{1,0:T(8,128)(2,1)}), bf16[1280,1280]{1,0:T(8,128)(2,1)}) %all-gather.19.cloned.1.call-update) | async-done | bytes 3276816 | tf_op jit(solution)/shard_map/all_gather | solution.py:171
  247.8 3.6 convolution_add_fusion.5
  252.8 26.5 %all-gather.21.cloned.1.call-done = bf16[1280,1280]{1,0:T(8,128)(2,1)} async-done(((bf16[320,1280]{1,0:T(8,128)(2,1)}), bf16[1280,1280]{1,0:T(8,128)(2,1)}) %all-gather.21.cloned.1.call-update) | async-done | bytes 3276816 | tf_op jit(solution)/shard_map/all_gather | solution.py:172
  279.3 3.8 convert_reduce_fusion.4
  289.3 31.2 %all-gather = bf16[256,768]{1,0:T(8,128)(2,1)S(1)} all-gather(bf16[32,768]{1,0:T(8,128)(2,1)S(1)} %convolution_convert_fusion.8), channel_id=2, replica_groups=mesh['seq'=8,'opt'=4] {'seq'}, dimensions={0}, use_global_device_ids=true | all-gather | bytes 442368 | tf_op jit(solution)/shard_map/all_gather | solution.py:286
  327.9 2.6 fusion.125
  330.6 3.8 fusion.136
  334.4 4.0 fusion.112
  339.0 31.2 %all-gather.1 = bf16[256,768]{1,0:T(8,128)(2,1)S(1)} all-gather(bf16[32,768]{1,0:T(8,128)(2,1)S(1)} %convolution_convert_fusion.7), channel_id=3, replica_groups=mesh['seq'=8,'opt'=4] {'seq'}, dimensions={0}, use_global_device_ids=true | all-gather | bytes 442368 | tf_op jit(solution)/shard_map/all_gather | solution.py:286
  400.7 5.2 multiply_reduce_fusion
  408.3 232.2 %all-reduce.15.cloned.1.call-done = (bf16[1280,768]{1,0:T(8,128)(2,1)}, bf16[768,768]{1,0:T(8,128)(2,1)}, bf16[768,768]{1,0:T(8,128)(2,1)}, bf16[768,1280]{1,0:T...) async-done(((bf16[1280,768]{1,0:T(8,128)(2,1)}, bf16[768,768]{1,0:T(8,128)(2,1)}, bf16[768,768]{1,0:T(8,128)(2,1)}, bf16[768,1280]{1,0:T(8,128)(2,1)}, ...) | async-done | bytes 12845072 | tf_op jit(solution)/shard_map/psum | solution.py:359
  640.4 7.7 conditional.2
  640.4 4.0 copy.121
  644.4 3.5 pad.10
  648.1 5.7 copy.107.rows_ref
  653.9 60.1 %newton.1 = bf16[1280,1280]{1,0:T(8,128)(2,1)} custom-call(bf16[1280,1280]{1,0:T(8,128)(2,1)} %copy.107.rows_ref), custom_call_target="tpu_custom_call" | custom-call | tf_op jit(solution)/shard_map/newton/pallas_call | solution.py:115
  714.1 2.6 dynamic-slice_select_fusion
  717.0 2.8 fusion.66
  722.1 46.2 %all-reduce.4 = (f32[6,1280]{1,0:T(8,128)S(1)}, f32[2,768]{1,0:T(2,128)S(1)}) all-reduce(f32[6,1280]{1,0:T(8,128)S(1)} %stack.44, f32[2,768]{1,0:T(2,128)S(1)} %pad_maximum_fusion.2), channel_id=1, replica_groups=mesh['seq'=8,'opt'=4] {'seq','opt'}, use_global_device_ids=true, to_apply=%region_54.55 | all-reduce | flops 9216 | bytes 73728 | tf_op jit(solution)/shard_map/psum | solution.py:360
  775.3 3.1 all-reduce.13.cloned.1.call-done
  778.4 4.2 add_subtract_fusion
  795.4 87.1 %all-gather.23.cloned.1.call-done = bf16[2560,1280]{1,0:T(8,128)(2,1)} async-done(((bf16[320,1280]{1,0:T(8,128)(2,1)}), bf16[2560,1280]{1,0:T(8,128)(2,1)}) %all-gather.23.cloned.1.call-update) | async-done | bytes 6553616 | tf_op jit(solution)/shard_map/all_gather | solution.py:391
  889.2 3.5 convert_subtract_fusion
  (449 shorter events, 116.1 us)
Async XLA Ops:
  7.2 23.2 %all-gather.11.cloned.1.call-start = ((), (), s32[]{:S(2)}) async-start(), calls=%async_computation | async-start | bytes 1474560 | tf_op jit(solution)/shard_map/all_gather | solution.py:168
  9.2 40.8 %all-gather.13.cloned.1.call-start = ((), (), s32[]{:S(2)}) async-start(), calls=%async_computation.1 | async-start | bytes 1474560 | tf_op jit(solution)/shard_map/all_gather | solution.py:169
  11.2 62.8 %all-gather.15.cloned.1.call-start = ((), (), s32[]{:S(2)}) async-start(), calls=%async_computation.2 | async-start | bytes 2457600 | tf_op jit(solution)/shard_map/all_gather | solution.py:167
  12.1 181.4 %all-reduce.17.cloned.1.call-start = ((), (), s32[]{:S(2)}) async-start(), calls=%async_computation.9 | async-start | bytes 1572864 | tf_op jit(solution)/shard_map/psum | solution.py:225
  12.4 43.7 %copy-start.81 = (f32[768]{0:T(1024)}, f32[768]{0:T(1024)S(1)}, u32[]{:S(2)}) copy-start(f32[768]{0:T(1024)S(1)} %get-tuple-element.83) | copy-start | bytes 9220
  12.4 43.7 %copy-start.85 = (f32[768]{0:T(1024)}, f32[768]{0:T(1024)S(1)}, u32[]{:S(2)}) copy-start(f32[768]{0:T(1024)S(1)} %get-tuple-element.84) | copy-start | bytes 9220
  13.2 60.9 %copy-start.91 = (f32[1280]{0:T(1024)}, f32[1280]{0:T(1024)S(1)}, u32[]{:S(2)}) copy-start(f32[1280]{0:T(1024)S(1)} %get-tuple-element.80) | copy-start | bytes 15364
  13.2 39.3 %copy-start.97 = (f32[256]{0:T(256)}, f32[256]{0:T(256)S(1)}, u32[]{:S(2)}) copy-start(f32[256]{0:T(256)S(1)} %get-tuple-element.145) | copy-start | bytes 3076
  13.2 43.0 %copy-start.105 = (f32[256]{0:T(256)}, f32[256]{0:T(256)S(1)}, u32[]{:S(2)}) copy-start(f32[256]{0:T(256)S(1)} %get-tuple-element.146) | copy-start | bytes 3076
  14.3 59.7 %copy-start.93 = (f32[256]{0:T(256)}, f32[256]{0:T(256)S(1)}, u32[]{:S(2)}) copy-start(f32[256]{0:T(256)S(1)} %broadcast_multiply_fusion.2) | copy-start | bytes 3076
  14.6 37.8 %copy-start.113 = (f32[256]{0:T(256)}, f32[256]{0:T(256)S(1)}, u32[]{:S(2)}) copy-start(f32[256]{0:T(256)S(1)} %add_rsqrt_fusion) | copy-start | bytes 3076
  14.6 59.4 %copy-start.103 = (f32[256]{0:T(256)}, f32[256]{0:T(256)S(1)}, u32[]{:S(2)}) copy-start(f32[256]{0:T(256)S(1)} %add_rsqrt_fusion.1) | copy-start | bytes 3076
  14.6 41.5 %copy-start.115 = (f32[256]{0:T(256)}, f32[256]{0:T(256)S(1)}, u32[]{:S(2)}) copy-start(f32[256]{0:T(256)S(1)} %add_rsqrt_fusion.2) | copy-start | bytes 3076
  16.0 112.1 %copy-start.133 = (pred[256]{0:T(512)(128)(4,1)}, pred[256]{0:T(512)(128)(4,1)S(1)}, u32[]{:S(2)}) copy-start(pred[256]{0:T(512)(128)(4,1)S(1)} %get-tuple-element.147) | copy-start | bytes 772
  16.0 112.7 %copy-start.135 = (pred[256]{0:T(512)(128)(4,1)}, pred[256]{0:T(512)(128)(4,1)S(1)}, u32[]{:S(2)}) copy-start(pred[256]{0:T(512)(128)(4,1)S(1)} %get-tuple-element.148) | copy-start | bytes 772
  80.3 40.4 %copy-start.13 = (f32[8,256,256]{2,1,0:T(8,128)S(1)}, f32[8,256,256]{2,1,0:T(8,128)}, u32[]{:S(2)}) copy-start(f32[8,256,256]{2,1,0:T(8,128)} %get-tuple-element.133) | copy-start | bytes 6291460
  122.1 94.3 %all-gather.17.cloned.1.call-start = ((), (), s32[]{:S(2)}) async-start(), calls=%async_computation.3 | async-start | bytes 2457600 | tf_op jit(solution)/shard_map/all_gather | solution.py:170
  124.4 123.5 %all-gather.19.cloned.1.call-start = ((), (), s32[]{:S(2)}) async-start(), calls=%async_computation.4 | async-start | bytes 4096000 | tf_op jit(solution)/shard_map/all_gather | solution.py:171
  125.4 153.9 %all-gather.21.cloned.1.call-start = ((), (), s32[]{:S(2)}) async-start(), calls=%async_computation.5 | async-start | bytes 4096000 | tf_op jit(solution)/shard_map/all_gather | solution.py:172
  128.0 512.4 %all-reduce.15.cloned.1.call-start = ((), (), s32[]{:S(2)}) async-start(), calls=%async_computation.8 | async-start | bytes 25690112 | tf_op jit(solution)/shard_map/psum | solution.py:359
  148.2 70.5 %copy-start.99 = (bf16[1,8,256]{2,1,0:T(8,128)(2,1)}, bf16[1,8,256]{2,1,0:T(8,128)(2,1)S(1)}, u32[]{:S(2)}) copy-start(bf16[1,8,256]{2,1,0:T(8,128)(2,1)S(1)} %get-tuple-element.97) | copy-start | bytes 12292
  148.2 70.5 %copy-start.101 = (bf16[1,8,256]{2,1,0:T(8,128)(2,1)}, bf16[1,8,256]{2,1,0:T(8,128)(2,1)S(1)}, u32[]{:S(2)}) copy-start(bf16[1,8,256]{2,1,0:T(8,128)(2,1)S(1)} %get-tuple-element.98) | copy-start | bytes 12292
  148.2 70.5 %copy-start.79 = (f32[256,8]{0,1:T(8,128)}, f32[256,8]{0,1:T(8,128)S(1)}, u32[]{:S(2)}) copy-start(f32[256,8]{0,1:T(8,128)S(1)} %convert_bitcast_fusion.5) | copy-start | bytes 24580
  219.6 110.9 %copy-start.21 = (f32[32,1280]{1,0:T(8,128)}, f32[32,1280]{1,0:T(8,128)S(1)}, u32[]{:S(2)}) copy-start(f32[32,1280]{1,0:T(8,128)S(1)} %get-tuple-element.137) | copy-start | bytes 491524
  219.6 33.2 %copy-start.110 = (f32[32]{0:T(128)}, f32[32]{0:T(128)S(1)}, u32[]{:S(2)}) copy-start(f32[32]{0:T(128)S(1)} %broadcast_multiply_fusion.14) | copy-start | bytes 388
  219.8 33.0 %copy-start.122 = (f32[32]{0:T(128)}, f32[32]{0:T(128)S(1)}, u32[]{:S(2)}) copy-start(f32[32]{0:T(128)S(1)} %add_rsqrt_fusion.3) | copy-start | bytes 388
  219.9 32.9 %copy-start.125 = (f32[32]{0:T(128)}, f32[32]{0:T(128)S(1)}, u32[]{:S(2)}) copy-start(f32[32]{0:T(128)S(1)} %add_rsqrt_fusion.4) | copy-start | bytes 388
  400.7 377.8 %all-reduce.13.cloned.1.call-start = ((), (), s32[]{:S(2)}) async-start(), calls=%async_computation.6 | async-start | bytes 2621440 | tf_op jit(solution)/shard_map/psum | solution.py:360
  408.2 474.3 %all-gather.23.cloned.1.call-start = ((), (), s32[]{:S(2)}) async-start(), calls=%async_computation.7 | async-start | bytes 7372800 | tf_op jit(solution)/shard_map/all_gather | solution.py:391
  790.4 92.1 %copy-start.28 = (f32[320,768]{1,0:T(8,128)S(1)}, f32[320,768]{1,0:T(8,128)}, u32[]{:S(2)}) copy-start(f32[320,768]{1,0:T(8,128)} %param.40) | copy-start | bytes 2949124
  792.9 91.8 %copy-start.41 = (f32[192,768]{1,0:T(8,128)S(1)}, f32[192,768]{1,0:T(8,128)}, u32[]{:S(2)}) copy-start(f32[192,768]{1,0:T(8,128)} %param.41) | copy-start | bytes 1769476
  792.9 91.8 %copy-start.42 = (f32[192,768]{1,0:T(8,128)S(1)}, f32[192,768]{1,0:T(8,128)}, u32[]{:S(2)}) copy-start(f32[192,768]{1,0:T(8,128)} %param.42) | copy-start | bytes 1769476
  (123 other events, 520.1 us)
Sparse Core Ops, SparseCore 0:
  10.2 20.1 all-gather.10
  32.5 17.4 all-gather.12
  52.1 21.8 all-gather.14
  122.3 71.1 all-reduce.16
  195.6 20.8 all-gather.16
  218.5 29.2 all-gather.18
  250.0 29.2 all-gather.20
  400.8 239.5 all-reduce.14
  647.3 131.0 all-reduce.12
  781.3 101.1 all-gather.22

commit v2 on v1

--- a/solution.py
+++ b/solution.py
@@ -1,3 +1,6 @@
+import functools
+import types
+
 import jax
 import jax.numpy as jnp
 from jax import lax
@@ -12,6 +15,10 @@
 STEP = 10
 OUT_FAN = 4
 TILE = 256
+PARTS = 4
+ORDER = (4, 5, 3, 0, 1, 2)
+VMEM_LIMIT = 60 * 2**20
+MESH = pl.DeviceIdType.MESH
 
 
 highest = lax.Precision.HIGHEST
@@ -129,11 +136,1054 @@
     )(rows)
 
 
+CORE, X, Y, Z0, Z1 = range(5)
+LEAD, ROWS, COLS = range(3)
+
+
+def partners(seq, opt):
+    bits = (opt % 2, opt // 2, seq % 2, (seq // 2) % 2, seq // 4)
+    steps = ((0, 1), (0, 2), (1, 0), (2, 0), (4, 0))
+    targets = [
+        (seq + (1 - 2 * bit) * along_seq, opt + (1 - 2 * bit) * along_opt)
+        for bit, (along_seq, along_opt) in zip(bits, steps)
+    ]
+    return bits, targets
+
+
+def greet(targets):
+    barrier = pltpu.get_barrier_semaphore()
+    for target in targets:
+        pl.semaphore_signal(barrier, inc=1, device_id=target, device_id_type=MESH)
+    pl.semaphore_wait(barrier, len(targets))
+
+
+class Courier:
+    def __init__(self, send_sem, recv_sem):
+        self.send_sem, self.recv_sem, self.started = send_sem, recv_sem, []
+
+    def send(self, source, target_ref, device):
+        index = len(self.started)
+        copy = pltpu.make_async_remote_copy(
+            src_ref=source,
+            dst_ref=target_ref,
+            send_sem=self.send_sem.at[index],
+            recv_sem=self.recv_sem.at[index],
+            device_id=device,
+            device_id_type=MESH,
+        )
+        copy.start()
+        self.started.append(copy)
+        return copy
+
+    def finish(self):
+        for copy in self.started:
+            copy.wait_send()
+
+
+class Loader:
+    def __init__(self, sem):
+        self.sem, self.count = sem, 0
+
+    def start(self, source, target):
+        copy = pltpu.make_async_copy(source, target, self.sem.at[self.count])
+        self.count += 1
+        copy.start()
+        return copy
+
+
+def rows_at(start, count, unit=16):
+    return pl.ds(pl.multiple_of(start, unit), count)
+
+
+def lanes_at(start, count):
+    return pl.ds(pl.multiple_of(start, 128), count)
+
+
+def dot_nn(left, right):
+    return jnp.dot(left, right, preferred_element_type=jnp.float32)
+
+
+def dot_nt(left, right):
+    return lax.dot_general(
+        left, right, (((1,), (1,)), ((), ())), preferred_element_type=jnp.float32
+    )
+
+
+def dot_tn(left, right):
+    return lax.dot_general(
+        left, right, (((0,), (0,)), ((), ())), preferred_element_type=jnp.float32
+    )
+
+
+def named(keys, refs):
+    return types.SimpleNamespace(**dict(zip(keys, refs)))
+
+
+def low(values):
+    return values.astype(jnp.bfloat16)
+
+
+def wide(values):
+    return values.astype(jnp.float32)
+
+
+def head_lanes(first, shape):
+    row = lax.broadcasted_iota(jnp.int32, shape, 0) - first
+    column = lax.broadcasted_iota(jnp.int32, shape, 1)
+    inside = (row >= 0) & (row < HEADS)
+    inside &= (column >= row * HEAD_DIM) & (column < (row + 1) * HEAD_DIM)
+    return inside.astype(jnp.float32)
+
+
+def pass_body(keys, *refs):
+    r = named(keys, refs)
+    seq, opt = lax.axis_index("seq"), lax.axis_index("opt")
+    bits, targets = partners(seq, opt)
+    core, y = bits[CORE], bits[Y]
+    opt_x = targets[X][1]
+    ring = [((seq + step) % 8, opt) for step in range(1, 8)]
+    micro, span = r.usable.shape[0], r.usable.shape[2]
+    width = r.in_low.shape[1]
+    lat_count, width_lat = r.latents.shape
+    own = lat_count // 8
+    scale = HEAD_DIM ** (-0.5)
+    load = Loader(r.local)
+    loads = [
+        load.start(source, target)
+        for source, target in (
+            (r.w_key, r.f_key),
+            (r.w_value, r.f_value),
+            (r.w_query, r.f_query),
+            (r.w_out, r.f_out),
+            (r.w_up, r.f_up),
+            (r.w_down, r.f_down),
+        )
+    ]
+    greet([targets[CORE], targets[X], *ring])
+    courier = Courier(r.send, r.recv)
+
+    def begin(full, rows):
+        block = full.at[rows_at(opt * rows, rows)]
+        half = full.at[rows_at(opt * rows + y * (rows // 2), rows // 2)]
+        return [
+            courier.send(half, half, targets[X]),
+            courier.send(block, block, targets[CORE]),
+        ]
+
+    def relay(full, rows, state):
+        state[0].wait_recv()
+        half = full.at[rows_at(opt_x * rows + y * (rows // 2), rows // 2)]
+        state.append(courier.send(half, half, targets[Y]))
+        state.append(courier.send(half, half, targets[CORE]))
+
+    def relay_more(full, rows, state):
+        state[2].wait_recv()
+        half = full.at[rows_at(opt_x * rows + (1 - y) * (rows // 2), rows // 2)]
+        state.append(courier.send(half, half, targets[CORE]))
+
+    def complete(state):
+        for index in (1, 3, 4):
+            state[index].wait_recv()
+
+    def place(full, source):
+        rows = source.shape[0]
+
+        def body(step, carry):
+            at = rows_at(step * 32, 32)
+            full[rows_at(opt * rows + step * 32, 32), :] = low(source[at, :])
+            return carry
+
+        lax.fori_loop(0, rows // 32, body, 0)
+        return begin(full, rows)
+
+    key_rows = r.f_key.shape[0]
+    loads[0].wait()
+    loads[1].wait()
+
+    def place_pair(step, carry):
+        at = rows_at(opt * key_rows + step * 32, 32)
+        source = rows_at(step * 32, 32)
+        r.pair_full[at, :width] = low(r.f_key[source, :])
+        r.pair_full[at, width:] = low(r.f_value[source, :])
+        return carry
+
+    lax.fori_loop(0, key_rows // 32, place_pair, 0)
+    pair_state = begin(r.pair_full, key_rows)
+
+    def norm(values):
+        shifted = values - jnp.mean(values, axis=-1, keepdims=True)
+        inverse = lax.rsqrt(jnp.mean(shifted * shifted, axis=-1, keepdims=True) + 1e-05)
+        return shifted * inverse, inverse
+
+    def norm_in(step, carry):
+        at = rows_at(step * 64, 64)
+        hat, inverse = norm(wide(r.tokens[at, :]))
+        r.in_hat[at, :] = hat
+        r.in_inv[at, :] = inverse
+        r.in_low[at, :] = low(hat * r.in_vectors[0:1, :] + r.in_vectors[1:2, :])
+        return carry
+
+    lax.fori_loop(0, r.in_low.shape[0] // 64, norm_in, 0)
+    loads[2].wait()
+    query_state = place(r.query_full, r.f_query)
+
+    def norm_lat(step, carry):
+        at = rows_at(step * 32, 32)
+        hat, _ = norm(r.latents[at, :])
+        r.lat_low[at, :] = low(hat * r.lat_vectors[0:1, :] + r.lat_vectors[1:2, :])
+        return carry
+
+    lax.fori_loop(0, lat_count // 32, norm_lat, 0)
+    query_rows, out_rows, up_rows = (
+        r.f_query.shape[0],
+        r.f_out.shape[0],
+        r.f_up.shape[0],
+    )
+    relay(r.pair_full, key_rows, pair_state)
+    relay_more(r.pair_full, key_rows, pair_state)
+    loads[3].wait()
+    out_state = place(r.out_full, r.f_out)
+    complete(pair_state)
+
+    def project(step, carry):
+        at = rows_at(step * 128, 128)
+        r.pairs[at, :] = low(dot_nn(r.in_low[at, :], r.pair_full[...]))
+        return carry
+
+    lax.fori_loop(0, r.in_low.shape[0] // 128, project, 0)
+    relay(r.query_full, query_rows, query_state)
+    relay_more(r.query_full, query_rows, query_state)
+    loads[4].wait()
+    up_state = place(r.up_full, r.f_up)
+    complete(query_state)
+
+    def project_query(step, carry):
+        at = rows_at(step * 128, 128)
+        r.queries[at, :] = low(dot_nn(r.lat_low[at, :], r.query_full[...]))
+        return carry
+
+    lax.fori_loop(0, lat_count // 128, project_query, 0)
+
+    to_owner = []
+    for m in range(micro):
+        at = slice(m * span, (m + 1) * span)
+        usable = r.usable[m] > 0.5
+        for h in range(HEADS):
+            ch = slice(h * HEAD_DIM, (h + 1) * HEAD_DIM)
+            ch_v = slice(width + h * HEAD_DIM, width + (h + 1) * HEAD_DIM)
+            masked = jnp.where(
+                usable, dot_nt(r.queries[:, ch], r.pairs[at, ch]) * scale, -1e30
+            )
+            top = jnp.max(masked, axis=1, keepdims=True)
+            weights = jnp.exp(masked - top)
+            sums = jnp.sum(weights, axis=1, keepdims=True)
+            r.weights[m * HEADS + h] = weights
+            lane = m * HEADS + h
+            r.top[:, lane : lane + 1] = top
+            r.lse[:, lane : lane + 1] = top + jnp.log(sums)
+            r.part[m, :, ch] = low(dot_nn(low(weights), r.pairs[at, ch_v]) / sums)
+        for target in ring:
+            rows = rows_at(target[0] * own, own)
+            to_owner.append(
+                courier.send(r.part.at[m, rows], r.part_in.at[seq, m], target)
+            )
+        if m == 0:
+            relay(r.out_full, out_rows, out_state)
+            relay_more(r.out_full, out_rows, out_state)
+            loads[5].wait()
+            down_state = place(r.down_full, r.f_down)
+    for target in ring:
+        rows = rows_at(target[0] * own, own)
+        to_owner.append(courier.send(r.lse.at[rows], r.lse_in.at[seq], target))
+    mine = rows_at(seq * own, own)
+    r.part_in[seq] = r.part[:, mine, :]
+    r.lse_in[seq] = r.lse[mine, :]
+    relay(r.up_full, up_rows, up_state)
+    relay_more(r.up_full, up_rows, up_state)
+    relay(r.down_full, up_rows, down_state)
+    relay_more(r.down_full, up_rows, down_state)
+    for copy in to_owner:
+        copy.wait_recv()
+
+    peak = r.lse_in[0]
+    for peer in range(1, 8):
+        peak = jnp.maximum(peak, r.lse_in[peer])
+    total = jnp.exp(r.lse_in[0] - peak)
+    for peer in range(1, 8):
+        total = total + jnp.exp(r.lse_in[peer] - peak)
+    lse_all = peak + jnp.log(total)
+    spread_heads = [head_lanes(m * HEADS, (128, width)) for m in range(micro)]
+    collect_heads = [head_lanes((micro + m) * HEADS, (128, width)) for m in range(micro)]
+    for m in range(micro):
+        rows = slice(m * own, (m + 1) * own)
+        for peer in range(8):
+            share = jnp.dot(
+                jnp.exp(r.lse_in[peer] - lse_all),
+                spread_heads[m],
+                precision=highest,
+                preferred_element_type=jnp.float32,
+            ) * wide(r.part_in[peer, m])
+            r.attended[rows, :] = share if peer == 0 else r.attended[rows, :] + share
+    local_rows = rows_at(core * (micro * own), micro * own)
+    att_low = low(r.attended[...])
+    r.x_att[local_rows, :] = att_low
+    back_rows = r.cotangent[...]
+    r.x_cot[local_rows, :] = back_rows
+    complete(out_state)
+    own_latents = jnp.concatenate([r.latents[mine, :]] * micro, axis=0)
+    r.hidden[...] = own_latents + dot_nn(att_low, r.out_full[...])
+    mlp_hat, mlp_inv = norm(r.hidden[...])
+    r.mlp_hat[...] = mlp_hat
+    mlp_low = low(mlp_hat * r.lat_vectors[2:3, :] + r.lat_vectors[3:4, :])
+    r.x_mlp[local_rows, :] = mlp_low
+    complete(up_state)
+    pre_act = dot_nn(mlp_low, r.up_full[...]) + r.lat_vectors[4:5, :]
+    cdf = 0.5 * (1.0 + lax.erf(pre_act * 0.7071067811865476))
+    act_low = low(pre_act * cdf)
+    r.slope[...] = cdf + pre_act * jnp.exp(-0.5 * pre_act * pre_act) * 0.3989422804014327
+    r.x_act[local_rows, :] = act_low
+    complete(down_state)
+    grad_pre = low(dot_nt(back_rows, r.down_full[...]) * r.slope[...])
+    r.x_pre[local_rows, :] = grad_pre
+    grad_mlp = dot_nt(grad_pre, r.up_full[...])
+    mlp_hat = r.mlp_hat[...]
+    r.vectors[...] = jnp.zeros_like(r.vectors)
+    r.vectors[0:1, :] = jnp.sum(grad_mlp * mlp_hat, axis=0, keepdims=True)
+    r.vectors[1:2, :] = jnp.sum(grad_mlp, axis=0, keepdims=True)
+    r.vectors[2:3, :] = jnp.sum(wide(grad_pre), axis=0, keepdims=True)
+    r.vectors[3:4, :] = jnp.sum(wide(back_rows), axis=0, keepdims=True)
+    scaled = grad_mlp * r.lat_vectors[2:3, :]
+    grad_hidden = wide(back_rows) + mlp_inv * (
+        scaled
+        - jnp.mean(scaled, axis=-1, keepdims=True)
+        - mlp_hat * jnp.mean(scaled * mlp_hat, axis=-1, keepdims=True)
+    )
+    rest = grad_hidden[:own]
+    for m in range(1, micro):
+        rest = rest + grad_hidden[m * own : (m + 1) * own]
+    r.rest[...] = low(rest)
+    grad_branch = low(grad_hidden)
+    r.x_branch[local_rows, :] = grad_branch
+    grad_own = low(dot_nt(grad_branch, r.out_full[...]))
+    products = wide(grad_own) * r.attended[...]
+    back = jnp.where(
+        lax.broadcasted_iota(jnp.int32, lse_all.shape, 1) < micro * HEADS, lse_all, 0.0
+    )
+    for m in range(micro):
+        rows = slice(m * own, (m + 1) * own)
+        r.grad_att[m, mine, :] = grad_own[rows]
+        back = back + lax.dot_general(
+            products[rows],
+            collect_heads[m],
+            (((1,), (1,)), ((), ())),
+            precision=highest,
+            preferred_element_type=jnp.float32,
+        )
+    r.back[mine, :] = back
+    returns = []
+    for target in ring:
+        for view in (r.grad_att.at[:, mine], r.back.at[mine]):
+            returns.append(courier.send(view, view, target))
+    chip = []
+    for array in (r.x_act, r.x_cot, r.x_mlp, r.x_pre, r.x_att, r.x_branch):
+        view = array.at[local_rows]
+        chip.append(courier.send(view, view, targets[CORE]))
+    r.block_out[...] = low(
+        r.hidden[...] + dot_nn(act_low, r.down_full[...]) + r.lat_vectors[5:6, :]
+    )
+    for copy in chip:
+        copy.wait_recv()
+    half = lanes_at(core * (width_lat // 2), width_lat // 2)
+    for target, left, right in (
+        (r.grad_down, r.x_act, r.x_cot),
+        (r.grad_up, r.x_mlp, r.x_pre),
+        (r.grad_out, r.x_att, r.x_branch),
+    ):
+        for tile in range(left.shape[1] // TILE):
+            cols = slice(tile * TILE, (tile + 1) * TILE)
+            target[cols, :] = low(dot_tn(left[:, cols], right[:, half]))
+    for copy in returns:
+        copy.wait_recv()
+
+    for h in range(HEADS):
+        ch = slice(h * HEAD_DIM, (h + 1) * HEAD_DIM)
+        ch_v = slice(width + h * HEAD_DIM, width + (h + 1) * HEAD_DIM)
+        grad_query = None
+        for m in range(micro):
+            at = slice(m * span, (m + 1) * span)
+            lane = m * HEADS + h
+            lane_in = (micro + m) * HEADS + h
+            prob = r.weights[lane] * jnp.exp(
+                r.top[:, lane : lane + 1] - r.back[:, lane : lane + 1]
+            )
+            grad_att = r.grad_att[m, :, ch]
+            grad_prob = dot_nt(grad_att, r.pairs[at, ch_v])
+            grad_scores = low(prob * (grad_prob - r.back[:, lane_in : lane_in + 1]))
+            part = dot_nn(grad_scores, r.pairs[at, ch])
+            grad_query = part if grad_query is None else grad_query + part
+            r.grad_pairs[at, ch] = low(scale * dot_tn(grad_scores, r.queries[:, ch]))
+            r.grad_pairs[at, ch_v] = low(dot_tn(low(prob), grad_att))
+        r.grad_query[:, ch] = low(scale * grad_query)
+
+    part_width = width // 2
+
+    def pair_product(target, which):
+        for kind in range(2):
+            cols = lanes_at(kind * width + which * part_width, part_width)
+            right = r.grad_pairs[:, cols]
+            for tile in range(width // TILE):
+                rows = slice(tile * TILE, (tile + 1) * TILE)
+                target[rows, kind * part_width : (kind + 1) * part_width] = low(
+                    dot_tn(r.in_low[:, rows], right)
+                )
+
+    pair_product(r.pair_other, 1 - core)
+    pair_copy = courier.send(r.pair_other, r.pair_in, targets[CORE])
+    pair_product(r.grad_pair, core)
+    r.in_sums[...] = jnp.zeros_like(r.in_sums)
+
+    def norm_in_back(step, carry):
+        at = rows_at(step * 64, 64)
+        grad_in = dot_nt(r.grad_pairs[at, :], r.pair_full[...])
+        hat = r.in_hat[at, :]
+        r.in_sums[0:1, :] = r.in_sums[0:1, :] + jnp.sum(grad_in * hat, axis=0, keepdims=True)
+        r.in_sums[1:2, :] = r.in_sums[1:2, :] + jnp.sum(grad_in, axis=0, keepdims=True)
+        scaled = grad_in * r.in_vectors[0:1, :]
+        r.input_grad[at, :] = r.in_inv[at, :] * (
+            scaled
+            - jnp.mean(scaled, axis=-1, keepdims=True)
+            - hat * jnp.mean(scaled * hat, axis=-1, keepdims=True)
+        )
+        return carry
+
+    lax.fori_loop(0, r.in_low.shape[0] // 64, norm_in_back, 0)
+    r.vectors[4:6, :width] = r.in_sums[0:2, :]
+    pair_copy.wait_recv()
+    add_into(r.grad_pair, r.pair_in)
+    courier.finish()
+
+
+def run_pass(tokens, usable, cotangent, latents, lat_vectors, in_vectors, weights):
+    f32, bf16 = jnp.float32, jnp.bfloat16
+    w_query, w_key, w_value, w_out, w_up, w_down = weights
+    operands = dict(
+        tokens=tokens,
+        usable=usable,
+        cotangent=cotangent,
+        latents=latents,
+        lat_vectors=lat_vectors,
+        in_vectors=in_vectors,
+        w_query=w_query,
+        w_key=w_key,
+        w_value=w_value,
+        w_out=w_out,
+        w_up=w_up,
+        w_down=w_down,
+    )
+    count, width = tokens.shape
+    micro, _, span = usable.shape
+    lat_count, width_lat = latents.shape
+    own = lat_count // 8
+    rows = micro * own
+    outputs = dict(
+        block_out=((rows, width_lat), bf16),
+        input_grad=((count, width), f32),
+        grad_up=((width_lat, width_lat // 2), bf16),
+        grad_down=((width_lat, width_lat // 2), bf16),
+        grad_out=((width, width_lat // 2), bf16),
+        grad_pair=((width, width), bf16),
+        grad_query=((lat_count, width), bf16),
+        vectors=((8, width_lat), f32),
+        rest=((own, width_lat), bf16),
+        lat_low=((lat_count, width_lat), bf16),
+        query_full=((width_lat, width), bf16),
+    )
+    scratch = dict(
+        f_query=(w_query.shape, f32),
+        f_key=(w_key.shape, f32),
+        f_value=(w_value.shape, f32),
+        f_out=(w_out.shape, f32),
+        f_up=(w_up.shape, f32),
+        f_down=(w_down.shape, f32),
+        pair_full=((width, 2 * width), bf16),
+        out_full=((width, width_lat), bf16),
+        up_full=((width_lat, width_lat), bf16),
+        down_full=((width_lat, width_lat), bf16),
+        in_low=((count, width), bf16),
+        in_hat=((count, width), f32),
+        in_inv=((count, 1), f32),
+        in_sums=((8, width), f32),
+        pairs=((count, 2 * width), bf16),
+        queries=((lat_count, width), bf16),
+        weights=((micro * HEADS, lat_count, span), f32),
+        top=((lat_count, 128), f32),
+        lse=((lat_count, 128), f32),
+        part=((micro, lat_count, width), bf16),
+        part_in=((8, micro, own, width), bf16),
+        lse_in=((8, own, 128), f32),
+        attended=((rows, width), f32),
+        hidden=((rows, width_lat), f32),
+        mlp_hat=((rows, width_lat), f32),
+        slope=((rows, width_lat), f32),
+        x_att=((2 * rows, width), bf16),
+        x_branch=((2 * rows, width_lat), bf16),
+        x_mlp=((2 * rows, width_lat), bf16),
+        x_pre=((2 * rows, width_lat), bf16),
+        x_act=((2 * rows, width_lat), bf16),
+        x_cot=((2 * rows, width_lat), bf16),
+        grad_att=((micro, lat_count, width), bf16),
+        back=((lat_count, 128), f32),
+        grad_pairs=((count, 2 * width), bf16),
+        pair_other=((width, width), bf16),
+        pair_in=((width, width), bf16),
+    )
+    copies = 5 * 5 + 7 * micro + 7 + 14 + 6 + 1
+    sems = dict(
+        send=pltpu.SemaphoreType.DMA((copies,)),
+        recv=pltpu.SemaphoreType.DMA((copies,)),
+        local=pltpu.SemaphoreType.DMA((6,)),
+    )
+    keys = (*operands, *outputs, *scratch, *sems)
+    vmem, anywhere = pl.BlockSpec(memory_space=pltpu.VMEM), pl.BlockSpec(memory_space=pl.ANY)
+    results = pl.pallas_call(
+        functools.partial(pass_body, keys),
+        out_shape=[jax.ShapeDtypeStruct(*spec) for spec in outputs.values()],
+        in_specs=[vmem] * 6 + [anywhere] * 6,
+        out_specs=[vmem] * len(outputs),
+        scratch_shapes=[*(pltpu.VMEM(*spec) for spec in scratch.values()), *sems.values()],
+        compiler_params=pltpu.CompilerParams(
+            collective_id=2, has_side_effects=True, vmem_limit_bytes=VMEM_LIMIT
+        ),
+        name="pass",
+    )(*operands.values())
+    return named(outputs, results)
+
+
+def cut(ref, kind, bit):
+    if kind == LEAD:
+        return ref.at[bit]
+    rows, cols = ref.shape[-2:]
+    lead = (slice(None),) * (len(ref.shape) - 2)
+    if kind == ROWS:
+        return ref.at[(*lead, rows_at(bit * (rows // 2), rows // 2), slice(None))]
+    return ref.at[(*lead, slice(None), lanes_at(bit * (cols // 2), cols // 2))]
+
+
+def half_shape(shape, kind):
+    if kind == LEAD:
+        return shape[1:]
+    if kind == ROWS:
+        return (*shape[:-2], shape[-2] // 2, shape[-1])
+    return (*shape[:-1], shape[-1] // 2)
+
+
+def add_into(total, term):
+    def body(step, carry):
+        at = rows_at(step * 16, 16)
+        for lead in range(total.shape[0]) if len(total.shape) == 3 else (None,):
+            where = (at, slice(None)) if lead is None else (lead, at, slice(None))
+            total[where] = low(wide(total[where]) + wide(term[where]))
+        return carry
+
+    lax.fori_loop(0, total.shape[-2] // 16, body, 0)
+
+
+ROUTES = (
+    ((X, LEAD), (Y, ROWS), (Z0, ROWS), (Z1, ROWS)),
+    ((Y, ROWS), (X, LEAD), (Z0, ROWS), (Z1, ROWS)),
+    ((Z0, ROWS), (X, LEAD), (Y, ROWS), (Z1, ROWS)),
+    ((Z0, ROWS), (Y, ROWS), (X, LEAD), (Z1, ROWS)),
+    ((CORE, COLS), (X, ROWS), (Y, ROWS), (Z0, ROWS), (Z1, ROWS)),
+)
+UP, DOWN, PAIR, OUT, QUERY = range(5)
+SLOTS = (3, 0, 7, 4, 2, 5)
+
+
+def combine_body(keys, shapes, *refs):
+    r = named(keys, refs)
+    seq, opt = lax.axis_index("seq"), lax.axis_index("opt")
+    bits, targets = partners(seq, opt)
+    core, z0, z1, y = bits[CORE], bits[Z0], bits[Z1], bits[Y]
+    load = Loader(r.local)
+    moments = (r.mom_query, r.mom_key, r.mom_value, r.mom_out, r.mom_up, r.mom_down)
+    held = (r.h_query, r.h_key, r.h_value, r.h_out, r.h_up, r.h_down)
+    loads = [load.start(source, target) for source, target in zip(moments, held)]
+    greet(targets)
+    courier = Courier(r.send, r.recv)
+    sums = [r.up, r.down, r.pair, r.out, r.query]
+    first = 0
+    stages = []
+    for shape_list in shapes:
+        stages.append([getattr(r, f"s{first + index}") for index in range(len(shape_list))])
+        first += len(shape_list)
+    pending = {}
+
+    def give(which, stage):
+        axis, kind = ROUTES[which][stage]
+        pending[which] = courier.send(
+            cut(sums[which], kind, 1 - bits[axis]), stages[which][stage], targets[axis]
+        )
+
+    def take(which, stage):
+        axis, kind = ROUTES[which][stage]
+        pending[which].wait_recv()
+        add_into(stages[which][stage], cut(sums[which], kind, bits[axis]))
+        sums[which] = stages[which][stage]
+
+    give(QUERY, 0)
+    for which in (PAIR, OUT, UP, DOWN):
+        give(which, 0)
+    r.vectors_sum[...] = r.vectors[...]
+    vector_copy = courier.send(r.vectors, r.vectors_in.at[0], targets[CORE])
+    rest_width = r.rest.shape[1] // 2
+    column = lanes_at(core * rest_width, rest_width)
+    rest_copy = courier.send(
+        r.rest.at[:, lanes_at((1 - core) * rest_width, rest_width)], r.rest_in.at[0], targets[CORE]
+    )
+    take(QUERY, 0)
+    give(QUERY, 1)
+    vector_copy.wait_recv()
+    r.vectors_sum[...] = r.vectors_sum[...] + r.vectors_in[0]
+    rest_copy.wait_recv()
+    r.rest_sum[...] = low(wide(r.rest[:, column]) + wide(r.rest_in[0]))
+    rest_copy = courier.send(r.rest_sum, r.rest_in.at[1], targets[X])
+    for stage in range(4):
+        axis = (X, Y, Z0, Z1)[stage]
+        r.vectors_out[stage] = r.vectors_sum[...]
+        vector_copy = courier.send(
+            r.vectors_out.at[stage], r.vectors_in.at[stage + 1], targets[axis]
+        )
+        if stage > 0:
+            rest_copy.wait_recv()
+            if stage == 1:
+                r.rest_all[z1, z0, y, :, column] = low(wide(r.rest_sum[...]) + wide(r.rest_in[1]))
+            every = slice(None)
+            lead = ((z1, z0, y), (every, z0, y), (every, every, y))[stage - 1]
+            view = r.rest_all.at[(*lead, every, column)]
+            rest_copy = courier.send(view, view, targets[(Z1, Z0, Y)[stage - 1]])
+        for which in (QUERY, PAIR, OUT, UP, DOWN):
+            own_stage = stage + 1 if which == QUERY else stage
+            take(which, own_stage)
+            if stage < 3:
+                give(which, own_stage + 1)
+        vector_copy.wait_recv()
+        r.vectors_sum[...] = r.vectors_sum[...] + r.vectors_in[stage + 1]
+    rest_copy.wait_recv()
+    view = r.rest_all.at[:, :, :, :, column]
+    rest_copy = courier.send(view, view, targets[CORE])
+
+    rows, width = sums[QUERY].shape
+    query_column = lanes_at(core * width, width)
+    start = (bits[X] * 8 + y * 4 + z0 * 2 + z1) * rows
+    r.query_all[rows_at(start, rows), query_column] = sums[QUERY][...]
+    query_steps = (
+        (Z1, 1, start),
+        (Z0, 2, start - z1 * rows),
+        (Y, 4, start - (z1 + z0 * 2) * rows),
+        (X, 8, bits[X] * (8 * rows)),
+    )
+    gathered = (r.g_up, r.g_down, r.g_pair, r.g_out)
+    for which in range(4):
+        high, mid = (y, z0) if which in (UP, DOWN) else (z0, y)
+        rows = sums[which].shape[0]
+        gathered[which][rows_at((high * 4 + mid * 2 + z1) * rows, rows), :] = sums[which][...]
+
+    def query_step(step):
+        axis, count, base = query_steps[step]
+        view = r.query_all.at[rows_at(base, count * sums[QUERY].shape[0]), query_column]
+        return courier.send(view, view, targets[axis])
+
+    query_copy = None
+    for step in range(3):
+        if step > 0:
+            query_copy.wait_recv()
+        query_copy = query_step(step)
+        for which in (UP, DOWN, PAIR, OUT):
+            first_axis, last_axis = (Y, Z0) if which in (UP, DOWN) else (Z0, Y)
+            high, mid = bits[first_axis], bits[last_axis]
+            rows = sums[which].shape[0]
+            if step > 0:
+                pending[which].wait_recv()
+            base, count = ((high * 4 + mid * 2 + z1, 1), (high * 4 + mid * 2, 2), (high * 4, 4))[
+                step
+            ]
+            view = gathered[which].at[rows_at(base * rows, count * rows)]
+            pending[which] = courier.send(
+                view, view, targets[(Z1, last_axis, first_axis)[step]]
+            )
+    full = (r.n_up, r.n_down, r.n_pair, r.n_out)
+    for which in (OUT, PAIR, DOWN, UP):
+        pending[which].wait_recv()
+        rows, cols = gathered[which].shape
+        at = lanes_at(core * cols, cols)
+        pending[which] = courier.send(
+            gathered[which].at[rows_at((1 - core) * (rows // 2), rows // 2)],
+            full[which].at[:, at],
+            targets[CORE],
+        )
+        full[which][:, at] = gathered[which][rows_at(core * (rows // 2), rows // 2), :]
+    query_copy.wait_recv()
+    query_copy = query_step(3)
+    query_copy.wait_recv()
+    view = r.query_all.at[:, query_column]
+    query_copy = courier.send(view, view, targets[CORE])
+    height, side = r.whole.shape[1:]
+    clear_rows = 32
+
+    def clear(step, carry):
+        r.whole[opt, rows_at(step * clear_rows, clear_rows), :] = jnp.zeros(
+            (clear_rows, side), jnp.bfloat16
+        )
+        return carry
+
+    lax.fori_loop(0, height // clear_rows, clear, 0)
+    for copy in loads:
+        copy.wait()
+    for which in range(4):
+        pending[which].wait_recv()
+    query_copy.wait_recv()
+    part = r.g_pair.shape[1] // 2
+    r.new_query[...] = 0.95 * r.h_query[...] + dot_tn(r.lat_block[...], r.query_all[...])
+    for kind, (target, moment) in enumerate(((r.new_key, r.h_key), (r.new_value, r.h_value))):
+        for side_core in range(2):
+            cols = slice(side_core * part, (side_core + 1) * part)
+            source = side_core * (2 * part) + kind * part
+            target[:, cols] = 0.95 * moment[:, cols] + wide(r.n_pair[:, source : source + part])
+    for target, moment, source in (
+        (r.new_out, r.h_out, r.n_out),
+        (r.new_up, r.h_up, r.n_up),
+        (r.new_down, r.h_down, r.n_down),
+    ):
+        target[...] = 0.95 * moment[...] + wide(source[...])
+
+    news = (r.new_query, r.new_key, r.new_value, r.new_out, r.new_up, r.new_down)
+    for new, slot in zip(news, SLOTS):
+
+        @pl.when(seq == slot)
+        def _(new=new):
+            r.whole[opt, : new.shape[0], : new.shape[1]] = low(new[...])
+
+    own = r.whole.at[opt]
+    across = courier.send(own, own, targets[X])
+    beside = courier.send(own, own, targets[CORE])
+    across.wait_recv()
+    other = r.whole.at[targets[X][1]]
+    last = courier.send(other, other, targets[CORE])
+    beside.wait_recv()
+    last.wait_recv()
+    rest_copy.wait_recv()
+    courier.finish()
+
+
+def combine(done, lat_block, moments, height):
+    f32, bf16 = jnp.float32, jnp.bfloat16
+    mom_query, mom_key, mom_value, mom_out, mom_up, mom_down = moments
+    width_lat = done.grad_up.shape[0]
+    halved = [
+        grad.reshape(2, grad.shape[0] // 2, grad.shape[1])
+        for grad in (done.grad_up, done.grad_down, done.grad_pair, done.grad_out)
+    ]
+    operands = dict(
+        vectors=done.vectors,
+        rest=done.rest,
+        lat_block=lat_block,
+        up=halved[0],
+        down=halved[1],
+        pair=halved[2],
+        out=halved[3],
+        query=done.grad_query,
+        mom_query=mom_query,
+        mom_key=mom_key,
+        mom_value=mom_value,
+        mom_out=mom_out,
+        mom_up=mom_up,
+        mom_down=mom_down,
+    )
+    outputs = dict(
+        new_query=(mom_query.shape, f32),
+        new_key=(mom_key.shape, f32),
+        new_value=(mom_value.shape, f32),
+        new_out=(mom_out.shape, f32),
+        new_up=(mom_up.shape, f32),
+        new_down=(mom_down.shape, f32),
+        query_all=(done.grad_query.shape, bf16),
+        vectors_sum=(done.vectors.shape, f32),
+        rest_all=((2, 2, 2, *done.rest.shape), bf16),
+        whole=((4, height, width_lat), bf16),
+    )
+    half_rest = (done.rest.shape[0], done.rest.shape[1] // 2)
+    scratch = dict(
+        vectors_in=((5, *done.vectors.shape), f32),
+        vectors_out=((4, *done.vectors.shape), f32),
+        rest_in=((2, *half_rest), bf16),
+        rest_sum=(half_rest, bf16),
+        h_query=(mom_query.shape, f32),
+        h_key=(mom_key.shape, f32),
+        h_value=(mom_value.shape, f32),
+        h_out=(mom_out.shape, f32),
+        h_up=(mom_up.shape, f32),
+        h_down=(mom_down.shape, f32),
+        g_up=(halved[0].shape[1:], bf16),
+        g_down=(halved[1].shape[1:], bf16),
+        g_pair=(halved[2].shape[1:], bf16),
+        g_out=(halved[3].shape[1:], bf16),
+        n_up=(mom_up.shape, bf16),
+        n_down=(mom_down.shape, bf16),
+        n_pair=((mom_key.shape[0], 2 * mom_key.shape[1]), bf16),
+        n_out=(mom_out.shape, bf16),
+    )
+    shapes = []
+    for array, route in zip((*halved, done.grad_query), ROUTES):
+        shape, chain = array.shape, []
+        for _, kind in route:
+            shape = half_shape(shape, kind)
+            chain.append(shape)
+        shapes.append(chain)
+    for index, shape in enumerate(sum(shapes, [])):
+        scratch[f"s{index}"] = (shape, bf16)
+    copies = 64
+    sems = dict(
+        send=pltpu.SemaphoreType.DMA((copies,)),
+        recv=pltpu.SemaphoreType.DMA((copies,)),
+        local=pltpu.SemaphoreType.DMA((6,)),
+    )
+    keys = (*operands, *outputs, *scratch, *sems)
+    vmem, anywhere = pl.BlockSpec(memory_space=pltpu.VMEM), pl.BlockSpec(memory_space=pl.ANY)
+    results = pl.pallas_call(
+        functools.partial(combine_body, keys, shapes),
+        out_shape=[jax.ShapeDtypeStruct(*spec) for spec in outputs.values()],
+        in_specs=[vmem] * 8 + [anywhere] * 6,
+        out_specs=[vmem] * len(outputs),
+        scratch_shapes=[*(pltpu.VMEM(*spec) for spec in scratch.values()), *sems.values()],
+        compiler_params=pltpu.CompilerParams(
+            collective_id=0, has_side_effects=True, vmem_limit_bytes=VMEM_LIMIT
+        ),
+        name="combine",
+    )(*operands.values())
+    return named(outputs, results)
+
+
+def spread_body(result_ref, *refs):
+    count = len(SLOTS)
+    outs = refs[:count]
+    send_sem, recv_sem, local_sem = refs[count:]
+    seq, opt = lax.axis_index("seq"), lax.axis_index("opt")
+    y, z = seq % 2, seq // 2
+    targets = partners(seq, opt)[1]
+    depth = 4
+    barrier = pltpu.get_barrier_semaphore()
+    pl.semaphore_signal(barrier, inc=1, device_id=targets[Y], device_id_type=MESH)
+    for step in (-1, 1):
+
+        @pl.when((z + step >= 0) & (z + step < depth))
+        def _(step=step):
+            pl.semaphore_signal(
+                barrier, inc=1, device_id=(seq + 2 * step, opt), device_id_type=MESH
+            )
+
+    inside = (z > 0) & (z < depth - 1)
+
+    @pl.when(inside)
+    def _():
+        pl.semaphore_wait(barrier, 3)
+
+    @pl.when(jnp.logical_not(inside))
+    def _():
+        pl.semaphore_wait(barrier, 2)
+
+    def copy(which, part, way):
+        index = which * PARTS + part
+        out = outs[which]
+        rows = out.shape[0] // PARTS
+        view = out.at[pl.ds(part * rows, rows)]
+        return pltpu.make_async_remote_copy(
+            src_ref=view,
+            dst_ref=view,
+            send_sem=send_sem.at[way, index],
+            recv_sem=recv_sem.at[index],
+            device_id=((seq + 2, opt), (seq - 2, opt), targets[Y])[way],
+            device_id_type=MESH,
+        )
+
+    for which, slot in enumerate(SLOTS):
+        out = outs[which]
+
+        @pl.when(seq == slot)
+        def _(out=out):
+            load = pltpu.make_async_copy(
+                result_ref.at[opt, pl.ds(0, out.shape[0]), pl.ds(0, out.shape[1])], out, local_sem
+            )
+            load.start()
+            load.wait()
+
+    def ways(which, mine):
+        slot_y, slot_z = SLOTS[which] % 2, SLOTS[which] // 2
+        turn = (y == slot_y) & ((z == slot_z) if mine else (z != slot_z))
+        return (
+            turn & (z >= slot_z) & (z < depth - 1),
+            turn & (z <= slot_z) & (z > 0),
+            turn,
+        )
+
+    for mine in (True, False):
+        for part in range(PARTS):
+            for which in ORDER:
+                on = ways(which, mine)
+                if not mine:
+
+                    @pl.when(on[2])
+                    def _(which=which, part=part):
+                        copy(which, part, 2).wait_recv()
+
+                for way in range(3):
+
+                    @pl.when(on[way])
+                    def _(which=which, part=part, way=way):
+                        copy(which, part, way).start()
+
+    for part in range(PARTS):
+        for which in ORDER:
+
+            @pl.when(y != SLOTS[which] % 2)
+            def _(which=which, part=part):
+                copy(which, part, 2).wait_recv()
+
+    for mine in (True, False):
+        for part in range(PARTS):
+            for which in ORDER:
+                on = ways(which, mine)
+                for way in range(3):
+
+                    @pl.when(on[way])
+                    def _(which=which, part=part, way=way):
+                        copy(which, part, way).wait_send()
+
+
+def spread(result, shapes):
+    vmem = pl.BlockSpec(memory_space=pltpu.VMEM)
+    count = len(SLOTS) * PARTS
+    return pl.pallas_call(
+        spread_body,
+        out_shape=[jax.ShapeDtypeStruct(shape, jnp.bfloat16) for shape in shapes],
+        in_specs=[pl.BlockSpec(memory_space=pl.ANY)],
+        out_specs=[vmem] * len(SLOTS),
+        scratch_shapes=[
+            pltpu.SemaphoreType.DMA((3, count)),
+            pltpu.SemaphoreType.DMA((count,)),
+            pltpu.SemaphoreType.DMA,
+        ],
+        compiler_params=pltpu.CompilerParams(
+            collective_id=1, has_side_effects=True, vmem_limit_bytes=VMEM_LIMIT
+        ),
+        name="spread",
+    )(result)
+
+
 def adam_update(param, gradient, first, second, step_rate, decay):
     first_new = 0.9 * first + 0.1 * gradient
     second_new = 0.95 * second + 0.05 * gradient * gradient
     ratio = first_new / (1.0 - 0.9**STEP) / (jnp.sqrt(second_new / (1.0 - 0.95**STEP)) + 1e-08)
     return (first_new, second_new, param - step_rate * (ratio + decay * param))
+
+
+def local_small(
+    inputs,
+    key_mask,
+    lengths,
+    cotangent,
+    latents,
+    lat_vectors,
+    in_vectors,
+    w_query,
+    w_key,
+    w_value,
+    w_out,
+    w_up,
+    w_down,
+    mom_query,
+    mom_key,
+    mom_value,
+    mom_out,
+    mom_up,
+    mom_down,
+    lat_first,
+    lat_second,
+    in_first,
+    in_second,
+    latent_first,
+    latent_second,
+):
+    seq_index, opt_index = lax.axis_index("seq"), lax.axis_index("opt")
+    micro_count, _, span, width_in = inputs.shape
+    lat_count, width_lat = latents.shape
+    positions = seq_index * span + jnp.arange(span, dtype=jnp.int32)
+    usable = (positions < lengths[:, :, None]) & ((key_mask == 1) | (positions == 0))
+    masters = (w_query, w_key, w_value, w_out, w_up, w_down)
+    moments = (mom_query, mom_key, mom_value, mom_out, mom_up, mom_down)
+    done = run_pass(
+        inputs.reshape(-1, width_in),
+        usable.astype(jnp.float32),
+        cotangent.reshape(-1, width_lat),
+        latents,
+        lat_vectors,
+        in_vectors,
+        masters,
+    )
+    height = w_up.shape[0]
+    summed = combine(
+        done,
+        lax.dynamic_slice_in_dim(done.lat_low, opt_index * height, height, 1),
+        moments,
+        height,
+    )
+    moments_new = (
+        summed.new_query,
+        summed.new_key,
+        summed.new_value,
+        summed.new_out,
+        summed.new_up,
+        summed.new_down,
+    )
+    own_result = newton(summed.whole.reshape(-1, width_lat))
+    currents = spread(
+        own_result.reshape(summed.whole.shape), [moment.shape for moment in moments]
+    )
+    new_masters = update_masters(masters, currents)
+    _, lat_hat, lat_inv = layer_norm(latents, lat_vectors[0], lat_vectors[1])
+    grad_lat = jnp.dot(summed.query_all, done.query_full.T, preferred_element_type=jnp.float32)
+    lat_vec_sum = jnp.concatenate(
+        [
+            jnp.sum(grad_lat * lat_hat, axis=0)[None],
+            jnp.sum(grad_lat, axis=0)[None],
+            summed.vectors_sum[:4],
+        ]
+    )
+    in_vec_sum = summed.vectors_sum[4:6, :width_in]
+    latent_sum = norm_back(grad_lat, lat_hat, lat_inv, lat_vectors[0]) + summed.rest_all.reshape(
+        latents.shape
+    ).astype(jnp.float32)
+    return (
+        done.block_out.reshape(cotangent.shape),
+        done.input_grad.reshape(inputs.shape),
+        *moments_new,
+        *new_masters,
+        *adam_update(lat_vectors, lat_vec_sum, lat_first, lat_second, 0.6, 0.0),
+        *adam_update(in_vectors, in_vec_sum, in_first, in_second, 0.6, 0.0),
+        *adam_update(latents, latent_sum, latent_first, latent_second, 1.0, 0.1),
+    )
+
+
+def update_masters(masters, currents):
+    fans = (D_LAT, E_IN, E_IN, OUT_FAN, D_LAT, D_LAT)
+    sides = (D_LAT, E_IN, E_IN, D_LAT, D_LAT, D_LAT)
+    new_masters = []
+    for master, current, fan_in, long_side in zip(masters, currents, fans, sides):
+        step_rate = fan_in ** (-0.5)
+        new_masters.append(
+            (1.0 - 0.1 * step_rate) * master
+            - step_rate * long_side**0.5 * current.astype(jnp.float32)
+        )
+    return new_masters
 
 
 def local(
@@ -393,12 +1443,7 @@
         spread[index, : moment.shape[0], : moment.shape[1]].astype(jnp.float32)
         for index, moment in enumerate(moments)
     ]
-    fans = (D_LAT, E_IN, E_IN, OUT_FAN, D_LAT, D_LAT)
-    sides = (D_LAT, E_IN, E_IN, D_LAT, D_LAT, D_LAT)
-    new_masters = []
-    for master, current, fan_in, long_side in zip(masters, currents, fans, sides):
-        step_rate = fan_in ** (-0.5)
-        new_masters.append((1.0 - 0.1 * step_rate) * master - step_rate * long_side**0.5 * current)
+    new_masters = update_masters(masters, currents)
     lat_m, lat_v, lat_p = adam_update(lat_vectors, lat_vec_sum, lat_first, lat_second, 0.6, 0.0)
     in_m, in_v, in_p = adam_update(in_vectors, in_vec_sum, in_first, in_second, 0.6, 0.0)
     latent_m, latent_v, latent_p = adam_update(
@@ -434,8 +1479,9 @@
 
 
 def solution(mesh):
+    small = (mesh.shape["seq"], mesh.shape["opt"]) == (8, 4)
     return jax.shard_map(
-        local,
+        local_small if small else local,
         mesh=mesh,
         in_specs=(
             P(None, "opt", "seq", None),

time: 908 us -> 413 us (0.45)
  waiting for transfers between devices: 488 us -> 0 us
  Pallas kernels: 60.1 us -> 378 us
  blocking collectives: 164 us -> 0 us
  matrix products: 73.8 us -> 1 us
  other arithmetic: 63.4 us -> 13.6 us
  local copies, waits for them, and re-layouts: 33.3 us -> 14.1 us
  between operations: 16.6 us -> 1.15 us
    pallas_call x0 -> x3, Pallas kernels: none -> 318 us  [the longest x1 135 us: combine(): pl.pallas_call(functools.partial(combine_body, keys, shapes), out_shape=[...]
    psum x3 -> x0, waiting for transfers between devices: 281 us -> none  [the longest x1 232 us: local(): summed_low = lax.psum(tuple(with_moment), ('seq', 'opt'))]
    all_gather x7 -> x0, waiting for transfers between devices: 208 us -> none  [the longest x1 87.1 us: local(): spread = lax.all_gather(mine, 'seq', axis=0, tiled=False)]
    dot_general x39 -> x1, matrix products: 73.8 us -> 1 us  [local_small(): jnp.dot(summed.query_all, done.query_full.T, preferred_element_type=jnp.f...]
    psum x2 -> x0, blocking collectives: 64.1 us -> none  [the longest x1 46.2 us: local(): lax.psum((lat_vec_grad, in_vec_grad, latent_grad), ('seq', 'opt'))]
    all_gather x2 -> x0, blocking collectives: 62.4 us -> none  [local(): lax.all_gather(grad_own, 'seq', axis=1, tiled=True).astype(jnp.float32)]
    pmax x1 -> x0, blocking collectives: 37.2 us -> none  [local(): row_max = lax.pmax(jnp.max(masked, axis=-1), 'seq')]
    convert_element_type x18 -> x1, other arithmetic: 32.5 us -> 1.34 us  [local_small(): usable.astype(jnp.float32)]
  transfers between devices with their start and end apart: 10 -> 0, of which waited for: 10 -> 0; matrix products, arithmetic and copies ran while one was open for 10% -> 0% of each run, Pallas kernels for 7% -> 0%
where the time goes in v2:
time: 413 us; the launch traced here: 408 us
  Pallas kernels  378 us (92%)
  local copies, waits for them, and re-layouts  14.1 us (3%)
  other arithmetic  13.6 us (3%)
    pallas_call x1, Pallas kernels, combine(): pl.pallas_call(functools.partial(combine_body, keys, shapes), out_shape=[...  135 us
    pallas_call x1, Pallas kernels, run_pass(): pl.pallas_call(functools.partial(pass_body, keys), out_shape=[jax.ShapeDt...  122 us
    pallas_call x1, Pallas kernels, spread(): pl.pallas_call(spread_body, out_shape=[jax.ShapeDtypeStruct(shape, jnp.bf...  61.1 us
    pallas_call x1, Pallas kernels, newton(): pl.pallas_call(newton_body, out_shape=jax.ShapeDtypeStruct(shape, jnp.bfl...  60.4 us
    unnamed x70, local copies, waits for them, and re-layouts  12.3 us

profile of v2, /device:TPU:0, one launch (start us, length us, event | category | flops | bytes accessed | tf_op | source)
XLA Modules:
  0.0 408.2 jit_solution(3459594198497204101)
XLA Ops:
  0.7 1.3 and_convert_fusion.refs_1_
  2.0 121.7 %pass.1 = (bf16[64,1280]{1,0:T(8,128)(2,1)}, f32[512,768]{1,0:T(8,128)}, bf16[1280,640]{1,0:T(8,128)(2,1)}, bf16[1280,640]{1,0:T(8,128)(2,1)}, bf16[768,640]{1,0...) custom-call(bf16[512,768]{1,0:T(8,128)(2,1)} %bitcast.33, ...), custom_call_target="tpu_custom_call" | custom-call | tf_op jit(solution)/shard_map/pass/pallas_call | solution.py:648
  123.7 1.8 constant_dynamic-slice_fusion.refs_2_
  125.5 135.1 %combine.1 = (f32[320,768]{1,0:T(8,128)}, f32[192,768]{1,0:T(8,128)}, f32[192,768]{1,0:T(8,128)}, f32[192,1280]{1,0:T(8,128)}, f32[320,1280]{1,0:T(8,128)}, /*in...) custom-call(f32[8,1280]{1,0:T(8,128)} %get-tuple-element.52.refs_0_,, ...), custom_call_target="tpu_custom_call" | custom-call | tf_op jit(solution)/shard_map/combine/pallas_call | solution.py:952
  260.8 0.3 multiply_reduce_fusion.2
  261.1 0.3 copy-done.21
  261.4 0.8 copy-done.29
  262.2 1.0 multiply_reduce_fusion
  263.3 0.3 copy-done.10
  263.5 0.4 copy-done.11
  264.1 3.7 add_subtract_fusion
  267.9 0.7 multiply_subtract_fusion.1
  268.5 60.4 %newton.1 = bf16[1280,1280]{1,0:T(8,128)(2,1)} custom-call(bf16[1280,1280]{1,0:T(8,128)(2,1)} %bitcast.27), custom_call_target="tpu_custom_call" | custom-call | tf_op jit(solution)/shard_map/newton/pallas_call | solution.py:122
  328.9 61.1 %spread.1 = (bf16[320,768]{1,0:T(8,128)(2,1)}, bf16[192,768]{1,0:T(8,128)(2,1)}, bf16[192,768]{1,0:T(8,128)(2,1)}, bf16[192,1280]{1,0:T(8,128)(2,1)}, bf16[320,1...) custom-call(bf16[4,320,1280]{2,1,0:T(8,128)(2,1)} %bitcast.26), custom_call_target="tpu_custom_call" | custom-call | tf_op jit(solution)/shard_map/spread/pallas_call | solution.py:1065
  390.1 3.6 convert_subtract_fusion
  393.8 1.1 convert_subtract_fusion.3
  394.9 0.4 copy-done.3
  395.3 0.2 copy-done.18
  395.5 1.0 convert_subtract_fusion.2
  396.6 1.1 multiply_subtract_fusion
  397.7 0.6 multiply_subtract_fusion.2
  398.3 0.7 copy.58
  399.0 1.1 copy.59
  400.1 0.6 copy-done.13
  400.7 0.9 copy.60
  401.7 0.5 copy-done.16
  402.2 0.8 copy.61
  403.0 0.8 copy.62
  403.8 0.9 copy.63
  404.7 1.2 copy.64
  405.9 0.9 copy-done.7
  406.8 1.2 copy.65
  (63 shorter events, 0.5 us)
Async XLA Ops:
  125.5 135.1 %copy-start = (f32[256,1280]{1,0:T(8,128)S(1)}, f32[256,1280]{1,0:T(8,128)}, u32[]{:S(2)}) copy-start(f32[256,1280]{1,0:T(8,128)} %refs_3_.1) | copy-start | bytes 3932164
  260.6 0.8 copy-start.21
  260.6 1.6 copy-start.29
  260.8 1.5 copy-start.30
  262.2 1.3 copy-start.10
  262.2 1.7 copy-start.11
  262.2 1.9 copy-start.14
  264.1 3.7 copy-start.26
  264.1 3.7 copy-start.23
  264.1 3.7 copy-start.24
  328.9 61.2 %copy-start.1 = (f32[320,1280]{1,0:T(8,128)S(1)}, f32[320,1280]{1,0:T(8,128)}, u32[]{:S(2)}) copy-start(f32[320,1280]{1,0:T(8,128)} %refs_10_.2) | copy-start | bytes 4915204
  328.9 61.2 %copy-start.2 = (f32[320,1280]{1,0:T(8,128)S(1)}, f32[320,1280]{1,0:T(8,128)}, u32[]{:S(2)}) copy-start(f32[320,1280]{1,0:T(8,128)} %refs_11_.2) | copy-start | bytes 4915204
  390.1 3.6 copy-start.5
  390.1 3.6 copy-start.6
  390.1 3.6 copy-start.19
  390.1 3.6 copy-start.20
  393.7 1.5 copy-start.3
  393.7 1.7 copy-start.18
  394.9 1.6 copy-start.4
  394.9 1.7 copy-start.17
  396.5 1.1 copy-start.25
  396.5 1.1 copy-start.27
  396.5 1.1 copy-start.28
  396.5 1.8 copy-start.22
  396.6 2.4 copy-start.9
  399.0 1.8 copy-start.13
  400.7 1.4 copy-start.16
  400.7 2.2 copy-start.15
  402.2 1.6 copy-start.12
  403.0 1.8 copy-start.8
  404.7 2.0 copy-start.7

commit v3 on v2

--- a/solution.py
+++ b/solution.py
@@ -17,6 +17,8 @@
 TILE = 256
 PARTS = 4
 ORDER = (4, 5, 3, 0, 1, 2)
+AHEAD = 2
+POINTS = {0: (0, 0), 1: (4, 0), 2: (1, 0), 4: (0, 1), 5: (4, 1), 6: (1, 1)}
 VMEM_LIMIT = 60 * 2**20
 MESH = pl.DeviceIdType.MESH
 
@@ -56,9 +58,35 @@
     return jnp.where(usable[:, None, None, :], scores, -1e30)
 
 
+def polynomial(low, gram, poly):
+    side_tiles = gram.shape[0] // TILE
+    for i in range(side_tiles):
+        own = slice(i * TILE, (i + 1) * TILE)
+        for j in range(i, side_tiles):
+            other = slice(j * TILE, (j + 1) * TILE)
+            block = lax.dot_general(
+                low[:, own],
+                low[:, other],
+                (((0,), (0,)), ((), ())),
+                preferred_element_type=jnp.float32,
+            )
+            gram[own, other] = block.astype(jnp.bfloat16)
+            if j > i:
+                gram[other, own] = block.T.astype(jnp.bfloat16)
+    for i in range(side_tiles):
+        own = slice(i * TILE, (i + 1) * TILE)
+        block = coef_three * jnp.dot(
+            gram[own, :], gram[:, i * TILE :], preferred_element_type=jnp.float32
+        ) + coef_two * gram[own, i * TILE :].astype(jnp.float32)
+        poly[own, i * TILE :] = block.astype(jnp.bfloat16)
+        for j in range(i + 1, side_tiles):
+            part = block[:, (j - i) * TILE : (j - i + 1) * TILE]
+            poly[j * TILE : (j + 1) * TILE, own] = part.T.astype(jnp.bfloat16)
+
+
 def newton_body(rows_ref, out_ref, wide, low, gram, poly, total):
     count, side = rows_ref.shape
-    row_tiles, side_tiles = count // TILE, side // TILE
+    row_tiles = count // TILE
     total[0] = 0.0
 
     def add_squares(tile, carry):
@@ -78,28 +106,7 @@
     lax.fori_loop(0, row_tiles, normalise, 0)
 
     def sweep(index, carry):
-        for i in range(side_tiles):
-            own = slice(i * TILE, (i + 1) * TILE)
-            for j in range(i, side_tiles):
-                other = slice(j * TILE, (j + 1) * TILE)
-                block = lax.dot_general(
-                    low[:, own],
-                    low[:, other],
-                    (((0,), (0,)), ((), ())),
-                    preferred_element_type=jnp.float32,
-                )
-                gram[own, other] = block.astype(jnp.bfloat16)
-                if j > i:
-                    gram[other, own] = block.T.astype(jnp.bfloat16)
-        for i in range(side_tiles):
-            own = slice(i * TILE, (i + 1) * TILE)
-            block = coef_three * jnp.dot(
-                gram[own, :], gram[:, i * TILE :], preferred_element_type=jnp.float32
-            ) + coef_two * gram[own, i * TILE :].astype(jnp.float32)
-            poly[own, i * TILE :] = block.astype(jnp.bfloat16)
-            for j in range(i + 1, side_tiles):
-                part = block[:, (j - i) * TILE : (j - i + 1) * TILE]
-                poly[j * TILE : (j + 1) * TILE, own] = part.T.astype(jnp.bfloat16)
+        polynomial(low, gram, poly)
 
         def update(tile, inner):
             rows = pl.ds(tile * TILE, TILE)
@@ -138,6 +145,17 @@
 
 CORE, X, Y, Z0, Z1 = range(5)
 LEAD, ROWS, COLS = range(3)
+UP, DOWN, KEY, VALUE, OUT, QUERY = range(6)
+ROUTES = (
+    ((X, LEAD), (Y, ROWS), (Z0, ROWS), (Z1, ROWS)),
+    ((Y, ROWS), (X, LEAD), (Z0, ROWS), (Z1, ROWS)),
+    ((X, LEAD), (Y, ROWS), (Z0, ROWS), (Z1, ROWS)),
+    ((Z0, ROWS), (X, LEAD), (Y, ROWS), (Z1, ROWS)),
+    ((Z0, ROWS), (Y, ROWS), (X, LEAD), (Z1, ROWS)),
+    ((CORE, COLS), (X, ROWS), (Y, ROWS), (Z0, ROWS), (Z1, ROWS)),
+)
+Y_FIRST = (UP, DOWN, KEY)
+SLOTS = (3, 0, 7, 4, 2, 5)
 
 
 def partners(seq, opt):
@@ -199,6 +217,14 @@
     return pl.ds(pl.multiple_of(start, 128), count)
 
 
+def clear(ref):
+    def body(step, carry):
+        ref[rows_at(step * 32, 32), :] = jnp.zeros((32, ref.shape[1]), ref.dtype)
+        return carry
+
+    lax.fori_loop(0, ref.shape[0] // 32, body, 0)
+
+
 def dot_nn(left, right):
     return jnp.dot(left, right, preferred_element_type=jnp.float32)
 
@@ -225,6 +251,69 @@
 
 def wide(values):
     return values.astype(jnp.float32)
+
+
+def norm(values):
+    shifted = values - jnp.mean(values, axis=-1, keepdims=True)
+    inverse = lax.rsqrt(jnp.mean(shifted * shifted, axis=-1, keepdims=True) + 1e-05)
+    return shifted * inverse, inverse
+
+
+def cut(ref, kind, bit):
+    if kind == LEAD:
+        return ref.at[bit]
+    rows, cols = ref.shape[-2:]
+    lead = (slice(None),) * (len(ref.shape) - 2)
+    if kind == ROWS:
+        return ref.at[(*lead, rows_at(bit * (rows // 2), rows // 2), slice(None))]
+    return ref.at[(*lead, slice(None), lanes_at(bit * (cols // 2), cols // 2))]
+
+
+def half_shape(shape, kind):
+    if kind == LEAD:
+        return shape[1:]
+    if kind == ROWS:
+        return (*shape[:-2], shape[-2] // 2, shape[-1])
+    return (*shape[:-1], shape[-1] // 2)
+
+
+def add_into(total, term):
+    def body(step, carry):
+        at = rows_at(step * 16, 16)
+        for lead in range(total.shape[0]) if len(total.shape) == 3 else (None,):
+            where = (at, slice(None)) if lead is None else (lead, at, slice(None))
+            total[where] = low(wide(total[where]) + wide(term[where]))
+        return carry
+
+    lax.fori_loop(0, total.shape[-2] // 16, body, 0)
+
+
+class Halving:
+    def __init__(self, courier, bits, targets, sums, stages):
+        self.courier, self.bits, self.targets = courier, bits, targets
+        self.sums, self.stages, self.pending = sums, stages, {}
+
+    def give(self, which, stage):
+        axis, kind = ROUTES[which][stage]
+        self.pending[which] = self.courier.send(
+            cut(self.sums[which], kind, 1 - self.bits[axis]),
+            self.stages[which][stage],
+            self.targets[axis],
+        )
+
+    def take(self, which, stage):
+        axis, kind = ROUTES[which][stage]
+        self.pending[which].wait_recv()
+        add_into(self.stages[which][stage], cut(self.sums[which], kind, self.bits[axis]))
+        self.sums[which] = self.stages[which][stage]
+
+
+def chain_of(which, shape):
+    chain = []
+    for _, kind in ROUTES[which]:
+        shape = half_shape(shape, kind)
+        chain.append(shape)
+    return chain
 
 
 def head_lanes(first, shape):
@@ -259,6 +348,7 @@
             (r.w_down, r.f_down),
         )
     ]
+    clear(r.base)
     greet([targets[CORE], targets[X], *ring])
     courier = Courier(r.send, r.recv)
 
@@ -294,7 +384,6 @@
             return carry
 
         lax.fori_loop(0, rows // 32, body, 0)
-        return begin(full, rows)
 
     key_rows = r.f_key.shape[0]
     loads[0].wait()
@@ -309,11 +398,6 @@
 
     lax.fori_loop(0, key_rows // 32, place_pair, 0)
     pair_state = begin(r.pair_full, key_rows)
-
-    def norm(values):
-        shifted = values - jnp.mean(values, axis=-1, keepdims=True)
-        inverse = lax.rsqrt(jnp.mean(shifted * shifted, axis=-1, keepdims=True) + 1e-05)
-        return shifted * inverse, inverse
 
     def norm_in(step, carry):
         at = rows_at(step * 64, 64)
@@ -324,9 +408,6 @@
         return carry
 
     lax.fori_loop(0, r.in_low.shape[0] // 64, norm_in, 0)
-    loads[2].wait()
-    query_state = place(r.query_full, r.f_query)
-
     def norm_lat(step, carry):
         at = rows_at(step * 32, 32)
         hat, _ = norm(r.latents[at, :])
@@ -339,10 +420,25 @@
         r.f_out.shape[0],
         r.f_up.shape[0],
     )
+    for index in range(4):
+
+        @pl.when(opt == index)
+        def _(index=index):
+            r.lat_block[...] = r.lat_low[:, index * up_rows : (index + 1) * up_rows]
+
+    for index, (full, staged) in enumerate(
+        (
+            (r.query_full, r.f_query),
+            (r.out_full, r.f_out),
+            (r.up_full, r.f_up),
+            (r.down_full, r.f_down),
+        )
+    ):
+        loads[2 + index].wait()
+        place(full, staged)
     relay(r.pair_full, key_rows, pair_state)
+    query_state = begin(r.query_full, query_rows)
     relay_more(r.pair_full, key_rows, pair_state)
-    loads[3].wait()
-    out_state = place(r.out_full, r.f_out)
     complete(pair_state)
 
     def project(step, carry):
@@ -352,9 +448,8 @@
 
     lax.fori_loop(0, r.in_low.shape[0] // 128, project, 0)
     relay(r.query_full, query_rows, query_state)
+    out_state = begin(r.out_full, out_rows)
     relay_more(r.query_full, query_rows, query_state)
-    loads[4].wait()
-    up_state = place(r.up_full, r.f_up)
     complete(query_state)
 
     def project_query(step, carry):
@@ -364,6 +459,8 @@
 
     lax.fori_loop(0, lat_count // 128, project_query, 0)
 
+    relay(r.out_full, out_rows, out_state)
+    up_state = begin(r.up_full, up_rows)
     to_owner = []
     for m in range(micro):
         at = slice(m * span, (m + 1) * span)
@@ -388,19 +485,35 @@
                 courier.send(r.part.at[m, rows], r.part_in.at[seq, m], target)
             )
         if m == 0:
-            relay(r.out_full, out_rows, out_state)
             relay_more(r.out_full, out_rows, out_state)
-            loads[5].wait()
-            down_state = place(r.down_full, r.f_down)
+            relay(r.up_full, up_rows, up_state)
+            down_state = begin(r.down_full, up_rows)
     for target in ring:
         rows = rows_at(target[0] * own, own)
         to_owner.append(courier.send(r.lse.at[rows], r.lse_in.at[seq], target))
     mine = rows_at(seq * own, own)
     r.part_in[seq] = r.part[:, mine, :]
     r.lse_in[seq] = r.lse[mine, :]
-    relay(r.up_full, up_rows, up_state)
     relay_more(r.up_full, up_rows, up_state)
     relay(r.down_full, up_rows, down_state)
+    for moment, staged, slot in zip(
+        (r.mom_query, r.mom_key, r.mom_value, r.mom_out, r.mom_up, r.mom_down),
+        (r.f_query, r.f_key, r.f_value, r.f_out, r.f_up, r.f_down),
+        SLOTS,
+    ):
+
+        @pl.when(seq == slot)
+        def _(moment=moment, staged=staged):
+            copy = pltpu.make_async_copy(moment, staged, r.moment_sem)
+            copy.start()
+            copy.wait()
+            r.base[rows_at(opt * up_rows, staged.shape[0]), : staged.shape[1]] = low(
+                0.95 * staged[...]
+            )
+
+    own_base = r.base.at[rows_at(opt * up_rows, up_rows)]
+    base_across = courier.send(own_base, own_base, targets[X])
+    base_beside = courier.send(own_base, own_base, targets[CORE])
     relay_more(r.down_full, up_rows, down_state)
     for copy in to_owner:
         copy.wait_recv()
@@ -499,13 +612,31 @@
         (r.grad_up, r.x_mlp, r.x_pre),
         (r.grad_out, r.x_att, r.x_branch),
     ):
-        for tile in range(left.shape[1] // TILE):
-            cols = slice(tile * TILE, (tile + 1) * TILE)
-            target[cols, :] = low(dot_tn(left[:, cols], right[:, half]))
+        for tile in range(left.shape[1] // 128):
+            cols = slice(tile * 128, (tile + 1) * 128)
+            x_half, first = divmod(tile * 128, target.shape[1])
+            target[x_half, first : first + 128, :] = low(dot_tn(left[:, cols], right[:, half]))
+    halving = Halving(
+        courier,
+        bits,
+        targets,
+        {UP: r.grad_up, DOWN: r.grad_down, OUT: r.grad_out},
+        {
+            UP: (r.up_0, r.up_1, r.up_2, r.piece_up),
+            DOWN: (r.down_0, r.down_1, r.down_2, r.piece_down),
+            OUT: (r.out_0, r.out_1, r.out_2, r.piece_out),
+        },
+    )
+    for which in (UP, DOWN, OUT):
+        halving.give(which, 0)
     for copy in returns:
         copy.wait_recv()
 
     for h in range(HEADS):
+        if h in POINTS:
+            which, stage = POINTS[h]
+            halving.take(which, stage)
+            halving.give(which, stage + 1)
         ch = slice(h * HEAD_DIM, (h + 1) * HEAD_DIM)
         ch_v = slice(width + h * HEAD_DIM, width + (h + 1) * HEAD_DIM)
         grad_query = None
@@ -527,19 +658,24 @@
 
     part_width = width // 2
 
-    def pair_product(target, which):
-        for kind in range(2):
+    def pair_product(targets_two, which):
+        for kind, target in enumerate(targets_two):
             cols = lanes_at(kind * width + which * part_width, part_width)
             right = r.grad_pairs[:, cols]
             for tile in range(width // TILE):
                 rows = slice(tile * TILE, (tile + 1) * TILE)
-                target[rows, kind * part_width : (kind + 1) * part_width] = low(
-                    dot_tn(r.in_low[:, rows], right)
-                )
-
-    pair_product(r.pair_other, 1 - core)
+                target[rows, :] = low(dot_tn(r.in_low[:, rows], right))
+
+    base_across.wait_recv()
+    other_base = r.base.at[rows_at(opt_x * up_rows, up_rows)]
+    base_last = courier.send(other_base, other_base, targets[CORE])
+    base_beside.wait_recv()
+    pair_product((r.pair_other.at[0], r.pair_other.at[1]), 1 - core)
     pair_copy = courier.send(r.pair_other, r.pair_in, targets[CORE])
-    pair_product(r.grad_pair, core)
+    for which in (UP, OUT, DOWN):
+        halving.take(which, 2)
+        halving.give(which, 3)
+    pair_product((r.grad_key, r.grad_value), core)
     r.in_sums[...] = jnp.zeros_like(r.in_sums)
 
     def norm_in_back(step, carry):
@@ -558,12 +694,16 @@
 
     lax.fori_loop(0, r.in_low.shape[0] // 64, norm_in_back, 0)
     r.vectors[4:6, :width] = r.in_sums[0:2, :]
+    base_last.wait_recv()
     pair_copy.wait_recv()
-    add_into(r.grad_pair, r.pair_in)
+    add_into(r.grad_key, r.pair_in.at[0])
+    add_into(r.grad_value, r.pair_in.at[1])
+    for which in (UP, OUT, DOWN):
+        halving.take(which, 3)
     courier.finish()
 
 
-def run_pass(tokens, usable, cotangent, latents, lat_vectors, in_vectors, weights):
+def run_pass(tokens, usable, cotangent, latents, lat_vectors, in_vectors, weights, moments):
     f32, bf16 = jnp.float32, jnp.bfloat16
     w_query, w_key, w_value, w_out, w_up, w_down = weights
     operands = dict(
@@ -579,6 +719,12 @@
         w_out=w_out,
         w_up=w_up,
         w_down=w_down,
+        mom_query=moments[0],
+        mom_key=moments[1],
+        mom_value=moments[2],
+        mom_out=moments[3],
+        mom_up=moments[4],
+        mom_down=moments[5],
     )
     count, width = tokens.shape
     micro, _, span = usable.shape
@@ -588,17 +734,20 @@
     outputs = dict(
         block_out=((rows, width_lat), bf16),
         input_grad=((count, width), f32),
-        grad_up=((width_lat, width_lat // 2), bf16),
-        grad_down=((width_lat, width_lat // 2), bf16),
-        grad_out=((width, width_lat // 2), bf16),
-        grad_pair=((width, width), bf16),
+        grad_key=((width, width // 2), bf16),
+        grad_value=((width, width // 2), bf16),
         grad_query=((lat_count, width), bf16),
         vectors=((8, width_lat), f32),
         rest=((own, width_lat), bf16),
         lat_low=((lat_count, width_lat), bf16),
+        lat_block=((lat_count, width_lat // 4), bf16),
         query_full=((width_lat, width), bf16),
+        base=((width_lat, width_lat), bf16),
     )
     scratch = dict(
+        grad_up=((2, width_lat // 2, width_lat // 2), bf16),
+        grad_down=((2, width_lat // 2, width_lat // 2), bf16),
+        grad_out=((2, width // 2, width_lat // 2), bf16),
         f_query=(w_query.shape, f32),
         f_key=(w_key.shape, f32),
         f_value=(w_value.shape, f32),
@@ -634,21 +783,27 @@
         grad_att=((micro, lat_count, width), bf16),
         back=((lat_count, 128), f32),
         grad_pairs=((count, 2 * width), bf16),
-        pair_other=((width, width), bf16),
-        pair_in=((width, width), bf16),
-    )
-    copies = 5 * 5 + 7 * micro + 7 + 14 + 6 + 1
+        pair_other=((2, width, width // 2), bf16),
+        pair_in=((2, width, width // 2), bf16),
+    )
+    for which, name in ((UP, "up"), (DOWN, "down"), (OUT, "out")):
+        chain = chain_of(which, scratch["grad_" + name][0])
+        for stage, shape in enumerate(chain[:-1]):
+            scratch[f"{name}_{stage}"] = (shape, bf16)
+        outputs["piece_" + name] = (chain[-1], bf16)
+    copies = 5 * 5 + 7 * micro + 7 + 14 + 6 + 1 + 3 + 12
     sems = dict(
         send=pltpu.SemaphoreType.DMA((copies,)),
         recv=pltpu.SemaphoreType.DMA((copies,)),
         local=pltpu.SemaphoreType.DMA((6,)),
+        moment_sem=pltpu.SemaphoreType.DMA,
     )
     keys = (*operands, *outputs, *scratch, *sems)
     vmem, anywhere = pl.BlockSpec(memory_space=pltpu.VMEM), pl.BlockSpec(memory_space=pl.ANY)
     results = pl.pallas_call(
         functools.partial(pass_body, keys),
         out_shape=[jax.ShapeDtypeStruct(*spec) for spec in outputs.values()],
-        in_specs=[vmem] * 6 + [anywhere] * 6,
+        in_specs=[vmem] * 6 + [anywhere] * 12,
         out_specs=[vmem] * len(outputs),
         scratch_shapes=[*(pltpu.VMEM(*spec) for spec in scratch.values()), *sems.values()],
         compiler_params=pltpu.CompilerParams(
@@ -659,80 +814,65 @@
     return named(outputs, results)
 
 
-def cut(ref, kind, bit):
-    if kind == LEAD:
-        return ref.at[bit]
-    rows, cols = ref.shape[-2:]
-    lead = (slice(None),) * (len(ref.shape) - 2)
-    if kind == ROWS:
-        return ref.at[(*lead, rows_at(bit * (rows // 2), rows // 2), slice(None))]
-    return ref.at[(*lead, slice(None), lanes_at(bit * (cols // 2), cols // 2))]
-
-
-def half_shape(shape, kind):
-    if kind == LEAD:
-        return shape[1:]
-    if kind == ROWS:
-        return (*shape[:-2], shape[-2] // 2, shape[-1])
-    return (*shape[:-1], shape[-1] // 2)
-
-
-def add_into(total, term):
-    def body(step, carry):
-        at = rows_at(step * 16, 16)
-        for lead in range(total.shape[0]) if len(total.shape) == 3 else (None,):
-            where = (at, slice(None)) if lead is None else (lead, at, slice(None))
-            total[where] = low(wide(total[where]) + wide(term[where]))
-        return carry
-
-    lax.fori_loop(0, total.shape[-2] // 16, body, 0)
-
-
-ROUTES = (
-    ((X, LEAD), (Y, ROWS), (Z0, ROWS), (Z1, ROWS)),
-    ((Y, ROWS), (X, LEAD), (Z0, ROWS), (Z1, ROWS)),
-    ((Z0, ROWS), (X, LEAD), (Y, ROWS), (Z1, ROWS)),
-    ((Z0, ROWS), (Y, ROWS), (X, LEAD), (Z1, ROWS)),
-    ((CORE, COLS), (X, ROWS), (Y, ROWS), (Z0, ROWS), (Z1, ROWS)),
-)
-UP, DOWN, PAIR, OUT, QUERY = range(5)
-SLOTS = (3, 0, 7, 4, 2, 5)
-
-
-def combine_body(keys, shapes, *refs):
+def tail_body(keys, *refs):
     r = named(keys, refs)
     seq, opt = lax.axis_index("seq"), lax.axis_index("opt")
     bits, targets = partners(seq, opt)
-    core, z0, z1, y = bits[CORE], bits[Z0], bits[Z1], bits[Y]
-    load = Loader(r.local)
-    moments = (r.mom_query, r.mom_key, r.mom_value, r.mom_out, r.mom_up, r.mom_down)
-    held = (r.h_query, r.h_key, r.h_value, r.h_out, r.h_up, r.h_down)
-    loads = [load.start(source, target) for source, target in zip(moments, held)]
-    greet(targets)
+    core, z0, z1, y, x = bits[CORE], bits[Z0], bits[Z1], bits[Y], bits[X]
+    ring = [((seq + step) % 8, opt) for step in range(1, 8)]
+    height = r.lat_block.shape[1]
+    clear(r.g_full.at[0])
+    clear(r.g_full.at[1])
+    beyond = [((seq + step) % 8, targets[X][1]) for step in range(8)]
+    greet([targets[CORE], *ring, *beyond])
     courier = Courier(r.send, r.recv)
-    sums = [r.up, r.down, r.pair, r.out, r.query]
-    first = 0
-    stages = []
-    for shape_list in shapes:
-        stages.append([getattr(r, f"s{first + index}") for index in range(len(shape_list))])
-        first += len(shape_list)
-    pending = {}
-
-    def give(which, stage):
-        axis, kind = ROUTES[which][stage]
-        pending[which] = courier.send(
-            cut(sums[which], kind, 1 - bits[axis]), stages[which][stage], targets[axis]
-        )
-
-    def take(which, stage):
-        axis, kind = ROUTES[which][stage]
-        pending[which].wait_recv()
-        add_into(stages[which][stage], cut(sums[which], kind, bits[axis]))
-        sums[which] = stages[which][stage]
-
-    give(QUERY, 0)
-    for which in (PAIR, OUT, UP, DOWN):
-        give(which, 0)
+    sums = {UP: r.up, DOWN: r.down, OUT: r.out, KEY: r.key, VALUE: r.value, QUERY: r.query}
+    halving = Halving(
+        courier,
+        bits,
+        targets,
+        sums,
+        {
+            KEY: (r.key_0, r.key_1, r.key_2, r.key_3),
+            VALUE: (r.value_0, r.value_1, r.value_2, r.value_3),
+            QUERY: (r.query_0, r.query_1, r.query_2, r.query_3, r.query_4),
+        },
+    )
+    for which in (QUERY, KEY, VALUE):
+        halving.give(which, 0)
+    def piece_place(which, seq_from, x_from):
+        bit_y, bit_z0, bit_z1 = seq_from % 2, (seq_from // 2) % 2, seq_from // 4
+        high, mid = (bit_y, bit_z0) if which in Y_FIRST else (bit_z0, bit_y)
+        rows = sums[which].shape[0]
+        return rows_at(x_from * (2 * height) + high * height + (mid * 2 + bit_z1) * rows, rows)
+
+    def piece_copy(index, which, seq_from, x_from, same):
+        cols = sums[which].shape[1]
+        place = piece_place(which, seq_from, x_from)
+        return pltpu.make_async_remote_copy(
+            src_ref=sums[which],
+            dst_ref=r.g_full.at[core, place, pl.ds(0, cols)],
+            send_sem=r.piece_send.at[index, 0 if same else 1],
+            recv_sem=r.piece_recv.at[0 if same else 1, seq_from],
+            device_id=(SLOTS[index], opt if same else targets[X][1]),
+            device_id_type=MESH,
+        )
+
+    def offer(index, which):
+        piece_copy(index, which, seq, x, False).start()
+
+        @pl.when(seq != SLOTS[index])
+        def _():
+            piece_copy(index, which, seq, x, True).start()
+
+        @pl.when(seq == SLOTS[index])
+        def _():
+            cols = sums[which].shape[1]
+            r.g_full[core, piece_place(which, seq, x), :cols] = sums[which][...]
+
+    owned = ((1, KEY), (2, VALUE), (3, OUT), (4, UP), (5, DOWN))
+    for index, which in owned[2:]:
+        offer(index, which)
     r.vectors_sum[...] = r.vectors[...]
     vector_copy = courier.send(r.vectors, r.vectors_in.at[0], targets[CORE])
     rest_width = r.rest.shape[1] // 2
@@ -740,8 +880,8 @@
     rest_copy = courier.send(
         r.rest.at[:, lanes_at((1 - core) * rest_width, rest_width)], r.rest_in.at[0], targets[CORE]
     )
-    take(QUERY, 0)
-    give(QUERY, 1)
+    halving.take(QUERY, 0)
+    halving.give(QUERY, 1)
     vector_copy.wait_recv()
     r.vectors_sum[...] = r.vectors_sum[...] + r.vectors_in[0]
     rest_copy.wait_recv()
@@ -761,260 +901,178 @@
             lead = ((z1, z0, y), (every, z0, y), (every, every, y))[stage - 1]
             view = r.rest_all.at[(*lead, every, column)]
             rest_copy = courier.send(view, view, targets[(Z1, Z0, Y)[stage - 1]])
-        for which in (QUERY, PAIR, OUT, UP, DOWN):
+        for which in (QUERY, KEY, VALUE):
             own_stage = stage + 1 if which == QUERY else stage
-            take(which, own_stage)
+            halving.take(which, own_stage)
             if stage < 3:
-                give(which, own_stage + 1)
+                halving.give(which, own_stage + 1)
         vector_copy.wait_recv()
         r.vectors_sum[...] = r.vectors_sum[...] + r.vectors_in[stage + 1]
     rest_copy.wait_recv()
     view = r.rest_all.at[:, :, :, :, column]
     rest_copy = courier.send(view, view, targets[CORE])
 
+    for index, which in owned[:2]:
+        offer(index, which)
     rows, width = sums[QUERY].shape
     query_column = lanes_at(core * width, width)
-    start = (bits[X] * 8 + y * 4 + z0 * 2 + z1) * rows
+    start = (x * 8 + y * 4 + z0 * 2 + z1) * rows
     r.query_all[rows_at(start, rows), query_column] = sums[QUERY][...]
-    query_steps = (
-        (Z1, 1, start),
-        (Z0, 2, start - z1 * rows),
-        (Y, 4, start - (z1 + z0 * 2) * rows),
-        (X, 8, bits[X] * (8 * rows)),
-    )
-    gathered = (r.g_up, r.g_down, r.g_pair, r.g_out)
-    for which in range(4):
-        high, mid = (y, z0) if which in (UP, DOWN) else (z0, y)
+    view = r.query_all.at[rows_at(start, rows), query_column]
+    query_copies = [courier.send(view, view, target) for target in ring]
+
+    gathered = (r.g_up, r.g_down, r.g_key, r.g_value, r.g_out)
+    full = (r.n_up, r.n_down, r.n_key, r.n_value, r.n_out)
+    for which in range(5):
+        high, mid = (y, z0) if which in Y_FIRST else (z0, y)
         rows = sums[which].shape[0]
         gathered[which][rows_at((high * 4 + mid * 2 + z1) * rows, rows), :] = sums[which][...]
 
-    def query_step(step):
-        axis, count, base = query_steps[step]
-        view = r.query_all.at[rows_at(base, count * sums[QUERY].shape[0]), query_column]
-        return courier.send(view, view, targets[axis])
-
-    query_copy = None
-    for step in range(3):
-        if step > 0:
-            query_copy.wait_recv()
-        query_copy = query_step(step)
-        for which in (UP, DOWN, PAIR, OUT):
-            first_axis, last_axis = (Y, Z0) if which in (UP, DOWN) else (Z0, Y)
-            high, mid = bits[first_axis], bits[last_axis]
-            rows = sums[which].shape[0]
-            if step > 0:
-                pending[which].wait_recv()
+    def gather(which, step):
+        first_axis, last_axis = (Y, Z0) if which in Y_FIRST else (Z0, Y)
+        high, mid = bits[first_axis], bits[last_axis]
+        rows = sums[which].shape[0]
+        if step < 3:
             base, count = ((high * 4 + mid * 2 + z1, 1), (high * 4 + mid * 2, 2), (high * 4, 4))[
                 step
             ]
-            view = gathered[which].at[rows_at(base * rows, count * rows)]
-            pending[which] = courier.send(
-                view, view, targets[(Z1, last_axis, first_axis)[step]]
+            source = target = gathered[which].at[rows_at(base * rows, count * rows)]
+        else:
+            cols = sums[which].shape[1]
+            source = gathered[which].at[rows_at((1 - core) * (4 * rows), 4 * rows)]
+            target = full[which].at[:, lanes_at(core * cols, cols)]
+        return pltpu.make_async_remote_copy(
+            src_ref=source,
+            dst_ref=target,
+            send_sem=r.gather_send.at[which, step],
+            recv_sem=r.gather_recv.at[which, step],
+            device_id=targets[(Z1, last_axis, first_axis, CORE)[step]],
+            device_id_type=MESH,
+        )
+
+    for which in range(5):
+        gather(which, 0).start()
+    for copy in query_copies:
+        copy.wait_recv()
+    view = r.query_all.at[rows_at(x * (8 * sums[QUERY].shape[0]), 8 * sums[QUERY].shape[0]), query_column]
+    courier.send(view, view, targets[X]).wait_recv()
+    view = r.query_all.at[:, query_column]
+    courier.send(view, view, targets[CORE]).wait_recv()
+    rest_copy.wait_recv()
+
+    for index, which in owned:
+
+        @pl.when(seq == SLOTS[index])
+        def _(index=index, which=which):
+            for seq_from in range(8):
+                if seq_from != SLOTS[index]:
+                    piece_copy(index, which, seq_from, x, True).wait_recv()
+                piece_copy(index, which, seq_from, 1 - x, False).wait_recv()
+
+    beside = courier.send(r.g_full.at[core], r.g_full.at[core], targets[CORE])
+    beside.wait_recv()
+    side = r.whole.shape[1]
+    tiles = side // TILE
+    narrow = (seq == SLOTS[1]) | (seq == SLOTS[2])
+    r.total[0] = 0.0
+
+    def join(tile, carry):
+        at = rows_at(tile * TILE, TILE)
+        r.wide[at, :] = wide(r.base[at, :])
+
+        @pl.when(jnp.logical_not(narrow))
+        def _():
+            for index in range(2):
+                lanes = slice(index * (side // 2), (index + 1) * (side // 2))
+                r.wide[at, lanes] = r.wide[at, lanes] + wide(r.g_full[index, at, :])
+
+        @pl.when(narrow)
+        def _():
+            part = width
+            for index in range(2):
+                lanes = slice(index * part, (index + 1) * part)
+                r.wide[at, lanes] = r.wide[at, lanes] + wide(r.g_full[index, at, :part])
+
+        @pl.when(seq == SLOTS[0])
+        def _():
+            lanes = slice(0, 2 * width)
+            r.wide[at, lanes] = r.wide[at, lanes] + dot_tn(
+                r.lat_low[:, lanes_at(tile * TILE, TILE)], r.query_all[...]
             )
-    full = (r.n_up, r.n_down, r.n_pair, r.n_out)
-    for which in (OUT, PAIR, DOWN, UP):
-        pending[which].wait_recv()
-        rows, cols = gathered[which].shape
-        at = lanes_at(core * cols, cols)
-        pending[which] = courier.send(
-            gathered[which].at[rows_at((1 - core) * (rows // 2), rows // 2)],
-            full[which].at[:, at],
-            targets[CORE],
-        )
-        full[which][:, at] = gathered[which][rows_at(core * (rows // 2), rows // 2), :]
-    query_copy.wait_recv()
-    query_copy = query_step(3)
-    query_copy.wait_recv()
-    view = r.query_all.at[:, query_column]
-    query_copy = courier.send(view, view, targets[CORE])
-    height, side = r.whole.shape[1:]
-    clear_rows = 32
-
-    def clear(step, carry):
-        r.whole[opt, rows_at(step * clear_rows, clear_rows), :] = jnp.zeros(
-            (clear_rows, side), jnp.bfloat16
-        )
+
+        block = r.wide[at, :]
+        r.total[0] = r.total[0] + jnp.sum(block * block)
         return carry
 
-    lax.fori_loop(0, height // clear_rows, clear, 0)
-    for copy in loads:
-        copy.wait()
-    for which in range(4):
-        pending[which].wait_recv()
-    query_copy.wait_recv()
-    part = r.g_pair.shape[1] // 2
-    r.new_query[...] = 0.95 * r.h_query[...] + dot_tn(r.lat_block[...], r.query_all[...])
-    for kind, (target, moment) in enumerate(((r.new_key, r.h_key), (r.new_value, r.h_value))):
-        for side_core in range(2):
-            cols = slice(side_core * part, (side_core + 1) * part)
-            source = side_core * (2 * part) + kind * part
-            target[:, cols] = 0.95 * moment[:, cols] + wide(r.n_pair[:, source : source + part])
-    for target, moment, source in (
-        (r.new_out, r.h_out, r.n_out),
-        (r.new_up, r.h_up, r.n_up),
-        (r.new_down, r.h_down, r.n_down),
-    ):
-        target[...] = 0.95 * moment[...] + wide(source[...])
-
-    news = (r.new_query, r.new_key, r.new_value, r.new_out, r.new_up, r.new_down)
-    for new, slot in zip(news, SLOTS):
-
-        @pl.when(seq == slot)
-        def _(new=new):
-            r.whole[opt, : new.shape[0], : new.shape[1]] = low(new[...])
-
-    own = r.whole.at[opt]
-    across = courier.send(own, own, targets[X])
-    beside = courier.send(own, own, targets[CORE])
-    across.wait_recv()
-    other = r.whole.at[targets[X][1]]
-    last = courier.send(other, other, targets[CORE])
-    beside.wait_recv()
-    last.wait_recv()
-    rest_copy.wait_recv()
-    courier.finish()
-
-
-def combine(done, lat_block, moments, height):
-    f32, bf16 = jnp.float32, jnp.bfloat16
-    mom_query, mom_key, mom_value, mom_out, mom_up, mom_down = moments
-    width_lat = done.grad_up.shape[0]
-    halved = [
-        grad.reshape(2, grad.shape[0] // 2, grad.shape[1])
-        for grad in (done.grad_up, done.grad_down, done.grad_pair, done.grad_out)
-    ]
-    operands = dict(
-        vectors=done.vectors,
-        rest=done.rest,
-        lat_block=lat_block,
-        up=halved[0],
-        down=halved[1],
-        pair=halved[2],
-        out=halved[3],
-        query=done.grad_query,
-        mom_query=mom_query,
-        mom_key=mom_key,
-        mom_value=mom_value,
-        mom_out=mom_out,
-        mom_up=mom_up,
-        mom_down=mom_down,
-    )
-    outputs = dict(
-        new_query=(mom_query.shape, f32),
-        new_key=(mom_key.shape, f32),
-        new_value=(mom_value.shape, f32),
-        new_out=(mom_out.shape, f32),
-        new_up=(mom_up.shape, f32),
-        new_down=(mom_down.shape, f32),
-        query_all=(done.grad_query.shape, bf16),
-        vectors_sum=(done.vectors.shape, f32),
-        rest_all=((2, 2, 2, *done.rest.shape), bf16),
-        whole=((4, height, width_lat), bf16),
-    )
-    half_rest = (done.rest.shape[0], done.rest.shape[1] // 2)
-    scratch = dict(
-        vectors_in=((5, *done.vectors.shape), f32),
-        vectors_out=((4, *done.vectors.shape), f32),
-        rest_in=((2, *half_rest), bf16),
-        rest_sum=(half_rest, bf16),
-        h_query=(mom_query.shape, f32),
-        h_key=(mom_key.shape, f32),
-        h_value=(mom_value.shape, f32),
-        h_out=(mom_out.shape, f32),
-        h_up=(mom_up.shape, f32),
-        h_down=(mom_down.shape, f32),
-        g_up=(halved[0].shape[1:], bf16),
-        g_down=(halved[1].shape[1:], bf16),
-        g_pair=(halved[2].shape[1:], bf16),
-        g_out=(halved[3].shape[1:], bf16),
-        n_up=(mom_up.shape, bf16),
-        n_down=(mom_down.shape, bf16),
-        n_pair=((mom_key.shape[0], 2 * mom_key.shape[1]), bf16),
-        n_out=(mom_out.shape, bf16),
-    )
-    shapes = []
-    for array, route in zip((*halved, done.grad_query), ROUTES):
-        shape, chain = array.shape, []
-        for _, kind in route:
-            shape = half_shape(shape, kind)
-            chain.append(shape)
-        shapes.append(chain)
-    for index, shape in enumerate(sum(shapes, [])):
-        scratch[f"s{index}"] = (shape, bf16)
-    copies = 64
-    sems = dict(
-        send=pltpu.SemaphoreType.DMA((copies,)),
-        recv=pltpu.SemaphoreType.DMA((copies,)),
-        local=pltpu.SemaphoreType.DMA((6,)),
-    )
-    keys = (*operands, *outputs, *scratch, *sems)
-    vmem, anywhere = pl.BlockSpec(memory_space=pltpu.VMEM), pl.BlockSpec(memory_space=pl.ANY)
-    results = pl.pallas_call(
-        functools.partial(combine_body, keys, shapes),
-        out_shape=[jax.ShapeDtypeStruct(*spec) for spec in outputs.values()],
-        in_specs=[vmem] * 8 + [anywhere] * 6,
-        out_specs=[vmem] * len(outputs),
-        scratch_shapes=[*(pltpu.VMEM(*spec) for spec in scratch.values()), *sems.values()],
-        compiler_params=pltpu.CompilerParams(
-            collective_id=0, has_side_effects=True, vmem_limit_bytes=VMEM_LIMIT
-        ),
-        name="combine",
-    )(*operands.values())
-    return named(outputs, results)
-
-
-def spread_body(result_ref, *refs):
-    count = len(SLOTS)
-    outs = refs[:count]
-    send_sem, recv_sem, local_sem = refs[count:]
-    seq, opt = lax.axis_index("seq"), lax.axis_index("opt")
-    y, z = seq % 2, seq // 2
-    targets = partners(seq, opt)[1]
-    depth = 4
-    barrier = pltpu.get_barrier_semaphore()
-    pl.semaphore_signal(barrier, inc=1, device_id=targets[Y], device_id_type=MESH)
-    for step in (-1, 1):
-
-        @pl.when((z + step >= 0) & (z + step < depth))
-        def _(step=step):
-            pl.semaphore_signal(
-                barrier, inc=1, device_id=(seq + 2 * step, opt), device_id_type=MESH
-            )
-
-    inside = (z > 0) & (z < depth - 1)
-
-    @pl.when(inside)
-    def _():
-        pl.semaphore_wait(barrier, 3)
-
-    @pl.when(jnp.logical_not(inside))
-    def _():
-        pl.semaphore_wait(barrier, 2)
-
-    def copy(which, part, way):
-        index = which * PARTS + part
+    lax.fori_loop(0, tiles, join, 0)
+    scale = 1.0 / (jnp.sqrt(jnp.full((1, 1), r.total[0], jnp.float32)) + 1e-07)
+
+    def normalise(tile, carry):
+        at = rows_at(tile * TILE, TILE)
+        block = r.wide[at, :] * scale
+        r.wide[at, :] = block
+        r.whole[at, :] = low(block)
+        return carry
+
+    lax.fori_loop(0, tiles, normalise, 0)
+
+    def update(at):
+        block = coef_one * r.wide[at, :] + dot_nn(r.whole[at, :], r.poly[...])
+        r.wide[at, :] = block
+        r.whole[at, :] = low(block)
+
+    def sweep(index, carry):
+        for step, turn in enumerate((0, 1, 3, 4)):
+
+            @pl.when(index == turn)
+            def _(step=step):
+                if step < 4:
+                    for which in range(5):
+                        gather(which, step).wait_recv()
+                if step < 3:
+                    for which in range(5):
+                        gather(which, step + 1).start()
+                if step == 3:
+                    for which in range(5):
+                        rows, cols = gathered[which].shape
+                        full[which][:, lanes_at(core * cols, cols)] = gathered[which][
+                            rows_at(core * (rows // 2), rows // 2), :
+                        ]
+
+        polynomial(r.whole, r.gram, r.poly)
+
+        @pl.when(index < 4)
+        def _():
+            def step_rows(tile, inner):
+                update(rows_at(tile * TILE, TILE))
+                return inner
+
+            lax.fori_loop(0, tiles, step_rows, 0)
+
+        return carry
+
+    lax.fori_loop(0, 5, sweep, 0)
+    own_first = opt * height
+    update(rows_at(own_first, height))
+
+    outs = (r.o_query, r.o_key, r.o_value, r.o_out, r.o_up, r.o_down)
+    z, depth = seq // 2, 4
+
+    def copy(which, part, way, mine):
         out = outs[which]
         rows = out.shape[0] // PARTS
         view = out.at[pl.ds(part * rows, rows)]
+        source = view
+        if mine:
+            source = r.whole.at[rows_at(own_first + part * rows, rows), pl.ds(0, out.shape[1])]
         return pltpu.make_async_remote_copy(
-            src_ref=view,
+            src_ref=source,
             dst_ref=view,
-            send_sem=send_sem.at[way, index],
-            recv_sem=recv_sem.at[index],
+            send_sem=r.spread_send.at[way, which * PARTS + part],
+            recv_sem=r.spread_recv.at[which * PARTS + part],
             device_id=((seq + 2, opt), (seq - 2, opt), targets[Y])[way],
             device_id_type=MESH,
         )
-
-    for which, slot in enumerate(SLOTS):
-        out = outs[which]
-
-        @pl.when(seq == slot)
-        def _(out=out):
-            load = pltpu.make_async_copy(
-                result_ref.at[opt, pl.ds(0, out.shape[0]), pl.ds(0, out.shape[1])], out, local_sem
-            )
-            load.start()
-            load.wait()
 
     def ways(which, mine):
         slot_y, slot_z = SLOTS[which] % 2, SLOTS[which] // 2
@@ -1025,58 +1083,177 @@
             turn,
         )
 
-    for mine in (True, False):
-        for part in range(PARTS):
-            for which in ORDER:
-                on = ways(which, mine)
-                if not mine:
-
-                    @pl.when(on[2])
-                    def _(which=which, part=part):
-                        copy(which, part, 2).wait_recv()
-
-                for way in range(3):
-
-                    @pl.when(on[way])
-                    def _(which=which, part=part, way=way):
-                        copy(which, part, way).start()
+    def for_ways(which, mine, action):
+        for way, on in enumerate(ways(which, mine)):
+
+            @pl.when(on)
+            def _(way=way):
+                action(way)
+
+    def latent_gradients():
+        r.lat_grads[...] = jnp.zeros_like(r.lat_grads)
+        r.lat_grads[2:6, :] = r.vectors_sum[0:4, :]
+
+        def latent_rows(step, carry):
+            at = rows_at(step * 32, 32)
+            hat, inverse = norm(r.latents[at, :])
+            grad = dot_nt(r.query_all[at, :], r.query_full[...])
+            r.lat_grads[0:1, :] = r.lat_grads[0:1, :] + jnp.sum(grad * hat, axis=0, keepdims=True)
+            r.lat_grads[1:2, :] = r.lat_grads[1:2, :] + jnp.sum(grad, axis=0, keepdims=True)
+            scaled = grad * r.lat_vectors[0:1, :]
+            r.latent_grad[at, :] = wide(r.rest_all[step // 4, (step // 2) % 2, step % 2]) + inverse * (
+                scaled
+                - jnp.mean(scaled, axis=-1, keepdims=True)
+                - hat * jnp.mean(scaled * hat, axis=-1, keepdims=True)
+            )
+            return carry
+
+        lax.fori_loop(0, r.latents.shape[0] // 32, latent_rows, 0)
+        r.query_grad[...] = dot_tn(r.lat_block[...], r.query_all[...])
+
+    for step in range(PARTS + 1):
+        if step == 1:
+            latent_gradients()
+        for which in ORDER if step < PARTS else ():
+            if step >= AHEAD:
+                for_ways(
+                    which, True, lambda way: copy(which, step - AHEAD, way, True).wait_send()
+                )
+            for_ways(which, True, lambda way: copy(which, step, way, True).start())
+        for which in ORDER if step > 0 else ():
+
+            @pl.when(ways(which, False)[2])
+            def _(which=which, step=step):
+                copy(which, step - 1, 2, False).wait_recv()
+
+            for_ways(which, False, lambda way: copy(which, step - 1, way, False).start())
+    for which in ORDER:
+
+        @pl.when(seq == SLOTS[which])
+        def _(which=which):
+            rows, cols = outs[which].shape
+            outs[which][...] = r.whole[rows_at(own_first, rows), :cols]
 
     for part in range(PARTS):
         for which in ORDER:
 
             @pl.when(y != SLOTS[which] % 2)
             def _(which=which, part=part):
-                copy(which, part, 2).wait_recv()
-
-    for mine in (True, False):
-        for part in range(PARTS):
-            for which in ORDER:
-                on = ways(which, mine)
-                for way in range(3):
-
-                    @pl.when(on[way])
-                    def _(which=which, part=part, way=way):
-                        copy(which, part, way).wait_send()
-
-
-def spread(result, shapes):
+                copy(which, part, 2, False).wait_recv()
+
+    for part in range(PARTS):
+        for which in ORDER:
+            for_ways(which, False, lambda way: copy(which, part, way, False).wait_send())
+            if part >= PARTS - AHEAD:
+                for_ways(which, True, lambda way: copy(which, part, way, True).wait_send())
+    for index, which in owned:
+        piece_copy(index, which, seq, x, False).wait_send()
+
+        @pl.when(seq != SLOTS[index])
+        def _(index=index, which=which):
+            piece_copy(index, which, seq, x, True).wait_send()
+
+    for which in range(5):
+        for step in range(4):
+            gather(which, step).wait_send()
+    courier.finish()
+
+
+def run_tail(done, latents, lat_vectors, moments):
+    f32, bf16 = jnp.float32, jnp.bfloat16
+    mom_query, mom_key, mom_value, mom_out, mom_up, mom_down = moments
+    width_lat = latents.shape[1]
+    key, value = (
+        grad.reshape(2, grad.shape[0] // 2, grad.shape[1])
+        for grad in (done.grad_key, done.grad_value)
+    )
+    operands = dict(
+        vectors=done.vectors,
+        rest=done.rest,
+        lat_low=done.lat_low,
+        lat_block=done.lat_block,
+        query_full=done.query_full,
+        base=done.base,
+        latents=latents,
+        lat_vectors=lat_vectors,
+        up=done.piece_up,
+        down=done.piece_down,
+        out=done.piece_out,
+        key=key,
+        value=value,
+        query=done.grad_query,
+    )
+    outputs = dict(
+        vectors_sum=(done.vectors.shape, f32),
+        lat_grads=((8, width_lat), f32),
+        latent_grad=(latents.shape, f32),
+        query_grad=(mom_query.shape, f32),
+        n_up=(mom_up.shape, bf16),
+        n_down=(mom_down.shape, bf16),
+        n_key=(mom_key.shape, bf16),
+        n_value=(mom_value.shape, bf16),
+        n_out=(mom_out.shape, bf16),
+        o_query=(mom_query.shape, bf16),
+        o_key=(mom_key.shape, bf16),
+        o_value=(mom_value.shape, bf16),
+        o_out=(mom_out.shape, bf16),
+        o_up=(mom_up.shape, bf16),
+        o_down=(mom_down.shape, bf16),
+    )
+    half_rest = (done.rest.shape[0], done.rest.shape[1] // 2)
+    scratch = dict(
+        vectors_in=((5, *done.vectors.shape), f32),
+        vectors_out=((4, *done.vectors.shape), f32),
+        rest_in=((2, *half_rest), bf16),
+        rest_sum=(half_rest, bf16),
+        rest_all=((2, 2, 2, *done.rest.shape), bf16),
+        query_all=(done.grad_query.shape, bf16),
+        g_full=((2, width_lat, width_lat // 2), bf16),
+        g_up=((width_lat // 2, width_lat // 2), bf16),
+        g_down=((width_lat // 2, width_lat // 2), bf16),
+        g_key=(key.shape[1:], bf16),
+        g_value=(value.shape[1:], bf16),
+        g_out=((2 * mom_out.shape[0], width_lat // 2), bf16),
+        wide=((width_lat, width_lat), f32),
+        whole=((width_lat, width_lat), bf16),
+        gram=((width_lat, width_lat), bf16),
+        poly=((width_lat, width_lat), bf16),
+    )
+    for which, name, array in (
+        (KEY, "key", key),
+        (VALUE, "value", value),
+        (QUERY, "query", done.grad_query),
+    ):
+        for stage, shape in enumerate(chain_of(which, array.shape)):
+            scratch[f"{name}_{stage}"] = (shape, bf16)
+    copies = 48
+    count = len(SLOTS) * PARTS
+    dma = pltpu.SemaphoreType.DMA
+    sems = dict(
+        send=dma((copies,)),
+        recv=dma((copies,)),
+        piece_send=dma((6, 2)),
+        piece_recv=dma((2, 8)),
+        gather_send=dma((5, 4)),
+        gather_recv=dma((5, 4)),
+        spread_send=dma((3, count)),
+        spread_recv=dma((count,)),
+        total=pltpu.SMEM((1,), f32),
+    )
+    keys = (*operands, *outputs, *scratch, *sems)
     vmem = pl.BlockSpec(memory_space=pltpu.VMEM)
-    count = len(SLOTS) * PARTS
-    return pl.pallas_call(
-        spread_body,
-        out_shape=[jax.ShapeDtypeStruct(shape, jnp.bfloat16) for shape in shapes],
-        in_specs=[pl.BlockSpec(memory_space=pl.ANY)],
-        out_specs=[vmem] * len(SLOTS),
-        scratch_shapes=[
-            pltpu.SemaphoreType.DMA((3, count)),
-            pltpu.SemaphoreType.DMA((count,)),
-            pltpu.SemaphoreType.DMA,
-        ],
+    results = pl.pallas_call(
+        functools.partial(tail_body, keys),
+        out_shape=[jax.ShapeDtypeStruct(*spec) for spec in outputs.values()],
+        in_specs=[vmem] * len(operands),
+        out_specs=[vmem] * len(outputs),
+        scratch_shapes=[*(pltpu.VMEM(*spec) for spec in scratch.values()), *sems.values()],
         compiler_params=pltpu.CompilerParams(
-            collective_id=1, has_side_effects=True, vmem_limit_bytes=VMEM_LIMIT
+            collective_id=0, has_side_effects=True, vmem_limit_bytes=VMEM_LIMIT
         ),
-        name="spread",
-    )(result)
+        name="tail",
+    )(*operands.values())
+    return named(outputs, results)
 
 
 def adam_update(param, gradient, first, second, step_rate, decay):
@@ -1113,7 +1290,7 @@
     latent_first,
     latent_second,
 ):
-    seq_index, opt_index = lax.axis_index("seq"), lax.axis_index("opt")
+    seq_index = lax.axis_index("seq")
     micro_count, _, span, width_in = inputs.shape
     lat_count, width_lat = latents.shape
     positions = seq_index * span + jnp.arange(span, dtype=jnp.int32)
@@ -1128,40 +1305,33 @@
         lat_vectors,
         in_vectors,
         masters,
-    )
-    height = w_up.shape[0]
-    summed = combine(
-        done,
-        lax.dynamic_slice_in_dim(done.lat_low, opt_index * height, height, 1),
         moments,
-        height,
-    )
-    moments_new = (
-        summed.new_query,
-        summed.new_key,
-        summed.new_value,
-        summed.new_out,
-        summed.new_up,
-        summed.new_down,
-    )
-    own_result = newton(summed.whole.reshape(-1, width_lat))
-    currents = spread(
-        own_result.reshape(summed.whole.shape), [moment.shape for moment in moments]
+    )
+    summed = run_tail(done, latents, lat_vectors, moments)
+    gradients = (
+        summed.query_grad,
+        summed.n_key,
+        summed.n_value,
+        summed.n_out,
+        summed.n_up,
+        summed.n_down,
+    )
+    moments_new = [
+        0.95 * moment + gradient.astype(jnp.float32)
+        for moment, gradient in zip(moments, gradients)
+    ]
+    currents = (
+        summed.o_query,
+        summed.o_key,
+        summed.o_value,
+        summed.o_out,
+        summed.o_up,
+        summed.o_down,
     )
     new_masters = update_masters(masters, currents)
-    _, lat_hat, lat_inv = layer_norm(latents, lat_vectors[0], lat_vectors[1])
-    grad_lat = jnp.dot(summed.query_all, done.query_full.T, preferred_element_type=jnp.float32)
-    lat_vec_sum = jnp.concatenate(
-        [
-            jnp.sum(grad_lat * lat_hat, axis=0)[None],
-            jnp.sum(grad_lat, axis=0)[None],
-            summed.vectors_sum[:4],
-        ]
-    )
+    lat_vec_sum = summed.lat_grads[:6]
     in_vec_sum = summed.vectors_sum[4:6, :width_in]
-    latent_sum = norm_back(grad_lat, lat_hat, lat_inv, lat_vectors[0]) + summed.rest_all.reshape(
-        latents.shape
-    ).astype(jnp.float32)
+    latent_sum = summed.latent_grad
     return (
         done.block_out.reshape(cotangent.shape),
         done.input_grad.reshape(inputs.shape),

time: 413 us -> 361 us (0.87)
  Pallas kernels: 378 us -> 328 us
  local copies, waits for them, and re-layouts: 14.1 us -> 8.18 us
    pallas_call x3 -> x1, Pallas kernels: 257 us -> 185 us  [run_tail(): pl.pallas_call(functools.partial(tail_body, keys), out_shape=[jax.ShapeDt...]
    pallas_call x1, Pallas kernels: 122 us -> 143 us  [run_pass(): pl.pallas_call(functools.partial(pass_body, keys), out_shape=[jax.ShapeDt...]
where the time goes in v3:
time: 361 us; the launch traced here: 355 us
  Pallas kernels  328 us (91%)
  other arithmetic  17.6 us (5%)
  local copies, waits for them, and re-layouts  8.18 us (2%)
    pallas_call x1, Pallas kernels, run_tail(): pl.pallas_call(functools.partial(tail_body, keys), out_shape=[jax.ShapeDt...  185 us
    pallas_call x1, Pallas kernels, run_pass(): pl.pallas_call(functools.partial(pass_body, keys), out_shape=[jax.ShapeDt...  143 us
    unnamed x70, local copies, waits for them, and re-layouts  8.18 us
    sub x4, other arithmetic, update_masters(): (1.0 - 0.1 * step_rate) * master  7.77 us

profile of v3, /device:TPU:0, one launch (start us, length us, event | category | flops | bytes accessed | tf_op | source)
XLA Modules:
  0.0 354.9 jit_solution(768912739164487281)
XLA Ops:
  0.7 1.3 and_convert_fusion.refs_1_
  2.0 142.9 %pass.1 = (bf16[64,1280]{1,0:T(8,128)(2,1)}, f32[512,768]{1,0:T(8,128)}, bf16[768,384]{1,0:T(8,128)(2,1)}, bf16[768,384]{1,0:T(8,128)(2,1)}, bf16[256,768]{1,0:T...) custom-call(bf16[512,768]{1,0:T(8,128)(2,1)} %bitcast.12, ...), custom_call_target="tpu_custom_call" | custom-call | tf_op jit(solution)/shard_map/pass/pallas_call | solution.py:803
  144.9 0.0 copy-start.31
  145.0 185.1 %tail.1 = (f32[8,1280]{1,0:T(8,128)}, f32[8,1280]{1,0:T(8,128)}, f32[256,1280]{1,0:T(8,128)}, f32[320,768]{1,0:T(8,128)}, bf16[320,1280]{1,0:T(8,128)(2,1)}, /*i...) custom-call(f32[8,1280]{1,0:T(8,128)} %get-tuple-element.54.refs_0_,, ...), custom_call_target="tpu_custom_call" | custom-call | tf_op jit(solution)/shard_map/tail/pallas_call | solution.py:1245
  330.1 1.4 multiply_subtract_fusion.2
  331.5 1.4 multiply_subtract_fusion.1
  333.0 3.0 convert_subtract_fusion.2
  336.0 1.1 convert_add_fusion.3
  337.2 0.5 copy-done.12
  337.6 0.1 copy-done.24
  337.7 0.1 copy-done.25
  337.8 1.1 convert_subtract_fusion.3
  339.0 0.4 copy-done.5
  339.4 0.4 copy-done.6
  339.8 0.1 copy-done.21
  339.9 0.1 copy-done.22
  340.0 1.6 multiply_subtract_fusion
  341.6 0.1 copy-done.1
  341.8 0.9 copy-done.2
  342.7 0.2 copy-done.19
  342.9 0.2 copy-done.20
  343.1 2.1 convert_add_fusion
  345.2 1.0 copy-done.4
  346.2 0.2 copy-done.17
  346.4 0.2 copy-done.18
  346.7 2.1 convert_subtract_fusion
  348.7 0.7 copy-done.14
  349.4 0.6 copy-done.15
  350.0 0.4 copy-done.16
  350.4 2.5 add_subtract_fusion
  352.8 0.7 copy.52
  353.5 1.1 copy.53
  (52 shorter events, 0.1 us)
Async XLA Ops:
  144.9 185.2 %copy-start.31 = (f32[2,768]{1,0:T(2,128)S(1)}, f32[2,768]{1,0:T(2,128)}, u32[]{:S(2)}) copy-start(f32[2,768]{1,0:T(2,128)} %refs_5_.1) | copy-start | bytes 18436
  145.0 185.2 %copy-start.32 = (f32[2,768]{1,0:T(2,128)S(1)}, f32[2,768]{1,0:T(2,128)}, u32[]{:S(2)}) copy-start(f32[2,768]{1,0:T(2,128)} %param.47) | copy-start | bytes 18436
  145.0 185.2 %copy-start.33 = (f32[2,768]{1,0:T(2,128)S(1)}, f32[2,768]{1,0:T(2,128)}, u32[]{:S(2)}) copy-start(f32[2,768]{1,0:T(2,128)} %param.46) | copy-start | bytes 18436
  145.0 186.5 %copy-start.23 = (f32[6,1280]{1,0:T(8,128)S(1)}, f32[6,1280]{1,0:T(8,128)}, u32[]{:S(2)}) copy-start(f32[6,1280]{1,0:T(8,128)} %refs_7_.3) | copy-start | bytes 92164
  145.0 186.5 %copy-start.29 = (f32[6,1280]{1,0:T(8,128)S(1)}, f32[6,1280]{1,0:T(8,128)}, u32[]{:S(2)}) copy-start(f32[6,1280]{1,0:T(8,128)} %param.45) | copy-start | bytes 92164
  145.0 186.5 %copy-start.30 = (f32[6,1280]{1,0:T(8,128)S(1)}, f32[6,1280]{1,0:T(8,128)}, u32[]{:S(2)}) copy-start(f32[6,1280]{1,0:T(8,128)} %param.44) | copy-start | bytes 92164
  145.0 187.9 %copy-start.7 = (f32[320,768]{1,0:T(8,128)S(1)}, f32[320,768]{1,0:T(8,128)}, u32[]{:S(2)}) copy-start(f32[320,768]{1,0:T(8,128)} %refs_6_.2) | copy-start | bytes 2949124
  145.0 187.9 %copy-start.8 = (f32[320,768]{1,0:T(8,128)S(1)}, f32[320,768]{1,0:T(8,128)}, u32[]{:S(2)}) copy-start(f32[320,768]{1,0:T(8,128)} %refs_12_.1) | copy-start | bytes 2949124
  333.0 3.0 copy-start.9
  333.0 3.0 copy-start.10
  333.0 3.0 copy-start.26
  333.0 3.0 copy-start.27
  336.0 1.6 copy-start.12
  336.0 1.7 copy-start.24
  336.0 1.8 copy-start.25
  337.8 1.9 copy-start.6
  337.8 2.0 copy-start.21
  337.8 2.2 copy-start.22
  340.0 1.8 copy-start.1
  340.0 2.6 copy-start.2
  340.0 2.8 copy-start.19
  340.0 3.1 copy-start.20
  343.1 2.1 copy-start.3
  343.1 3.1 copy-start.4
  343.1 3.3 copy-start.17
  343.1 3.6 %copy-start.18 = (bf16[320,1280]{1,0:T(8,128)(2,1)S(1)}, bf16[320,1280]{1,0:T(8,128)(2,1)}, u32[]{:S(2)}) copy-start(bf16[320,1280]{1,0:T(8,128)(2,1)} %get-tuple-element.77) | copy-start | bytes 2457604
  346.7 2.1 copy-start
  346.7 2.7 copy-start.14
  346.7 3.3 copy-start.15
  346.7 3.7 %copy-start.16 = (f32[256,1280]{1,0:T(8,128)S(1)}, f32[256,1280]{1,0:T(8,128)}, u32[]{:S(2)}) copy-start(f32[256,1280]{1,0:T(8,128)} %get-tuple-element.80) | copy-start | bytes 3932164
  350.4 2.5 copy-start.28
  350.4 3.2 copy-start.13
  (2 other events, 2.7 us)

commit v4 on v3

--- a/solution.py
+++ b/solution.py
@@ -15,8 +15,7 @@
 STEP = 10
 OUT_FAN = 4
 TILE = 256
-PARTS = 4
-ORDER = (4, 5, 3, 0, 1, 2)
+PARTS = (4, 4, 4, 4, 8, 8)
 AHEAD = 2
 POINTS = {0: (0, 0), 1: (4, 0), 2: (1, 0), 4: (0, 1), 5: (4, 1), 6: (1, 1)}
 VMEM_LIMIT = 60 * 2**20
@@ -60,28 +59,29 @@
 
 def polynomial(low, gram, poly):
     side_tiles = gram.shape[0] // TILE
+
+    def mirror(target, block, i):
+        own = slice(i * TILE, (i + 1) * TILE)
+        target[own, i * TILE :] = block
+        for j in range(i + 1, side_tiles):
+            part = block[:, (j - i) * TILE : (j - i + 1) * TILE]
+            target[j * TILE : (j + 1) * TILE, own] = part.T
+
     for i in range(side_tiles):
         own = slice(i * TILE, (i + 1) * TILE)
-        for j in range(i, side_tiles):
-            other = slice(j * TILE, (j + 1) * TILE)
-            block = lax.dot_general(
-                low[:, own],
-                low[:, other],
-                (((0,), (0,)), ((), ())),
-                preferred_element_type=jnp.float32,
-            )
-            gram[own, other] = block.astype(jnp.bfloat16)
-            if j > i:
-                gram[other, own] = block.T.astype(jnp.bfloat16)
+        block = lax.dot_general(
+            low[:, own],
+            low[:, i * TILE :],
+            (((0,), (0,)), ((), ())),
+            preferred_element_type=jnp.float32,
+        )
+        mirror(gram, block.astype(jnp.bfloat16), i)
     for i in range(side_tiles):
         own = slice(i * TILE, (i + 1) * TILE)
         block = coef_three * jnp.dot(
             gram[own, :], gram[:, i * TILE :], preferred_element_type=jnp.float32
         ) + coef_two * gram[own, i * TILE :].astype(jnp.float32)
-        poly[own, i * TILE :] = block.astype(jnp.bfloat16)
-        for j in range(i + 1, side_tiles):
-            part = block[:, (j - i) * TILE : (j - i + 1) * TILE]
-            poly[j * TILE : (j + 1) * TILE, own] = part.T.astype(jnp.bfloat16)
+        mirror(poly, block.astype(jnp.bfloat16), i)
 
 
 def newton_body(rows_ref, out_ref, wide, low, gram, poly, total):
@@ -821,6 +821,16 @@
     core, z0, z1, y, x = bits[CORE], bits[Z0], bits[Z1], bits[Y], bits[X]
     ring = [((seq + step) % 8, opt) for step in range(1, 8)]
     height = r.lat_block.shape[1]
+    load = Loader(r.local)
+    loads = [
+        load.start(source, target)
+        for source, target in (
+            (r.base, r.h_base),
+            (r.lat_low, r.h_lat_low),
+            (r.query_full, r.h_query_full),
+            (r.latents, r.h_latents),
+        )
+    ]
     clear(r.g_full.at[0])
     clear(r.g_full.at[1])
     beyond = [((seq + step) % 8, targets[X][1]) for step in range(8)]
@@ -971,124 +981,145 @@
 
     beside = courier.send(r.g_full.at[core], r.g_full.at[core], targets[CORE])
     beside.wait_recv()
+    for copy in loads:
+        copy.wait()
     side = r.whole.shape[1]
     tiles = side // TILE
-    narrow = (seq == SLOTS[1]) | (seq == SLOTS[2])
+    big = (seq == SLOTS[4]) | (seq == SLOTS[5])
+    small = (seq == SLOTS[0]) | (seq == SLOTS[1]) | (seq == SLOTS[2]) | (seq == SLOTS[3])
+    both = 2 * width
+    turned = r.out.shape[0] * 4
     r.total[0] = 0.0
 
-    def join(tile, carry):
-        at = rows_at(tile * TILE, TILE)
-        r.wide[at, :] = wide(r.base[at, :])
-
-        @pl.when(jnp.logical_not(narrow))
-        def _():
+    def joined(at, lanes, block):
+        r.wide[at, lanes] = block
+        r.total[0] = r.total[0] + jnp.sum(block * block)
+
+    def over_tiles(body):
+        def step(tile, carry):
+            body(rows_at(tile * TILE, TILE), tile)
+            return carry
+
+        lax.fori_loop(0, tiles, step, 0)
+
+    @pl.when(big)
+    def _():
+        def body(at, tile):
             for index in range(2):
                 lanes = slice(index * (side // 2), (index + 1) * (side // 2))
-                r.wide[at, lanes] = r.wide[at, lanes] + wide(r.g_full[index, at, :])
-
-        @pl.when(narrow)
-        def _():
-            part = width
+                joined(at, lanes, wide(r.h_base[at, lanes]) + wide(r.g_full[index, at, :]))
+
+        over_tiles(body)
+
+    @pl.when((seq == SLOTS[1]) | (seq == SLOTS[2]))
+    def _():
+        def body(at, tile):
             for index in range(2):
-                lanes = slice(index * part, (index + 1) * part)
-                r.wide[at, lanes] = r.wide[at, lanes] + wide(r.g_full[index, at, :part])
-
-        @pl.when(seq == SLOTS[0])
-        def _():
-            lanes = slice(0, 2 * width)
-            r.wide[at, lanes] = r.wide[at, lanes] + dot_tn(
-                r.lat_low[:, lanes_at(tile * TILE, TILE)], r.query_all[...]
+                lanes = slice(index * width, (index + 1) * width)
+                joined(at, lanes, wide(r.h_base[at, lanes]) + wide(r.g_full[index, at, :width]))
+
+        over_tiles(body)
+
+    @pl.when(seq == SLOTS[0])
+    def _():
+        def body(at, tile):
+            lanes = slice(0, both)
+            joined(
+                at,
+                lanes,
+                wide(r.h_base[at, lanes])
+                + dot_tn(r.h_lat_low[:, lanes_at(tile * TILE, TILE)], r.query_all[...]),
             )
 
-        block = r.wide[at, :]
-        r.total[0] = r.total[0] + jnp.sum(block * block)
-        return carry
-
-    lax.fori_loop(0, tiles, join, 0)
+        over_tiles(body)
+
+    @pl.when(seq == SLOTS[3])
+    def _():
+        for block in range(4):
+            at = slice(block * height, block * height + turned)
+            for index in range(2):
+                lanes = slice(index * (side // 2), (index + 1) * (side // 2))
+                part = wide(r.h_base[at, lanes]) + wide(r.g_full[index, at, :])
+                joined(lanes, slice(block * turned, (block + 1) * turned), part.T)
+
     scale = 1.0 / (jnp.sqrt(jnp.full((1, 1), r.total[0], jnp.float32)) + 1e-07)
 
-    def normalise(tile, carry):
-        at = rows_at(tile * TILE, TILE)
-        block = r.wide[at, :] * scale
-        r.wide[at, :] = block
-        r.whole[at, :] = low(block)
-        return carry
-
-    lax.fori_loop(0, tiles, normalise, 0)
-
-    def update(at):
-        block = coef_one * r.wide[at, :] + dot_nn(r.whole[at, :], r.poly[...])
-        r.wide[at, :] = block
-        r.whole[at, :] = low(block)
-
-    def sweep(index, carry):
-        for step, turn in enumerate((0, 1, 3, 4)):
-
-            @pl.when(index == turn)
-            def _(step=step):
-                if step < 4:
-                    for which in range(5):
-                        gather(which, step).wait_recv()
-                if step < 3:
-                    for which in range(5):
-                        gather(which, step + 1).start()
-                if step == 3:
-                    for which in range(5):
-                        rows, cols = gathered[which].shape
-                        full[which][:, lanes_at(core * cols, cols)] = gathered[which][
-                            rows_at(core * (rows // 2), rows // 2), :
-                        ]
-
-        polynomial(r.whole, r.gram, r.poly)
-
-        @pl.when(index < 4)
-        def _():
-            def step_rows(tile, inner):
-                update(rows_at(tile * TILE, TILE))
-                return inner
-
-            lax.fori_loop(0, tiles, step_rows, 0)
-
-        return carry
-
-    lax.fori_loop(0, 5, sweep, 0)
-    own_first = opt * height
-    update(rows_at(own_first, height))
+    def normalise(cols):
+        def body(at, tile):
+            block = r.wide[at, :cols] * scale
+            r.wide[at, :cols] = block
+            r.whole[at, :cols] = low(block)
+
+        over_tiles(body)
+
+    def update(at, cols):
+        block = coef_one * r.wide[at, :cols] + dot_nn(r.whole[at, :cols], r.poly[:cols, :cols])
+        r.wide[at, :cols] = block
+        r.whole[at, :cols] = low(block)
+
+    def gathers(step, action):
+        for which in range(5):
+            action(gather(which, step))
+
+    def gather_take(step):
+        gathers(step, lambda copy: copy.wait_recv())
+
+    def gather_give(step):
+        gathers(step, lambda copy: copy.start())
+        if step == 3:
+            for which in range(5):
+                rows, cols = gathered[which].shape
+                full[which][:, lanes_at(core * cols, cols)] = gathered[which][
+                    rows_at(core * (rows // 2), rows // 2), :
+                ]
 
     outs = (r.o_query, r.o_key, r.o_value, r.o_out, r.o_up, r.o_down)
     z, depth = seq // 2, 4
 
-    def copy(which, part, way, mine):
+    def copy(which, part, way):
         out = outs[which]
-        rows = out.shape[0] // PARTS
-        view = out.at[pl.ds(part * rows, rows)]
-        source = view
-        if mine:
-            source = r.whole.at[rows_at(own_first + part * rows, rows), pl.ds(0, out.shape[1])]
+        cols = out.shape[1] * 4 // PARTS[which]
+        rows = out.shape[0] // 4
+        across = out.shape[1] // cols
+        view = out.at[pl.ds(part // across * rows, rows), pl.ds(part % across * cols, cols)]
         return pltpu.make_async_remote_copy(
-            src_ref=source,
+            src_ref=view,
             dst_ref=view,
-            send_sem=r.spread_send.at[way, which * PARTS + part],
-            recv_sem=r.spread_recv.at[which * PARTS + part],
+            send_sem=r.spread_send.at[way, which * max(PARTS) + part],
+            recv_sem=r.spread_recv.at[which * max(PARTS) + part],
             device_id=((seq + 2, opt), (seq - 2, opt), targets[Y])[way],
             device_id_type=MESH,
         )
 
-    def ways(which, mine):
+    def for_ways(which, mine, action):
         slot_y, slot_z = SLOTS[which] % 2, SLOTS[which] // 2
         turn = (y == slot_y) & ((z == slot_z) if mine else (z != slot_z))
-        return (
+        on = (
             turn & (z >= slot_z) & (z < depth - 1),
             turn & (z <= slot_z) & (z > 0),
             turn,
         )
-
-    def for_ways(which, mine, action):
-        for way, on in enumerate(ways(which, mine)):
-
-            @pl.when(on)
+        for way in range(3):
+
+            @pl.when(on[way])
             def _(way=way):
                 action(way)
+
+    def send_own(which):
+        for part in range(PARTS[which]):
+            if part >= AHEAD:
+                for_ways(which, True, lambda way: copy(which, part - AHEAD, way).wait_send())
+            for_ways(which, True, lambda way: copy(which, part, way).start())
+
+    def pass_on(group, first, last):
+        for part in range(first, last):
+            for which in group:
+
+                @pl.when((y == SLOTS[which] % 2) & (z != SLOTS[which] // 2))
+                def _(which=which, part=part):
+                    copy(which, part, 2).wait_recv()
+
+                for_ways(which, False, lambda way: copy(which, part, way).start())
 
     def latent_gradients():
         r.lat_grads[...] = jnp.zeros_like(r.lat_grads)
@@ -1096,8 +1127,8 @@
 
         def latent_rows(step, carry):
             at = rows_at(step * 32, 32)
-            hat, inverse = norm(r.latents[at, :])
-            grad = dot_nt(r.query_all[at, :], r.query_full[...])
+            hat, inverse = norm(r.h_latents[at, :])
+            grad = dot_nt(r.query_all[at, :], r.h_query_full[...])
             r.lat_grads[0:1, :] = r.lat_grads[0:1, :] + jnp.sum(grad * hat, axis=0, keepdims=True)
             r.lat_grads[1:2, :] = r.lat_grads[1:2, :] + jnp.sum(grad, axis=0, keepdims=True)
             scaled = grad * r.lat_vectors[0:1, :]
@@ -1111,41 +1142,95 @@
         lax.fori_loop(0, r.latents.shape[0] // 32, latent_rows, 0)
         r.query_grad[...] = dot_tn(r.lat_block[...], r.query_all[...])
 
-    for step in range(PARTS + 1):
-        if step == 1:
-            latent_gradients()
-        for which in ORDER if step < PARTS else ():
-            if step >= AHEAD:
-                for_ways(
-                    which, True, lambda way: copy(which, step - AHEAD, way, True).wait_send()
-                )
-            for_ways(which, True, lambda way: copy(which, step, way, True).start())
-        for which in ORDER if step > 0 else ():
-
-            @pl.when(ways(which, False)[2])
-            def _(which=which, step=step):
-                copy(which, step - 1, 2, False).wait_recv()
-
-            for_ways(which, False, lambda way: copy(which, step - 1, way, False).start())
-    for which in ORDER:
+    few, many = (0, 1, 2, 3), (4, 5)
+    own_first = opt * height
+    gather_take(0)
+    gather_give(1)
+
+    @pl.when(big)
+    def _():
+        normalise(side)
+
+        def sweep(index, carry):
+            @pl.when(index == 1)
+            def _():
+                gather_take(1)
+                gather_give(2)
+
+            @pl.when(index == 3)
+            def _():
+                pass_on(few, 0, 2)
+
+            @pl.when(index == 4)
+            def _():
+                gather_take(2)
+                gather_give(3)
+                pass_on(few, 2, 4)
+
+            polynomial(r.whole, r.gram, r.poly)
+
+            @pl.when(index < 4)
+            def _():
+                update(slice(0, side), side)
+
+            return carry
+
+        lax.fori_loop(0, 5, sweep, 0)
+        update(rows_at(own_first, height), side)
+
+    @pl.when(small)
+    def _():
+        normalise(both)
+
+        def sweep(index, carry):
+            polynomial(r.whole.at[:, :both], r.gram.at[:both, :both], r.poly.at[:both, :both])
+            update(slice(0, side), both)
+            return carry
+
+        lax.fori_loop(0, 5, sweep, 0)
+
+    for which in few + many:
 
         @pl.when(seq == SLOTS[which])
         def _(which=which):
             rows, cols = outs[which].shape
-            outs[which][...] = r.whole[rows_at(own_first, rows), :cols]
-
-    for part in range(PARTS):
-        for which in ORDER:
+            if which == 3:
+                for block in range(4):
+
+                    @pl.when(opt == block)
+                    def _(block=block):
+                        lanes = slice(block * rows, (block + 1) * rows)
+                        outs[which][...] = low(wide(r.whole[:, lanes]).T)
+            else:
+                outs[which][...] = r.whole[rows_at(own_first, rows), :cols]
+
+    @pl.when(jnp.logical_not(big))
+    def _():
+        gather_take(1)
+        gather_give(2)
+        for which in few:
+            send_own(which)
+        pass_on(few, 0, 4)
+        gather_take(2)
+        gather_give(3)
+
+    for which in many:
+        send_own(which)
+    gather_take(3)
+    latent_gradients()
+    pass_on(many, 0, 8)
+    for which in few + many:
+        for part in range(PARTS[which]):
 
             @pl.when(y != SLOTS[which] % 2)
             def _(which=which, part=part):
-                copy(which, part, 2, False).wait_recv()
-
-    for part in range(PARTS):
-        for which in ORDER:
-            for_ways(which, False, lambda way: copy(which, part, way, False).wait_send())
-            if part >= PARTS - AHEAD:
-                for_ways(which, True, lambda way: copy(which, part, way, True).wait_send())
+                copy(which, part, 2).wait_recv()
+
+    for which in few + many:
+        for part in range(PARTS[which]):
+            for_ways(which, False, lambda way: copy(which, part, way).wait_send())
+            if part >= PARTS[which] - AHEAD:
+                for_ways(which, True, lambda way: copy(which, part, way).wait_send())
     for index, which in owned:
         piece_copy(index, which, seq, x, False).wait_send()
 
@@ -1153,9 +1238,8 @@
         def _(index=index, which=which):
             piece_copy(index, which, seq, x, True).wait_send()
 
-    for which in range(5):
-        for step in range(4):
-            gather(which, step).wait_send()
+    for step in range(4):
+        gathers(step, lambda copy: copy.wait_send())
     courier.finish()
 
 
@@ -1168,13 +1252,13 @@
         for grad in (done.grad_key, done.grad_value)
     )
     operands = dict(
+        base=done.base,
+        lat_low=done.lat_low,
+        query_full=done.query_full,
+        latents=latents,
         vectors=done.vectors,
         rest=done.rest,
-        lat_low=done.lat_low,
         lat_block=done.lat_block,
-        query_full=done.query_full,
-        base=done.base,
-        latents=latents,
         lat_vectors=lat_vectors,
         up=done.piece_up,
         down=done.piece_down,
@@ -1202,6 +1286,10 @@
     )
     half_rest = (done.rest.shape[0], done.rest.shape[1] // 2)
     scratch = dict(
+        h_base=(done.base.shape, bf16),
+        h_lat_low=(done.lat_low.shape, bf16),
+        h_query_full=(done.query_full.shape, bf16),
+        h_latents=(latents.shape, f32),
         vectors_in=((5, *done.vectors.shape), f32),
         vectors_out=((4, *done.vectors.shape), f32),
         rest_in=((2, *half_rest), bf16),
@@ -1227,7 +1315,7 @@
         for stage, shape in enumerate(chain_of(which, array.shape)):
             scratch[f"{name}_{stage}"] = (shape, bf16)
     copies = 48
-    count = len(SLOTS) * PARTS
+    count = len(SLOTS) * max(PARTS)
     dma = pltpu.SemaphoreType.DMA
     sems = dict(
         send=dma((copies,)),
@@ -1239,19 +1327,136 @@
         spread_send=dma((3, count)),
         spread_recv=dma((count,)),
         total=pltpu.SMEM((1,), f32),
+        local=dma((4,)),
     )
     keys = (*operands, *outputs, *scratch, *sems)
-    vmem = pl.BlockSpec(memory_space=pltpu.VMEM)
+    vmem, anywhere = pl.BlockSpec(memory_space=pltpu.VMEM), pl.BlockSpec(memory_space=pl.ANY)
     results = pl.pallas_call(
         functools.partial(tail_body, keys),
         out_shape=[jax.ShapeDtypeStruct(*spec) for spec in outputs.values()],
-        in_specs=[vmem] * len(operands),
+        in_specs=[anywhere] * 4 + [vmem] * (len(operands) - 4),
         out_specs=[vmem] * len(outputs),
         scratch_shapes=[*(pltpu.VMEM(*spec) for spec in scratch.values()), *sems.values()],
         compiler_params=pltpu.CompilerParams(
             collective_id=0, has_side_effects=True, vmem_limit_bytes=VMEM_LIMIT
         ),
         name="tail",
+    )(*operands.values())
+    return named(outputs, results)
+
+
+def finish_body(keys, rates, *refs):
+    r = named(keys, refs)
+    count = len(rates)
+    load = Loader(r.load_sem)
+    into = lambda name, index: getattr(r, f"{name}{index}")
+    loads = []
+    for index in range(count):
+        loads.append(
+            [
+                load.start(into(name, index), into("v" + name, index))
+                for name in ("m", "g", "w", "o")
+            ]
+        )
+    states = [
+        load.start(source, target)
+        for source, target in (
+            (r.latents, r.vlatents),
+            (r.first, r.vfirst),
+            (r.second, r.vsecond),
+            (r.grad, r.vgrad),
+        )
+    ]
+    store = Loader(r.store_sem)
+    stores = []
+
+    def over_rows(ref, body):
+        def step(index, carry):
+            body(rows_at(index * 32, 32))
+            return carry
+
+        lax.fori_loop(0, ref.shape[0] // 32, step, 0)
+
+    for index, (keep, rate) in enumerate(rates):
+        moment, grad, weight, turn = (into("v" + name, index) for name in ("m", "g", "w", "o"))
+        loads[index][0].wait()
+        loads[index][1].wait()
+
+        def new_moment(at, moment=moment, grad=grad):
+            moment[at, :] = 0.95 * moment[at, :] + wide(grad[at, :])
+
+        over_rows(moment, new_moment)
+        stores.append(store.start(moment, into("nm", index)))
+        loads[index][2].wait()
+        loads[index][3].wait()
+
+        def new_weight(at, weight=weight, turn=turn, keep=keep, rate=rate):
+            weight[at, :] = keep * weight[at, :] - rate * wide(turn[at, :])
+
+        over_rows(weight, new_weight)
+        stores.append(store.start(weight, into("nw", index)))
+    for copy in states:
+        copy.wait()
+
+    def new_latents(at):
+        first, second, new = adam_update(
+            r.vlatents[at, :], r.vgrad[at, :], r.vfirst[at, :], r.vsecond[at, :], 1.0, 0.1
+        )
+        r.vfirst[at, :], r.vsecond[at, :], r.vlatents[at, :] = first, second, new
+
+    over_rows(r.vlatents, new_latents)
+    for source, target in (
+        (r.vfirst, r.nfirst),
+        (r.vsecond, r.nsecond),
+        (r.vlatents, r.nlatents),
+    ):
+        stores.append(store.start(source, target))
+    r.lat_first_new[...], r.lat_second_new[...], r.lat_new[...] = adam_update(
+        r.lat_vectors[...], r.lat_grads[:6, :], r.lat_first[...], r.lat_second[...], 0.6, 0.0
+    )
+    width = r.in_vectors.shape[1]
+    r.in_first_new[...], r.in_second_new[...], r.in_new[...] = adam_update(
+        r.in_vectors[...], r.vectors[4:6, :width], r.in_first[...], r.in_second[...], 0.6, 0.0
+    )
+    for copy in stores:
+        copy.wait()
+
+
+def run_finish(moments, gradients, masters, turns, latent_state, vector_state):
+    f32 = jnp.float32
+    fans = (D_LAT, E_IN, E_IN, OUT_FAN, D_LAT, D_LAT)
+    sides = (D_LAT, E_IN, E_IN, D_LAT, D_LAT, D_LAT)
+    rates = [
+        (1.0 - 0.1 * fan ** (-0.5), fan ** (-0.5) * side**0.5) for fan, side in zip(fans, sides)
+    ]
+    large = {}
+    for index, arrays in enumerate(zip(moments, gradients, masters, turns)):
+        for name, array in zip(("m", "g", "w", "o"), arrays):
+            large[f"{name}{index}"] = array
+    large.update(latent_state)
+    operands = {**large, **vector_state}
+    outputs, scratch = {}, {}
+    for index, moment in enumerate(moments):
+        outputs[f"nm{index}"] = outputs[f"nw{index}"] = (moment.shape, f32)
+    latents = latent_state["latents"].shape
+    outputs.update(nfirst=(latents, f32), nsecond=(latents, f32), nlatents=(latents, f32))
+    in_place = len(outputs)
+    lat, inner = vector_state["lat_first"].shape, vector_state["in_first"].shape
+    outputs.update(lat_first_new=(lat, f32), lat_second_new=(lat, f32), lat_new=(lat, f32))
+    outputs.update(in_first_new=(inner, f32), in_second_new=(inner, f32), in_new=(inner, f32))
+    for name, array in large.items():
+        scratch["v" + name] = pltpu.VMEM(array.shape, array.dtype)
+    scratch["load_sem"] = pltpu.SemaphoreType.DMA((len(large),))
+    scratch["store_sem"] = pltpu.SemaphoreType.DMA((in_place,))
+    vmem, anywhere = pl.BlockSpec(memory_space=pltpu.VMEM), pl.BlockSpec(memory_space=pl.ANY)
+    results = pl.pallas_call(
+        functools.partial(finish_body, (*operands, *outputs, *scratch), rates),
+        out_shape=[jax.ShapeDtypeStruct(*spec) for spec in outputs.values()],
+        in_specs=[anywhere] * len(large) + [vmem] * len(vector_state),
+        out_specs=[anywhere] * in_place + [vmem] * 6,
+        scratch_shapes=list(scratch.values()),
+        compiler_params=pltpu.CompilerParams(vmem_limit_bytes=VMEM_LIMIT),
+        name="finish",
     )(*operands.values())
     return named(outputs, results)
 
@@ -1316,10 +1521,6 @@
         summed.n_up,
         summed.n_down,
     )
-    moments_new = [
-        0.95 * moment + gradient.astype(jnp.float32)
-        for moment, gradient in zip(moments, gradients)
-    ]
     currents = (
         summed.o_query,
         summed.o_key,
@@ -1328,18 +1529,47 @@
         summed.o_up,
         summed.o_down,
     )
-    new_masters = update_masters(masters, currents)
-    lat_vec_sum = summed.lat_grads[:6]
-    in_vec_sum = summed.vectors_sum[4:6, :width_in]
-    latent_sum = summed.latent_grad
+    new = run_finish(
+        moments,
+        gradients,
+        masters,
+        currents,
+        dict(latents=latents, first=latent_first, second=latent_second, grad=summed.latent_grad),
+        dict(
+            lat_vectors=lat_vectors,
+            lat_grads=summed.lat_grads,
+            lat_first=lat_first,
+            lat_second=lat_second,
+            in_vectors=in_vectors,
+            vectors=summed.vectors_sum,
+            in_first=in_first,
+            in_second=in_second,
+        ),
+    )
     return (
         done.block_out.reshape(cotangent.shape),
         done.input_grad.reshape(inputs.shape),
-        *moments_new,
-        *new_masters,
-        *adam_update(lat_vectors, lat_vec_sum, lat_first, lat_second, 0.6, 0.0),
-        *adam_update(in_vectors, in_vec_sum, in_first, in_second, 0.6, 0.0),
-        *adam_update(latents, latent_sum, latent_first, latent_second, 1.0, 0.1),
+        new.nm0,
+        new.nm1,
+        new.nm2,
+        new.nm3,
+        new.nm4,
+        new.nm5,
+        new.nw0,
+        new.nw1,
+        new.nw2,
+        new.nw3,
+        new.nw4,
+        new.nw5,
+        new.lat_first_new,
+        new.lat_second_new,
+        new.lat_new,
+        new.in_first_new,
+        new.in_second_new,
+        new.in_new,
+        new.nfirst,
+        new.nsecond,
+        new.nlatents,
     )
 
 

time: 361 us -> 343 us (0.950)
  other arithmetic: 17.6 us -> 1.35 us
  local copies, waits for them, and re-layouts: 8.18 us -> 1.82 us
  Pallas kernels: 328 us -> 333 us
    pallas_call x0 -> x1, Pallas kernels: none -> 18.1 us  [run_finish(): pl.pallas_call(functools.partial(finish_body, (*operands, *outputs, *scra...]
    pallas_call x1, Pallas kernels: 185 us -> 172 us  [run_tail(): pl.pallas_call(functools.partial(tail_body, keys), out_shape=[jax.ShapeDt...]
    sub x7 -> x0, other arithmetic: 13.1 us -> none  [the longest x4 7.77 us: update_masters(): (1.0 - 0.1 * step_rate) * master]
    unnamed x70 -> x6, local copies, waits for them, and re-layouts: 8.18 us -> 1.82 us
where the time goes in v4:
time: 343 us; the launch traced here: 337 us
  Pallas kernels  333 us (97%)
    pallas_call x1, Pallas kernels, run_tail(): pl.pallas_call(functools.partial(tail_body, keys), out_shape=[jax.ShapeDt...  172 us
    pallas_call x1, Pallas kernels, run_pass(): pl.pallas_call(functools.partial(pass_body, keys), out_shape=[jax.ShapeDt...  143 us
    pallas_call x1, Pallas kernels, run_finish(): pl.pallas_call(functools.partial(finish_body, (*operands, *outputs, *scra...  18.1 us

profile of v4, /device:TPU:0, one launch (start us, length us, event | category | flops | bytes accessed | tf_op | source)
XLA Modules:
  0.0 336.9 jit_solution(1621993743162279383)
XLA Ops:
  0.7 1.3 and_convert_fusion.refs_1_
  2.0 143.0 %pass.1 = (bf16[64,1280]{1,0:T(8,128)(2,1)}, f32[512,768]{1,0:T(8,128)}, bf16[768,384]{1,0:T(8,128)(2,1)}, bf16[768,384]{1,0:T(8,128)(2,1)}, bf16[256,768]{1,0:T...) custom-call(bf16[512,768]{1,0:T(8,128)(2,1)} %bitcast.12, ...), custom_call_target="tpu_custom_call" | custom-call | tf_op jit(solution)/shard_map/pass/pallas_call | solution.py:803
  145.0 171.7 %tail.1 = (f32[8,1280]{1,0:T(8,128)}, f32[8,1280]{1,0:T(8,128)}, f32[256,1280]{1,0:T(8,128)}, f32[320,768]{1,0:T(8,128)}, bf16[320,1280]{1,0:T(8,128)(2,1)}, /*i...) custom-call(bf16[1280,1280]{1,0:T(8,128)(2,1)} %get-tuple-element.75, ...), custom_call_target="tpu_custom_call" | custom-call | tf_op jit(solution)/shard_map/tail/pallas_call | solution.py:1334
  316.7 0.0 copy-start.1
  316.7 0.0 copy-start
  316.7 18.1 %finish.1 = (f32[320,768]{1,0:T(8,128)}, f32[320,768]{1,0:T(8,128)}, f32[192,768]{1,0:T(8,128)}, f32[192,768]{1,0:T(8,128)}, f32[192,768]{1,0:T(8,128)}, /*index...) custom-call(f32[320,768]{1,0:T(8,128)} %refs_0_.1, ...), custom_call_target="tpu_custom_call" | custom-call | tf_op jit(solution)/shard_map/finish/pallas_call | solution.py:1452
  334.8 0.0 copy-done.1
  334.8 0.7 copy.52
  335.5 0.0 copy-done
  335.5 1.1 copy.53
  (2 shorter events, 0.0 us)
Async XLA Ops:
  316.7 18.2 %copy-start.1 = (bf16[64,1280]{1,0:T(8,128)(2,1)S(1)}, bf16[64,1280]{1,0:T(8,128)(2,1)}, u32[]{:S(2)}) copy-start(bf16[64,1280]{1,0:T(8,128)(2,1)} %get-tuple-element.73) | copy-start | bytes 491524
  316.7 18.8 %copy-start = (f32[512,768]{1,0:T(8,128)S(1)}, f32[512,768]{1,0:T(8,128)}, u32[]{:S(2)}) copy-start(f32[512,768]{1,0:T(8,128)} %get-tuple-element.74) | copy-start | bytes 4718596
